TPU v7x, 256 devices: a whole 4x4x8 slice. The times are simulated.
256 devices in a mesh: section: 4 (over x_lo, core), band: 64 (over y, x_hi, z).
Axes of the slice: x: 4 (x_hi: 2, x_lo: 2; x = x_hi * 2 + x_lo), y: 4, z: 8, core: 2. Of those that a mesh axis runs over, the one named last changes fastest.
Arguments:
- fields: bfloat16 [4, 69, 512, 1024], P(None, None, 'band', 'section'), may hold values from -6 to 6
- conv_weight: bfloat16 [9, 69, 256], replicated, may hold values from -0.25 to 0.25
- kernel_blocks: bfloat16 [64, 128, 128], P('band'), may hold values from -0.25 to 0.25
- block_coords: int32 [64, 2], P('band'), may hold values from 0 to 31, as said below
- forcing_table: bfloat16 [24, 4096], replicated, may hold values from -6 to 6
- forcing_codes: int32 [2, 4, 256, 32], P(None, None, 'band', 'section'), may hold values from 0 to 23
- cotangent: bfloat16 [4, 256, 32, 4096], P(None, 'band', 'section'), may hold values from -0.078125 to 0.078125
Outputs:
- latent_next: bfloat16 [4, 256, 32, 4096], P(None, 'band', 'section')
- grad_conv: float32 [9, 69, 256], replicated
- grad_blocks: float32 [64, 128, 128], P('band')
- grad_forcing: float32 [24, 4096], replicated
Inputs may be any that keep to these rules, and one draw needn't show every extreme that they name: The rows of block_coords name distinct blocks of the 32 x 32 block grid.
All inputs are finite; a program needn't handle non-finite values.
Results may differ from a plain program's by a relative error of at most 0.0054.
Values may be sent and summed in bfloat16 or wider, within the bound.
No kernel may reach another device: no remote copies, remote signals or barrier semaphores. Data moves between devices by JAX's collectives and lax.ppermute only.
A program may use at most 128 MiB of HBM per device.

v0:
```python
import jax
import jax.numpy as jnp
from jax import lax
from jax.sharding import PartitionSpec as P

GROUP = 16
STEPS = 2


def from_behind(value, axis, steps):
    count = lax.axis_size(axis)
    initial, last = (max(0, -steps), min(count, count - steps))
    return lax.ppermute(value, axis, [(source, source + steps) for source in range(initial, last)])


def from_behind_2(array, axis, by):
    count = lax.axis_size(axis)
    return lax.ppermute(array, axis, [(i, (i + by) % count) for i in range(count)])


def apply_blocks(vectors, blocks, coords, transposed, initial, width):

    def one_block(index, summed):
        source = coords[index, 0] * width
        target = coords[index, 1] * width
        if transposed:
            source, target = (target, source)
        part = lax.dynamic_slice_in_dim(vectors, source, width, 1)
        if transposed:
            product = lax.dot_general(
                part, blocks[index], (((1,), (1,)), ((), ())), preferred_element_type=jnp.float32
            )
        else:
            product = jnp.dot(part, blocks[index], preferred_element_type=jnp.float32)
        current = lax.dynamic_slice_in_dim(summed, target, width, 1)
        return lax.dynamic_update_slice_in_dim(summed, current + product, target, 1)

    return lax.fori_loop(0, blocks.shape[0], one_block, initial)


def window_of(padded, row_tap, col_tap, half_rows, half_cols):
    return lax.slice(
        padded,
        (0, 0, row_tap, col_tap),
        (
            padded.shape[0],
            padded.shape[1],
            row_tap + 2 * half_rows - 1,
            col_tap + 2 * half_cols - 1,
        ),
        (1, 1, 2, 2),
    )


def per_device(
    fields, conv_weight, kernel_blocks, block_coords, forcing_table, forcing_codes, cotangent
):
    north = from_behind(fields[:, :, -1:, :], "band", 1)
    padded = jnp.concatenate([north, fields], axis=2)
    west = from_behind_2(padded[:, :, :, -1:], "section", 1)
    padded = jnp.concatenate([west, padded], axis=3)
    samples, channels, lat_rows, lon_cols = fields.shape
    half_rows = lat_rows // 2
    half_cols = lon_cols // 2
    latent_width = conv_weight.shape[2]
    width = kernel_blocks.shape[1]
    groups = half_cols // GROUP
    latent = jnp.zeros((samples, latent_width, half_rows, half_cols), jnp.float32)
    for row_tap in range(3):
        for col_tap in range(3):
            window = window_of(padded, row_tap, col_tap, half_rows, half_cols)
            latent = latent + jnp.einsum(
                "io,sirc->sorc",
                conv_weight[3 * row_tap + col_tap],
                window,
                preferred_element_type=jnp.float32,
            )
    shaped = latent.reshape(samples, latent_width, half_rows, groups, GROUP)
    state_zero = (
        jnp.transpose(shaped, (0, 2, 3, 1, 4))
        .reshape(-1, latent_width * GROUP)
        .astype(jnp.bfloat16)
    )
    full_blocks, full_coords = (
        lax.all_gather(kernel_blocks, "band", axis=0, tiled=True),
        lax.all_gather(block_coords, "band", axis=0, tiled=True),
    )

    def push(vectors, transposed):
        summed = apply_blocks(
            vectors,
            full_blocks,
            full_coords,
            transposed,
            jnp.zeros(vectors.shape, jnp.float32),
            width,
        )
        return (summed, full_coords)

    codes = forcing_codes.reshape(forcing_codes.shape[0], -1)
    num_codes = forcing_table.shape[0]
    code_range = jnp.arange(num_codes, dtype=jnp.int32)
    onehots = [
        (codes[step_index][:, None] == code_range[None, :]).astype(jnp.bfloat16)
        for step_index in range(STEPS)
    ]
    states = [state_zero]
    coords_all = None
    for step_index in range(STEPS):
        current = states[-1]
        pushed, coords_all = push(current, False)
        forcing = jnp.dot(onehots[step_index], forcing_table, preferred_element_type=jnp.float32)
        states.append((current.astype(jnp.float32) + pushed + forcing).astype(jnp.bfloat16))
    latent_next = states[-1].reshape(cotangent.shape)
    adjoints = [cotangent.reshape(-1, cotangent.shape[3])]
    for step_index in range(STEPS):
        later = adjoints[0]
        pulled, unused = push(later, True)
        adjoints.insert(0, (later.astype(jnp.float32) + pulled).astype(jnp.bfloat16))
    forcing_term = jnp.zeros(forcing_table.shape, jnp.float32)
    for step_index in range(STEPS):
        forcing_term = forcing_term + lax.dot_general(
            onehots[step_index],
            adjoints[step_index + 1],
            (((0,), (0,)), ((), ())),
            preferred_element_type=jnp.float32,
        )
    stack_states = jnp.concatenate(states[:STEPS], axis=0)
    stack_adjoint = jnp.concatenate(adjoints[1:], axis=0)

    def block_grad(index):
        left = lax.dynamic_slice_in_dim(stack_states, coords_all[index, 0] * width, width, 1)
        right = lax.dynamic_slice_in_dim(stack_adjoint, coords_all[index, 1] * width, width, 1)
        return lax.dot_general(
            left, right, (((0,), (0,)), ((), ())), preferred_element_type=jnp.float32
        )

    indices = jnp.arange(kernel_blocks.shape[0] * lax.axis_size("band"), dtype=jnp.int32)
    band_share = lax.psum_scatter(
        lax.map(block_grad, indices), "band", scatter_dimension=0, tiled=True
    )
    grad_blocks = lax.psum(band_share, "section")
    adjoint_shaped = adjoints[0].reshape(samples, half_rows, groups, latent_width, GROUP)
    latent_adjoint = jnp.transpose(adjoint_shaped, (0, 3, 1, 2, 4)).reshape(
        samples, latent_width, half_rows, half_cols
    )
    conv_pieces = []
    for row_tap in range(3):
        for col_tap in range(3):
            window = window_of(padded, row_tap, col_tap, half_rows, half_cols)
            conv_pieces.append(
                jnp.einsum(
                    "sirc,sorc->io", window, latent_adjoint, preferred_element_type=jnp.float32
                )
            )
    conv_term = jnp.stack(conv_pieces)
    grad_conv, grad_forcing = lax.psum((conv_term, forcing_term), ("section", "band"))
    return (latent_next, grad_conv, grad_blocks, grad_forcing)


def solution(mesh):
    return jax.shard_map(
        per_device,
        mesh=mesh,
        in_specs=(
            P(None, None, "band", "section"),
            P(),
            P("band", None, None),
            P("band", None),
            P(),
            P(None, None, "band", "section"),
            P(None, "band", "section", None),
        ),
        out_specs=(P(None, "band", "section", None), P(), P("band", None, None), P()),
        check_vma=False,
    )
```

profile of v0, /device:TPU:1, one launch (start us, length us, event | category | flops | bytes accessed | tf_op | source)
XLA Modules:
  0.0 1964.7 jit_solution(17825130253701032082)
XLA Ops:
  10.2 5.0 collective-permute-start
  15.2 25.4 %slice.95 = bf16[4,69,4,128]{3,2,1,0:T(4,128)(2,1)} slice(bf16[4,69,8,256]{3,2,1,0:T(8,128)(2,1)} %param.17), slice={[0:4:1], [0:69:1], [1:8:2], [1:256:2]} | slice | bytes 565248 | tf_op jit(solution)/shard_map/slice | solution.py:42
  40.7 25.5 %slice.93 = bf16[4,69,4,128]{3,2,1,0:T(4,128)(2,1)} slice(bf16[4,69,8,256]{3,2,1,0:T(8,128)(2,1)} %param.17), slice={[0:4:1], [0:69:1], [1:8:2], [0:255:2]} | slice | bytes 565248 | tf_op jit(solution)/shard_map/slice | solution.py:42
  66.1 15.9 slice.89
  82.0 15.8 slice.87
  97.8 152.9 %all-gather = s32[64,1,2]{2,1,0:T(1,128)S(1)} all-gather(s32[1,1,2]{2,1,0:T(1,128)S(1)} %bitcast.252), channel_id=1, replica_groups=mesh['section'=4,'band'=64] {'band'}, dimensions={0}, use_global_device_ids=true | all-gather | bytes 520 | tf_op jit(solution)/shard_map/all_gather | solution.py:86
  252.3 2.6 fusion.47
  254.9 2.6 fusion.50
  257.5 2.6 fusion.52
  263.4 21.6 %slice.83 = bf16[4,69,4,128]{3,1,2,0:T(8,128)(2,1)S(1)} slice(bf16[4,69,9,256]{3,1,2,0:T(8,128)(2,1)} %copy-done.8), slice={[0:4:1], [0:69:1], [0:7:2], [1:256:2]} | slice | bytes 565248 | tf_op jit(solution)/shard_map/slice | solution.py:42
  285.0 21.8 %slice.81 = bf16[4,69,4,128]{3,1,2,0:T(8,128)(2,1)S(1)} slice(bf16[4,69,9,256]{3,1,2,0:T(8,128)(2,1)} %copy-done.8), slice={[0:4:1], [0:69:1], [0:7:2], [0:255:2]} | slice | bytes 565248 | tf_op jit(solution)/shard_map/slice | solution.py:42
  307.8 29.0 %collective-permute-start.1 = (bf16[4,69,9,1]{1,0,3,2:T(4,128)(2,1)}, bf16[4,69,9,1]{1,0,3,2:T(4,128)(2,1)S(1)}, u32[]{:S(2)}, u32[]{:S(2)}) collective-permute-start(bf16[4,69,9,1]{1,0,3,2:T(4,128)(2,1)} %copy.58), channel_id=1, source_target_pairs={{0,64},{64,128},{128,192},{192,0},{1,65},{65,129},{129,193},{193,1... | collective-permute-start | bytes 14912 | tf_op jit(solution)/shard_map/ppermute | solution.py:18
  336.7 2.6 fusion.56
  339.4 2.5 fusion.58
  342.4 3.6 pad_maximum_fusion.2
  346.0 21.7 %slice.85 = bf16[4,69,4,128]{3,1,2,0:T(8,128)(2,1)S(1)} slice(bf16[4,69,9,257]{3,1,2,0:T(8,128)(2,1)} %pad_maximum_fusion.2), slice={[0:4:1], [0:69:1], [1:8:2], [0:255:2]} | slice | bytes 565248 | tf_op jit(solution)/shard_map/slice | solution.py:42
  367.7 21.8 %slice.79 = bf16[4,69,4,128]{3,1,2,0:T(8,128)(2,1)S(1)} slice(bf16[4,69,9,257]{3,1,2,0:T(8,128)(2,1)} %pad_maximum_fusion.2), slice={[0:4:1], [0:69:1], [0:7:2], [0:255:2]} | slice | bytes 565248 | tf_op jit(solution)/shard_map/slice | solution.py:42
  389.5 22.4 %slice.91 = bf16[4,69,4,128]{3,1,2,0:T(8,128)(2,1)} slice(bf16[4,69,9,257]{3,1,2,0:T(8,128)(2,1)} %pad_maximum_fusion.2), slice={[0:4:1], [0:69:1], [2:9:2], [0:255:2]} | slice | bytes 565248 | tf_op jit(solution)/shard_map/slice | solution.py:42
  414.6 4.2 add_convert_fusion
  418.8 5.8 copy.64
  424.6 15.1 convert_element_type.41
  441.4 226.3 %while.62 = (s32[]{:T(128)}, f32[128,4096]{1,0:T(8,128)}, s32[64,2]{0,1:T(2,128)S(1)}, bf16[128,4096]{1,0:T(8,128)(2,1)S(1)}, bf16[64,128,128]{2,1,0:T(8,128)(2,...) while((s32[]{:T(128)}, f32[128,4096]{1,0:T(8,128)}, s32[64,2]{0,1:T(2,128)S(1)}, ...), condition=%wide.region_1.0_spmd, body=%wide.region_0.0_spmd.sunk | while | flops 4210698 | bytes 197333 | solution.py:38
  669.2 227.5 %while.64 = (s32[]{:T(128)}, f32[128,4096]{1,0:T(8,128)}, s32[64,2]{0,1:T(2,128)S(1)}, bf16[128,4096]{1,0:T(8,128)(2,1)S(1)}, bf16[64,128,128]{2,1,0:T(8,128)(2,...) while((s32[]{:T(128)}, f32[128,4096]{1,0:T(8,128)}, s32[64,2]{0,1:T(2,128)S(1)}, ...), condition=%wide.region_5.0_spmd, body=%wide.region_4.0_spmd.sunk | while | flops 4210698 | bytes 197333 | solution.py:38
  900.2 2.2 pad_maximum_fusion
  902.5 392.2 %while.66 = (s32[]{:T(128)}, f32[64,128,128]{2,1,0:T(8,128)}, s32[64]{0:T(128)S(1)}, s32[64,2]{0,1:T(2,128)S(1)}, bf16[256,4096]{1,0:T(8,128)(2,1)}, /*index=5*/...) while((s32[]{:T(128)}, f32[64,128,128]{2,1,0:T(8,128)}, ...), condition=%wide.region_10.11_spmd, body=%wide.region_9.10_spmd.sunk | while | flops 8388621 | bytes 197395 | solution.py:140
  1296.5 225.9 %while.65 = (s32[]{:T(128)}, f32[128,4096]{1,0:T(8,128)}, s32[64,2]{0,1:T(2,128)S(1)}, bf16[128,4096]{1,0:T(8,128)(2,1)S(1)}, bf16[64,128,128]{2,1,0:T(8,128)(2,...) while((s32[]{:T(128)}, f32[128,4096]{1,0:T(8,128)}, s32[64,2]{0,1:T(2,128)S(1)}, ...), condition=%wide.region_7.0_spmd, body=%wide.region_6.0_spmd.sunk | while | flops 4210698 | bytes 197333 | solution.py:38
  1524.2 8.2 reshape.53
  1532.5 6.7 copy.121
  1546.4 179.2 %while.63 = (s32[]{:T(128)}, f32[128,4096]{1,0:T(8,128)S(1)}, s32[64,2]{0,1:T(2,128)S(1)}, bf16[128,4096]{1,0:T(8,128)(2,1)S(1)}, bf16[64,128,128]{2,1,0:T(8,128...) while((s32[]{:T(128)}, f32[128,4096]{1,0:T(8,128)S(1)}, s32[64,2]{0,1:T(2,128)S(1)}, ...), condition=%wide.region_3.0_spmd, body=%wide.region_2.0_spmd.sunk | while | flops 4210698 | bytes 197333 | solution.py:38
  1727.0 184.0 %all-reduce.6.cloned.1.call-done = (f32[9,69,256]{2,1,0:T(8,128)}, f32[24,4096]{1,0:T(8,128)}) async-done(((f32[9,69,256]{2,1,0:T(8,128)}, f32[24,4096]{1,0:T(8,128)}), (f32[9,69,256]{2,1,0:T(8,128)}, f32[24,4096]{1,0:T(8,128)})) %all-reduce.6.cloned.1.call-update) | async-done | bytes 1029136 | tf_op jit(solution)/shard_map/psum | solution.py:157
  1911.0 41.9 %all-reduce.4.cloned.1.call-done = f32[1,128,128]{2,1,0:T(8,128)} async-done(((f32[1,128,128]{2,1,0:T(8,128)}), f32[1,128,128]{2,1,0:T(8,128)}) %all-reduce.4.cloned.1.call-update) | async-done | bytes 65552 | tf_op jit(solution)/shard_map/psum | solution.py:142
  1953.0 2.0 copy.213
  (809 shorter events, 746.7 us)
Async XLA Ops:
  7.2 891.6 %copy-start = (bf16[24,4096]{1,0:T(8,128)(2,1)S(1)}, bf16[24,4096]{1,0:T(8,128)(2,1)}, u32[]{:S(2)}) copy-start(bf16[24,4096]{1,0:T(8,128)(2,1)} %param.21) | copy-start | bytes 589828
  7.2 59.0 %copy-start.7 = (bf16[4,69,8,256]{3,2,1,0:T(8,128)(2,1)S(1)}, bf16[4,69,8,256]{3,2,1,0:T(8,128)(2,1)}, u32[]{:S(2)}) copy-start(bf16[4,69,8,256]{3,2,1,0:T(8,128)(2,1)} %param.17) | copy-start | bytes 3391492
  7.2 90.6 %copy-start.27 = (s32[1,2]{1,0:T(1,128)S(1)}, s32[1,2]{1,0:T(1,128)}, u32[]{:S(2)}) copy-start(s32[1,2]{1,0:T(1,128)} %param.20) | copy-start | bytes 28
  7.2 432.6 %all-gather.3.cloned.1.call-start = ((), (), s32[]{:S(2)}) async-start(), calls=%async_computation.1 | async-start | bytes 2129920 | tf_op jit(solution)/shard_map/all_gather | solution.py:85
  7.9 1717.6 %reduce-scatter.2.cloned.1.call-start = ((), (), s32[]{:S(2)}) async-start(), calls=%async_computation.2 | async-start | bytes 4259840 | tf_op jit(solution)/shard_map/reduce_scatter | solution.py:139
  10.2 250.7 %collective-permute-start = (bf16[4,69,1,256]{3,1,2,0:T(8,128)(2,1)}, bf16[4,69,1,256]{3,1,2,0:T(8,128)(2,1)}, u32[]{:S(2)}, u32[]{:S(2)}) collective-permute-start(bf16[4,69,1,256]{3,1,2,0:T(8,128)(2,1)} %copy.145), channel_id=1, source_target_pairs={{0,1},{1,2},{2,3},{3,4},{4,5},{5,6},{6,7},{7,8},{8,9},{9,10},{10,1... | collective-permute-start | bytes 423944 | tf_op jit(solution)/shard_map/ppermute | solution.py:13
  250.7 1.5 copy-start.18
  250.7 4.2 copy-start.20
  252.3 5.3 copy-start.22
  254.9 5.2 copy-start.25
  262.1 1.1 copy-start.8
  285.0 56.9 %copy-start.9 = (bf16[4,69,4,128]{3,1,2,0:T(8,128)(2,1)}, bf16[4,69,4,128]{3,1,2,0:T(8,128)(2,1)S(1)}, u32[]{:S(2)}) copy-start(bf16[4,69,4,128]{3,1,2,0:T(8,128)(2,1)S(1)} %slice.83) | copy-start | bytes 847876
  306.8 35.1 %copy-start.11 = (bf16[4,69,4,128]{3,1,2,0:T(8,128)(2,1)}, bf16[4,69,4,128]{3,1,2,0:T(8,128)(2,1)S(1)}, u32[]{:S(2)}) copy-start(bf16[4,69,4,128]{3,1,2,0:T(8,128)(2,1)S(1)} %slice.81) | copy-start | bytes 847876
  307.8 34.2 %collective-permute-start.1 = (bf16[4,69,9,1]{1,0,3,2:T(4,128)(2,1)}, bf16[4,69,9,1]{1,0,3,2:T(4,128)(2,1)S(1)}, u32[]{:S(2)}, u32[]{:S(2)}) collective-permute-start(bf16[4,69,9,1]{1,0,3,2:T(4,128)(2,1)} %copy.58), channel_id=1, source_target_pairs={{0,64},{64,128},{128,192},{192,0},{1,65},{65,129},{129,193},{193,1... | collective-permute-start | bytes 14912 | tf_op jit(solution)/shard_map/ppermute | solution.py:18
  367.7 45.6 %copy-start.12 = (bf16[4,69,4,128]{3,1,2,0:T(8,128)(2,1)}, bf16[4,69,4,128]{3,1,2,0:T(8,128)(2,1)S(1)}, u32[]{:S(2)}) copy-start(bf16[4,69,4,128]{3,1,2,0:T(8,128)(2,1)S(1)} %slice.85) | copy-start | bytes 847876
  389.4 23.9 %copy-start.14 = (bf16[4,69,4,128]{3,1,2,0:T(8,128)(2,1)}, bf16[4,69,4,128]{3,1,2,0:T(8,128)(2,1)S(1)}, u32[]{:S(2)}) copy-start(bf16[4,69,4,128]{3,1,2,0:T(8,128)(2,1)S(1)} %slice.79) | copy-start | bytes 847876
  411.9 2.7 copy-start.5
  411.9 2.7 copy-start.6
  411.9 2.7 copy-start.15
  441.4 227.9 %copy-start.1 = (bf16[4,4,8,4096]{3,2,1,0:T(8,128)(2,1)S(1)}, bf16[4,4,8,4096]{3,2,1,0:T(8,128)(2,1)}, u32[]{:S(2)}) copy-start(bf16[4,4,8,4096]{3,2,1,0:T(8,128)(2,1)} %param.23) | copy-start | bytes 3145732
  896.8 2.2 copy-start.4
  899.0 1.2 copy-start.2
  1294.7 616.4 %all-reduce.6.cloned.1.call-start = ((), (), s32[]{:S(2)}) async-start(), calls=%async_computation.4 | async-start | bytes 2113536 | tf_op jit(solution)/shard_map/psum | solution.py:157
  1539.2 2.7 copy-start.10
  1539.2 3.0 copy-start.13
  1540.5 2.0 copy-start.23
  1542.2 1.0 copy-start.16
  1542.5 1.0 copy-start.19
  1542.8 1.0 copy-start.17
  1543.5 1.4 copy-start.3
  1543.5 1.4 copy-start.26
  1546.1 406.9 %all-reduce.4.cloned.1.call-start = ((), (), s32[]{:S(2)}) async-start(), calls=%async_computation.3 | async-start | bytes 131072 | tf_op jit(solution)/shard_map/psum | solution.py:142
  (2 other events, 1.8 us)
Sparse Core Ops, SparseCore 0:
  11.6 119.0 all-gather.2
  1294.8 312.4 reduce-scatter.1
  1614.3 296.7 all-reduce.5
  1913.5 39.4 all-reduce.3
where the time goes:
time: 1990 us; the launch traced here: 1960 us
  loops' own time  538 us (27%)
  matrix products  513 us (26%)
  local copies, waits for them, and re-layouts  476 us (24%)
  waiting for transfers between devices  227 us (11%)
  blocking collectives  153 us (8%)
  starting transfers between devices  34.4 us (2%)
    another operation x4, loops' own time, apply_blocks(): return lax.fori_loop(0, blocks.shape[0], one_block, initial)  331 us
    dot_general x128, matrix products, one_block(): lax.dot_general(part, blocks[index], (((1,), (1,)), ((), ())), preferred_...  212 us
    another operation x1, loops' own time, per_device(): lax.map(block_grad, indices)  207 us
    slice x9, local copies, waits for them, and re-layouts, window_of(): lax.slice(padded, (0, 0, row_tap, col_tap), (padded.shape[0], padded.shap...  192 us
    psum x1, waiting for transfers between devices, per_device(): lax.psum((conv_term, forcing_term), ('section', 'band'))  184 us
    dot_general x128, matrix products, one_block(): product = jnp.dot(part, blocks[index], preferred_element_type=jnp.float32)  163 us
    all_gather x1, blocking collectives, per_device(): lax.all_gather(block_coords, 'band', axis=0, tiled=True)  153 us
    dot_general x64, matrix products, block_grad(): lax.dot_general(left, right, (((0,), (0,)), ((), ())), preferred_element_...  109 us
  transfers between devices with their start and end apart: 6, of which 2 were waited for; matrix products, arithmetic and copies ran while one was open for 26% of the time, Pallas kernels for 0%

commit v1 on v0

v1 whole, which is shorter than its diff:
```python
import functools

import jax
import jax.numpy as jnp
from jax import lax
from jax.experimental import pallas as pl
from jax.experimental.pallas import tpu as pltpu
from jax.sharding import Mesh, PartitionSpec as P

BAND = ("y", "xh", "z")
SECTION = ("xl", "core")
ALL = ("xl", "core", "y", "xh", "z")
CIN, COUT, ROWS, PAD = 69, 256, 16, 80
TOK, WIDTH, NBLK, NNZ, NCODE = 128, 4096, 32, 64, 24
F32, BF16 = jnp.float32, jnp.bfloat16
VMEM_LIMIT = 56 * 1024 * 1024


def dot(a, b):
    return jnp.dot(a, b, preferred_element_type=F32)


def patches_kernel(fields_ref, north_ref, z_ref, east_ref, y0, y1, n0, n1):
    row = lax.broadcasted_iota(jnp.int32, (256, 256), 0)
    col = lax.broadcasted_iota(jnp.int32, (256, 256), 1)
    order = (row == (col & 7) * 32 + (col >> 3)).astype(BF16)

    def spread(step, carry):
        rows = pl.ds(pl.multiple_of(step * 368, 16), 368)
        mixed = dot(fields_ref[rows, :], order)
        y0[rows, :] = mixed[:, :128]
        y1[rows, :] = mixed[:, 128:]
        return carry

    lax.fori_loop(0, 6, spread, 0)
    y0[2208:2304, :] = jnp.zeros((96, 128), F32)
    y1[2208:2304, :] = jnp.zeros((96, 128), F32)
    mixed = dot(north_ref[...], order)
    n0[...] = mixed[:, :128]
    n1[...] = mixed[:, 128:]
    lane = lax.broadcasted_iota(jnp.int32, (16, 128), 1)

    def chunk(step, carry):
        for half, (rows_ref, top_ref) in enumerate(((y0, n0), (y1, n1))):
            for a in range(3):
                parts = []
                for s in range(4):
                    for r in range(4):
                        lat = 2 * r + a - 1
                        if lat < 0:
                            at = pl.ds(pl.multiple_of(s * PAD + step * 16, 16), 16)
                            parts.append(top_ref[at, :])
                        else:
                            at = pl.ds(s * CIN * 8 + lat + step * 128, 16, stride=8)
                            parts.append(rows_ref[at, :])
                for bit in (1, 2, 4, 8):
                    high = (lane & (8 * bit)) != 0
                    for i in range(16):
                        if i & bit:
                            continue
                        low_part, high_part = parts[i], parts[i | bit]
                        parts[i] = jnp.where(high, pltpu.roll(high_part, 8 * bit, 1), low_part)
                        parts[i | bit] = jnp.where(
                            high, high_part, pltpu.roll(low_part, 128 - 8 * bit, 1)
                        )
                for q in range(16):
                    at = pl.multiple_of((half * 16 + q + 1) * PAD + step * 16, 16)
                    z_ref[a, pl.ds(at, 16), :] = parts[q].astype(BF16)
                if half == 1:
                    at = pl.multiple_of(a * PAD + step * 16, 16)
                    east_ref[pl.ds(at, 16), :] = parts[15].astype(BF16)
        return carry

    lax.fori_loop(0, PAD // 16, chunk, 0)
    for a in range(3):
        z_ref[a, 0:PAD, :] = jnp.zeros((PAD, 128), BF16)


def make_patches(fields, north):
    return pl.pallas_call(
        patches_kernel,
        out_shape=(
            jax.ShapeDtypeStruct((3, 33 * PAD, 128), BF16),
            jax.ShapeDtypeStruct((3 * PAD, 128), BF16),
        ),
        in_specs=[pl.BlockSpec(memory_space=pltpu.VMEM)] * 2,
        out_specs=(pl.BlockSpec(memory_space=pltpu.VMEM),) * 2,
        scratch_shapes=[
            pltpu.VMEM((2304, 128), F32),
            pltpu.VMEM((2304, 128), F32),
            pltpu.VMEM((320, 128), F32),
            pltpu.VMEM((320, 128), F32),
        ],
        compiler_params=pltpu.CompilerParams(vmem_limit_bytes=VMEM_LIMIT),
        cost_estimate=pl.CostEstimate(flops=2 * 2528 * 256 * 256, bytes_accessed=4000000, transcendentals=0),
    )(fields, north)


def place(m):
    return (m // 64) % 2, m // 128, m % 64


def main_kernel(
    coords_ref, z_ref, west_ref, weight_ref, blocks_ref, table_ref, codes_ref, cot_ref,
    next_ref, out_ref,
    p0, wt, wf, sa, sb, aa, ab, at0, gc, left,
):
    lane = lax.broadcasted_iota(jnp.int32, (PAD, 128), 1)
    for a in range(3):
        own = pltpu.roll(z_ref[a, 32 * PAD:33 * PAD, :].astype(F32), 1, 1)
        other = pltpu.roll(west_ref[a * PAD:(a + 1) * PAD, :].astype(F32), 128 - 7, 1)
        p0[a, 0:PAD, :] = jnp.where((lane & 7) == 0, other, own).astype(BF16)
        p0[a, PAD:3 * PAD, :] = z_ref[a, PAD:3 * PAD, :]
        wf[...] = jnp.zeros(wf.shape, F32)
        for b in range(3):
            wf[b * PAD:b * PAD + CIN, :] = weight_ref[3 * a + b].astype(F32)
        wt[a] = wf[...].T.astype(BF16)

    def encode(patches, k):
        total = dot(wt[0], patches(0)) + dot(wt[1], patches(1)) + dot(wt[2], patches(2))
        sa[pl.ds(k, COUT, stride=16), :] = total

    def patch_of(k):
        rows = pl.ds(pl.multiple_of(k * 2 * PAD, 16), 3 * PAD)
        return lambda a: z_ref[a, rows, :]

    encode(lambda a: p0[a], 0)

    def encode_step(k, carry):
        encode(patch_of(k), k)
        return carry

    lax.fori_loop(1, 16, encode_step, 0)

    code = lax.broadcasted_iota(jnp.int32, (NCODE, TOK), 0)
    hot0 = (code == codes_ref[0:1, :]).astype(BF16)
    hot1 = (code == codes_ref[1:2, :]).astype(BF16)
    over_rows = (((0,), (0,)), ((), ()))

    def begin(b, carry):
        rows = pl.ds(pl.multiple_of(b * 128, 128), 128)
        state = sa[rows, :].astype(BF16)
        sb[rows, 0:128] = state
        forcing = lax.dot_general(table_ref[:, rows], hot0, over_rows, preferred_element_type=F32)
        sa[rows, :] = state.astype(F32) + forcing
        cot = cot_ref[:, rows]
        ab[b, 128:256, :] = cot
        aa[b] = cot.astype(F32)
        return carry

    lax.fori_loop(0, NBLK, begin, 0)

    def step_of(adjoint_rows, state_lanes):
        def body(group, carry):
            items = []
            for u in range(8):
                n = group * 8 + u
                i, j = coords_ref[n, 0], coords_ref[n, 1]
                block = blocks_ref[n, 0:128, :]
                pulled = dot(ab[j, adjoint_rows, :], block)
                source = pl.ds(pl.multiple_of(i * 128, 128), 128)
                pushed = dot(block, sb[source, state_lanes])
                items.append((i, j, pulled, pushed))
            for i, j, pulled, pushed in items:
                target = pl.ds(pl.multiple_of(j * 128, 128), 128)
                aa[i] = aa[i] + pulled
                sa[target, :] = sa[target, :] + pushed
            return carry

        lax.fori_loop(0, NNZ // 8, body, 0)

    step_of(slice(128, 256), slice(0, 128))

    def between(b, carry):
        rows = pl.ds(pl.multiple_of(b * 128, 128), 128)
        state = sa[rows, :].astype(BF16)
        sb[rows, 128:256] = state
        forcing = lax.dot_general(table_ref[:, rows], hot1, over_rows, preferred_element_type=F32)
        sa[rows, :] = state.astype(F32) + forcing
        adjoint = aa[b].astype(BF16)
        ab[b, 0:128, :] = adjoint
        aa[b] = adjoint.astype(F32)
        return carry

    lax.fori_loop(0, NBLK, between, 0)
    step_of(slice(0, 128), slice(128, 256))

    def end(b, carry):
        rows = pl.ds(pl.multiple_of(b * 128, 128), 128)
        next_ref[:, rows] = sa[rows, :].T.astype(BF16)
        at0[rows, :] = aa[b].T
        return carry

    lax.fori_loop(0, NBLK, end, 0)

    def block_grads(group, carry):
        for u in range(4):
            n = group * 4 + u
            i, j = coords_ref[n, 0], coords_ref[n, 1]
            grad = dot(sb[pl.ds(pl.multiple_of(i * 128, 128), 128), :], ab[j])
            for c in range(2):
                for x in range(2):
                    out_ref[c, x, n, 0:32, :] = grad[(2 * c + x) * 32:(2 * c + x + 1) * 32, :]
        return carry

    lax.fori_loop(0, NNZ // 4, block_grads, 0)

    hot = jnp.concatenate([hot0, hot1], axis=1)
    for j in range(NBLK):
        term = dot(hot, ab[j])
        for third in range(3):
            c, x, n = place(3 * j + third)
            out_ref[c, x, n, 32:40, :] = term[third * 8:(third + 1) * 8, :]

    def conv_grads(patches, k, first):
        adjoint = at0[pl.ds(k, COUT, stride=16), :].astype(BF16)
        for a in range(3):
            term = lax.dot_general(
                patches(a), adjoint, (((1,), (1,)), ((), ())), preferred_element_type=F32
            )
            gc[a] = term if first else gc[a] + term

    conv_grads(lambda a: p0[a], 0, True)

    def conv_grads_step(k, carry):
        conv_grads(patch_of(k), k, False)
        return carry

    lax.fori_loop(1, 16, conv_grads_step, 0)
    left[...] = jnp.zeros(left.shape, F32)
    for tap in range(9):
        a, b = divmod(tap, 3)
        for half in range(2):
            lanes = slice(half * 128, (half + 1) * 128)
            for g in range(8):
                c, x, n = place(96 + (tap * 8 + g) * 2 + half)
                out_ref[c, x, n, 32:40, :] = gc[a, b * PAD + g * 8:b * PAD + g * 8 + 8, lanes]
            at = 5 * (2 * tap + half)
            left[at:at + 5, :] = gc[a, b * PAD + 64:b * PAD + CIN, lanes]
    for m in range(240, 256):
        c, x, n = place(m)
        at = (m - 240) * 8
        out_ref[c, x, n, 32:40, :] = left[at:at + 8, :]


def run_main(coords, z, west, weight, blocks, table, codes, cot):
    vmem = pl.BlockSpec(memory_space=pltpu.VMEM)
    return pl.pallas_call(
        main_kernel,
        out_shape=(
            jax.ShapeDtypeStruct((TOK, WIDTH), BF16),
            jax.ShapeDtypeStruct((2, 2, 64, 40, 128), F32),
        ),
        in_specs=[pl.BlockSpec(memory_space=pltpu.SMEM)] + [vmem] * 7,
        out_specs=(vmem, vmem),
        scratch_shapes=[
            pltpu.VMEM((3, 3 * PAD, 128), BF16),
            pltpu.VMEM((3, COUT, 3 * PAD), BF16),
            pltpu.VMEM((3 * PAD, COUT), F32),
            pltpu.VMEM((WIDTH, TOK), F32),
            pltpu.VMEM((WIDTH, 2 * TOK), BF16),
            pltpu.VMEM((NBLK, TOK, 128), F32),
            pltpu.VMEM((NBLK, 2 * TOK, 128), BF16),
            pltpu.VMEM((WIDTH, TOK), F32),
            pltpu.VMEM((3, 3 * PAD, COUT), F32),
            pltpu.VMEM((128, 128), F32),
        ],
        compiler_params=pltpu.CompilerParams(vmem_limit_bytes=VMEM_LIMIT),
        cost_estimate=pl.CostEstimate(flops=3 * 10**9, bytes_accessed=14 * 10**6, transcendentals=0),
    )(coords, z, west, weight, blocks, table, codes, cot)


def unpack_kernel(sums_ref, conv_ref, forcing_ref, left):
    for j in range(NBLK):
        for third in range(3):
            forcing_ref[third * 8:(third + 1) * 8, j * 128:(j + 1) * 128] = sums_ref[3 * j + third]
    for m in range(12):
        left[m * 8:(m + 1) * 8, :] = sums_ref[240 + m]
    for tap in range(9):
        for half in range(2):
            lanes = slice(half * 128, (half + 1) * 128)
            for g in range(8):
                conv_ref[tap, g * 8:(g + 1) * 8, lanes] = sums_ref[96 + (tap * 8 + g) * 2 + half]
            at = 5 * (2 * tap + half)
            conv_ref[tap, 64:CIN, lanes] = left[at:at + 5, :]


def unpack(sums):
    vmem = pl.BlockSpec(memory_space=pltpu.VMEM)
    return pl.pallas_call(
        unpack_kernel,
        out_shape=(
            jax.ShapeDtypeStruct((9, CIN, COUT), F32),
            jax.ShapeDtypeStruct((NCODE, WIDTH), F32),
        ),
        in_specs=[vmem],
        out_specs=(vmem, vmem),
        scratch_shapes=[pltpu.VMEM((96, 128), F32)],
        compiler_params=pltpu.CompilerParams(vmem_limit_bytes=VMEM_LIMIT),
    )(sums)


def swap(value, axes, pairs):
    return lax.ppermute(value, axes, pairs)


def per_device(
    fields, conv_weight, kernel_blocks, block_coords, forcing_table, forcing_codes, cotangent
):
    top = jnp.pad(fields[:, :, 7, :], ((0, 0), (0, PAD - CIN), (0, 0))).reshape(4 * PAD, 256)
    north = lax.ppermute(top, BAND, [(i, i + 1) for i in range(63)])

    marks = jnp.pad(block_coords.astype(BF16), ((0, 15), (0, 126)))
    payload = jnp.concatenate([kernel_blocks[0].T, marks], axis=0)
    spread = jnp.broadcast_to(payload[None], (NNZ,) + payload.shape)
    z, east = make_patches(fields.reshape(-1, 256), north)
    west = lax.ppermute(east, SECTION, [(i, (i + 1) % 4) for i in range(4)])
    gathered = lax.all_to_all(spread, BAND, 0, 0, tiled=True)
    coords = gathered[:, 128, 0:2].astype(jnp.int32)

    latent_next, partial = run_main(
        coords, z, west, conv_weight, gathered, forcing_table,
        forcing_codes.reshape(2, TOK), cotangent.reshape(TOK, WIDTH),
    )
    chip = lax.psum_scatter(partial, "core", scatter_dimension=0, tiled=True)
    parts = lax.all_to_all(
        chip.reshape(128, 40, 128).astype(BF16), ("xl",) + BAND, 0, 0, tiled=True
    )
    sums = jnp.sum(parts.astype(F32), axis=0)
    own = sums[0:32]
    shared = jnp.broadcast_to(sums[None, 32:40].astype(BF16), (256, 8, 128))
    others = [
        lax.ppermute(own, SECTION, [(i, i ^ flip) for i in range(4)]) for flip in (1, 2, 3)
    ]
    everyone = lax.all_to_all(shared, ALL, 0, 0, tiled=True)
    grad_conv, grad_forcing = unpack(everyone.astype(F32))
    section = 2 * lax.axis_index("xl") + lax.axis_index("core")
    quarters = jnp.stack([own] + others)
    order = jnp.stack([section ^ (2 * (q % 2) + q // 2) for q in range(4)])
    grad_blocks = jnp.take(quarters, order, axis=0).reshape(1, 128, 128)
    return (latent_next.reshape(cotangent.shape), grad_conv, grad_blocks, grad_forcing)


def solution(mesh):
    fine = Mesh(mesh.devices.reshape(2, 2, 4, 2, 8), ALL)
    return jax.shard_map(
        per_device,
        mesh=fine,
        in_specs=(
            P(None, None, BAND, SECTION),
            P(),
            P(BAND, None, None),
            P(BAND, None),
            P(),
            P(None, None, BAND, SECTION),
            P(None, BAND, SECTION, None),
        ),
        out_specs=(P(None, BAND, SECTION, None), P(), P(BAND, None, None), P()),
        check_vma=False,
    )
```

time: 1990 us -> 246 us (0.12); the launches traced: 1960 us -> 245 us
  loops' own time: 538 us -> 0 us
  matrix products: 513 us -> 0 us
  local copies, waits for them, and re-layouts: 476 us -> 7.09 us
  waiting for transfers between devices: 227 us -> 85.7 us
  blocking collectives: 153 us -> 49.9 us
  Pallas kernels: 0 us -> 50.8 us
    another operation x5 -> x0, loops' own time: 538 us -> none  [the longest x4 331 us: apply_blocks(): return lax.fori_loop(0, blocks.shape[0], one_block, initial)]
    dot_general x342 -> x0, matrix products: 513 us -> none  [the longest x128 212 us: one_block(): lax.dot_general(part, blocks[index], (((1,), (1,)), ((), ())), preferred_...]
    dynamic_slice x384 -> x0, local copies, waits for them, and re-layouts: 229 us -> none  [the longest x128 76.7 us: one_block(): target = coords[index, 1] * width]
    psum x2 -> x0, waiting for transfers between devices: 226 us -> none  [the longest x1 184 us: per_device(): lax.psum((conv_term, forcing_term), ('section', 'band'))]
    slice x13 -> x2, local copies, waits for them, and re-layouts: 195 us -> 1.56 us  [the longest x1 1.55 us: per_device(): fields[:, :, 7, :]]
    all_gather x1 -> x0, blocking collectives: 153 us -> none  [per_device(): lax.all_gather(block_coords, 'band', axis=0, tiled=True)]
    pallas_call x0 -> x3, Pallas kernels: none -> 50.8 us  [the longest x1 38.9 us: run_main(): pl.pallas_call(main_kernel, out_shape=(jax.ShapeDtypeStruct((TOK, WIDTH),...]
    ppermute x2 -> x5, waiting for transfers between devices: 0.01 us -> 50.5 us  [the longest x1 47.6 us: per_device(): north = lax.ppermute(top, BAND, [(i, i + 1) for i in range(63)])]
  transfers between devices with their start and end apart: 6 -> 8, of which waited for: 2 -> 6; matrix products, arithmetic and copies ran while one was open for 26% -> 2% of each run, Pallas kernels for 0% -> 4%
where the time goes in v1:
time: 246 us; the launch traced here: 245 us
  waiting for transfers between devices  85.7 us (35%)
  Pallas kernels  50.8 us (21%)
  blocking collectives  49.9 us (20%)
  starting transfers between devices  31.4 us (13%)
  between operations  14.1 us (6%)
  local copies, waits for them, and re-layouts  7.09 us (3%)
  other arithmetic  6.24 us (3%)
    all_to_all x1, blocking collectives, per_device(): lax.all_to_all(chip.reshape(128, 40, 128).astype(BF16), ('xl',) + BAND, 0...  49.9 us
    ppermute x1, waiting for transfers between devices, per_device(): north = lax.ppermute(top, BAND, [(i, i + 1) for i in range(63)])  47.6 us
    pallas_call x1, Pallas kernels, run_main(): pl.pallas_call(main_kernel, out_shape=(jax.ShapeDtypeStruct((TOK, WIDTH),...  38.9 us
    reduce_scatter x1, waiting for transfers between devices, per_device(): chip = lax.psum_scatter(partial, 'core', scatter_dimension=0, tiled=True)  22.7 us
    all_to_all x1, starting transfers between devices, per_device(): gathered = lax.all_to_all(spread, BAND, 0, 0, tiled=True)  15.2 us
    all_to_all x1, waiting for transfers between devices, per_device(): everyone = lax.all_to_all(shared, ALL, 0, 0, tiled=True)  12.5 us
    pallas_call x1, Pallas kernels, make_patches(): pl.pallas_call(patches_kernel, out_shape=(jax.ShapeDtypeStruct((3, 33 * P...  9.69 us
    all_to_all x1, starting transfers between devices, per_device(): everyone = lax.all_to_all(shared, ALL, 0, 0, tiled=True)  7.06 us
  transfers between devices with their start and end apart: 8, of which 6 were waited for; matrix products, arithmetic and copies ran while one was open for 2% of the time, Pallas kernels for 4%

profile of v1, /device:TPU:1, one launch (start us, length us, event | category | flops | bytes accessed | tf_op | source)
XLA Modules:
  0.0 245.3 jit_solution(6607494618483049015)
XLA Ops:
  7.2 0.7 convert_element_type.26
  7.8 0.1 copy.27
  7.9 0.8 fusion.1
  8.7 0.1 copy.21
  8.8 1.7 broadcast_in_dim.26
  10.6 15.2 %all-to-all-start = ((bf16[64,144,128]{2,1,0:T(8,128)(2,1)}), bf16[64,144,128]{2,1,0:T(8,128)(2,1)S(1)}, u32[]{:S(2)}, u32[]{:S(2)}) async-start(bf16[64,144,128]{2,1,0:T(8,128)(2,1)} %broadcast_in_dim.26), calls=%async_computation | async-start | bytes 4718592 | tf_op jit(solution)/shard_map/all_to_all | solution.py:318
  25.9 1.5 slice.14
  27.5 2.9 %collective-permute-start = (bf16[320,256]{1,0:T(8,128)(2,1)S(1)}, bf16[320,256]{1,0:T(8,128)(2,1)S(1)}, u32[]{:S(2)}, u32[]{:S(2)}) collective-permute-start(bf16[320,256]{1,0:T(8,128)(2,1)S(1)} %bitcast.34), channel_id=1, source_target_pairs={{0,1},{1,2},{2,3},{3,4},{4,5},{5,6},{6,7},{7,8},{8,9},{9,10},{10,1... | collective-permute-start | bytes 491528 | tf_op jit(solution)/shard_map/ppermute | solution.py:311
  30.4 0.7 reshape.246.codes_ref
  31.1 47.6 %collective-permute-done.north_ref = bf16[320,256]{1,0:T(8,128)(2,1)S(1)} collective-permute-done((bf16[320,256]{1,0:T(8,128)(2,1)S(1)}, bf16[320,256]{1,0:T(8,128)(2,1)S(1)}, u32[]{:S(2)}, u32[]{:S(2)}) %collective-permute-start) | collective-permute-done | bytes 163872 | tf_op jit(solution)/shard_map/ppermute | solution.py:311
  78.7 0.7 copy-done.1
  79.4 9.7 %shard_map.102 = (bf16[3,2640,128]{2,1,0:T(8,128)(2,1)}, bf16[240,128]{1,0:T(8,128)(2,1)}) custom-call(bf16[2208,256]{1,0:T(8,128)(2,1)} %bitcast.31, bf16[320,256]{1,0:T(8,128)(2,1)} %copy-done.1), custom_call_target="tpu_custom_call" | custom-call | flops 331350016 | bytes 4000000 | tf_op jit(solution)/shard_map/pallas_call | solution.py:80
  89.1 2.0 collective-permute-start.1
  91.1 0.7 slice_convert_fusion
  91.8 0.9 collective-permute-done.1.west_ref
  92.7 0.6 copy-done.3
  93.3 38.9 %shard_map.103 = (bf16[128,4096]{1,0:T(8,128)(2,1)}, f32[2,2,64,40,128]{4,3,2,1,0:T(8,128)}) custom-call(s32[64,2]{1,0:T(8,128)} %bitcast.36, bf16[3,2640,128]{2,1,0:T(8,128)(2,1)} %get-tuple-element.10.z_ref, bf16[240,128]{1,0:T(8,128)(2,1)} %copy-done.3, bf16[9,69,256]{2,1,0:T(8,128)(2,1)} %weight_ref.1, bf16[64,144,128]{2,1,0:T(8,128)(2,1)} %copy-done, ...), custom_call_target="tpu_custom_call" | custom-call | flops 3000000000 | bytes 14000000 | tf_op jit(solution)/shard_map/pallas_call | solution.py:248
  132.2 22.7 %reduce-scatter.2.cloned.1.call-done = f32[1,2,64,40,128]{4,3,2,1,0:T(8,128)} async-done(((f32[2,2,64,40,128]{4,3,2,1,0:T(8,128)}), f32[1,2,64,40,128]{4,3,2,1,0:T(8,128)}) %reduce-scatter.2.cloned.1.call-update) | async-done | bytes 2621456 | tf_op jit(solution)/shard_map/reduce_scatter | solution.py:325
  155.0 1.9 convert_element_type.29
  156.9 49.9 %all_to_all.15 = bf16[128,40,128]{2,1,0:T(8,128)(2,1)S(1)} all-to-all(bf16[128,40,128]{2,1,0:T(8,128)(2,1)S(1)} %bitcast.30), channel_id=1, replica_groups=mesh['xl'=2,'core'=2,'y'=4,'xh'=2,'z'=8] {'xl','y','xh','z'}, dimensions={0} | all-to-all | bytes 2621440 | tf_op jit(solution)/shard_map/all_to_all | solution.py:326
  206.8 0.2 convert_reduce_fusion
  207.0 0.9 broadcast_in_dim.27
  207.9 7.1 %all-to-all-start.2 = ((bf16[256,8,128]{2,1,0:T(8,128)(2,1)}), bf16[256,8,128]{2,1,0:T(8,128)(2,1)S(1)}, u32[]{:S(2)}, u32[]{:S(2)}) async-start(bf16[256,8,128]{2,1,0:T(8,128)(2,1)} %broadcast_in_dim.27), calls=%async_computation.3 | async-start | bytes 1048576 | tf_op jit(solution)/shard_map/all_to_all | solution.py:335
  215.1 2.4 collective-permute-start.2
  217.5 1.7 collective-permute-start.4
  219.4 1.2 collective-permute-done.3
  220.7 0.7 collective-permute-done.4
  221.4 0.6 gather_fusion
  222.0 0.7 bitcast_select_fusion
  222.7 12.5 %all-to-all-done.2 = bf16[256,8,128]{2,1,0:T(8,128)(2,1)S(1)} async-done(((bf16[256,8,128]{2,1,0:T(8,128)(2,1)}), bf16[256,8,128]{2,1,0:T(8,128)(2,1)S(1)}, u32[]{:S(2)}, u32[]{:S(2)}) %all-to-all-start.2) | async-done | bytes 524320 | tf_op jit(solution)/shard_map/all_to_all | solution.py:335
  235.2 1.1 convert_element_type.32.sums_ref
  236.3 2.2 shard_map.104
  (21 shorter events, 0.5 us)
Async XLA Ops:
  10.6 19.8 %copy-start.2 = (s32[2,4,4,8]{3,2,1,0:T(4,128)S(1)}, s32[2,4,4,8]{3,2,1,0:T(4,128)}, u32[]{:S(2)}) copy-start(s32[2,4,4,8]{3,2,1,0:T(4,128)} %param.12) | copy-start | bytes 3076
  10.6 80.5 %all-to-all-start = ((bf16[64,144,128]{2,1,0:T(8,128)(2,1)}), bf16[64,144,128]{2,1,0:T(8,128)(2,1)S(1)}, u32[]{:S(2)}, u32[]{:S(2)}) async-start(bf16[64,144,128]{2,1,0:T(8,128)(2,1)} %broadcast_in_dim.26), calls=%async_computation | async-start | bytes 4718592 | tf_op jit(solution)/shard_map/all_to_all | solution.py:318
  25.8 129.1 %reduce-scatter.2.cloned.1.call-start = ((), (), s32[]{:S(2)}) async-start(), calls=%async_computation.4 | async-start | bytes 7864320 | tf_op jit(solution)/shard_map/reduce_scatter | solution.py:325
  27.5 51.2 %collective-permute-start = (bf16[320,256]{1,0:T(8,128)(2,1)S(1)}, bf16[320,256]{1,0:T(8,128)(2,1)S(1)}, u32[]{:S(2)}, u32[]{:S(2)}) collective-permute-start(bf16[320,256]{1,0:T(8,128)(2,1)S(1)} %bitcast.34), channel_id=1, source_target_pairs={{0,1},{1,2},{2,3},{3,4},{4,5},{5,6},{6,7},{7,8},{8,9},{9,10},{10,1... | collective-permute-start | bytes 491528 | tf_op jit(solution)/shard_map/ppermute | solution.py:311
  78.7 0.7 copy-start.1
  89.1 3.6 %collective-permute-start.1 = (bf16[240,128]{1,0:T(8,128)(2,1)}, bf16[240,128]{1,0:T(8,128)(2,1)S(1)}, u32[]{:S(2)}, u32[]{:S(2)}) collective-permute-start(bf16[240,128]{1,0:T(8,128)(2,1)} %get-tuple-element.11), channel_id=1, source_target_pairs={{0,64},{64,128},{128,192},{192,0},{1,65},{65,129},{129,193},{193,1... | collective-permute-start | bytes 184328 | tf_op jit(solution)/shard_map/ppermute | solution.py:317
  91.1 1.6 copy-start
  92.7 0.6 copy-start.3
  207.9 27.3 %all-to-all-start.2 = ((bf16[256,8,128]{2,1,0:T(8,128)(2,1)}), bf16[256,8,128]{2,1,0:T(8,128)(2,1)S(1)}, u32[]{:S(2)}, u32[]{:S(2)}) async-start(bf16[256,8,128]{2,1,0:T(8,128)(2,1)} %broadcast_in_dim.27), calls=%async_computation.3 | async-start | bytes 1048576 | tf_op jit(solution)/shard_map/all_to_all | solution.py:335
  215.1 4.4 %collective-permute-start.2 = (f32[32,128]{1,0:T(8,128)S(1)}, f32[32,128]{1,0:T(8,128)S(1)}, u32[]{:S(2)}, u32[]{:S(2)}) collective-permute-start(f32[32,128]{1,0:T(8,128)S(1)} %get-tuple-element.17), channel_id=1, source_target_pairs={{0,64},{64,0},{128,192},{192,128},{1,65},{65,1},{129,193},{193,129... | collective-permute-start | bytes 49160 | tf_op jit(solution)/shard_map/ppermute | solution.py:333
  217.4 3.2 %collective-permute-start.3 = (f32[32,128]{1,0:T(8,128)S(1)}, f32[32,128]{1,0:T(8,128)S(1)}, u32[]{:S(2)}, u32[]{:S(2)}) collective-permute-start(f32[32,128]{1,0:T(8,128)S(1)} %get-tuple-element.17), channel_id=1, source_target_pairs={{0,128},{64,192},{128,0},{192,64},{1,129},{65,193},{129,1},{193,65... | collective-permute-start | bytes 49160 | tf_op jit(solution)/shard_map/ppermute | solution.py:333
  217.5 3.9 %collective-permute-start.4 = (f32[32,128]{1,0:T(8,128)S(1)}, f32[32,128]{1,0:T(8,128)S(1)}, u32[]{:S(2)}, u32[]{:S(2)}) collective-permute-start(f32[32,128]{1,0:T(8,128)S(1)} %get-tuple-element.17), channel_id=1, source_target_pairs={{0,192},{64,128},{128,64},{192,0},{1,193},{65,129},{129,65},{193,1... | collective-permute-start | bytes 49160 | tf_op jit(solution)/shard_map/ppermute | solution.py:333
Sparse Core Ops, SparseCore 0:
  132.4 22.5 reduce-scatter.1

commit v2 on v1

v2 whole, which is shorter than its diff:
```python
import jax
import jax.numpy as jnp
from jax import lax
from jax.experimental import pallas as pl
from jax.experimental.pallas import tpu as pltpu
from jax.sharding import Mesh, PartitionSpec as P

BAND = ("y", "xh", "z")
SECTION = ("xl", "core")
ALL = ("xl", "core", "y", "xh", "z")
CIN, COUT, ROWS, PAD = 69, 256, 16, 80
TOK, WIDTH, NBLK, NNZ, NCODE = 128, 4096, 32, 64, 24
F32, BF16 = jnp.float32, jnp.bfloat16
VMEM_LIMIT = 56 * 1024 * 1024


def dot(a, b):
    return jnp.dot(a, b, preferred_element_type=F32)


def patches_kernel(fields_ref, north_ref, z_ref, east_ref, y0, y1, n0, n1):
    row = lax.broadcasted_iota(jnp.int32, (256, 256), 0)
    col = lax.broadcasted_iota(jnp.int32, (256, 256), 1)
    order = (row == (col & 7) * 32 + (col >> 3)).astype(BF16)

    def spread(step, carry):
        rows = pl.ds(pl.multiple_of(step * 368, 16), 368)
        mixed = dot(fields_ref[rows, :], order)
        y0[rows, :] = mixed[:, :128]
        y1[rows, :] = mixed[:, 128:]
        return carry

    lax.fori_loop(0, 6, spread, 0)
    y0[2208:2304, :] = jnp.zeros((96, 128), F32)
    y1[2208:2304, :] = jnp.zeros((96, 128), F32)
    mixed = dot(north_ref[...], order)
    n0[...] = mixed[:, :128]
    n1[...] = mixed[:, 128:]
    lane = lax.broadcasted_iota(jnp.int32, (16, 128), 1)

    def chunk(step, carry):
        for half, (rows_ref, top_ref) in enumerate(((y0, n0), (y1, n1))):
            for a in range(3):
                parts = []
                for s in range(4):
                    for r in range(4):
                        lat = 2 * r + a - 1
                        if lat < 0:
                            at = pl.ds(pl.multiple_of(s * PAD + step * 16, 16), 16)
                            parts.append(top_ref[at, :])
                        else:
                            at = pl.ds(s * CIN * 8 + lat + step * 128, 16, stride=8)
                            parts.append(rows_ref[at, :])
                for bit in (1, 2, 4, 8):
                    high = (lane & (8 * bit)) != 0
                    for i in range(16):
                        if i & bit:
                            continue
                        low_part, high_part = parts[i], parts[i | bit]
                        parts[i] = jnp.where(high, pltpu.roll(high_part, 8 * bit, 1), low_part)
                        parts[i | bit] = jnp.where(
                            high, high_part, pltpu.roll(low_part, 128 - 8 * bit, 1)
                        )
                for q in range(16):
                    at = pl.multiple_of((half * 16 + q + 1) * PAD + step * 16, 16)
                    z_ref[a, pl.ds(at, 16), :] = parts[q].astype(BF16)
                if half == 1:
                    at = pl.multiple_of(a * PAD + step * 16, 16)
                    east_ref[pl.ds(at, 16), :] = parts[15].astype(BF16)
        return carry

    lax.fori_loop(0, PAD // 16, chunk, 0)
    for a in range(3):
        z_ref[a, 0:PAD, :] = jnp.zeros((PAD, 128), BF16)


def make_patches(fields, north):
    return pl.pallas_call(
        patches_kernel,
        out_shape=(
            jax.ShapeDtypeStruct((3, 33 * PAD, 128), BF16),
            jax.ShapeDtypeStruct((3 * PAD, 128), BF16),
        ),
        in_specs=[pl.BlockSpec(memory_space=pltpu.VMEM)] * 2,
        out_specs=(pl.BlockSpec(memory_space=pltpu.VMEM),) * 2,
        scratch_shapes=[
            pltpu.VMEM((2304, 128), F32),
            pltpu.VMEM((2304, 128), F32),
            pltpu.VMEM((320, 128), F32),
            pltpu.VMEM((320, 128), F32),
        ],
        compiler_params=pltpu.CompilerParams(vmem_limit_bytes=VMEM_LIMIT),
        cost_estimate=pl.CostEstimate(flops=2 * 2528 * 256 * 256, bytes_accessed=4000000, transcendentals=0),
    )(fields, north)


OVER_ROWS = (((0,), (0,)), ((), ()))
OVER_LANES = (((1,), (1,)), ((), ()))


def rows_of(b):
    return pl.ds(pl.multiple_of(b * 128, 128), 128)


def vmem_call(kernel, out_shape, scratch, flops, size, *operands, smem=0):
    vmem = pl.BlockSpec(memory_space=pltpu.VMEM)
    scalar = pl.BlockSpec(memory_space=pltpu.SMEM)
    return pl.pallas_call(
        kernel,
        out_shape=out_shape,
        in_specs=[scalar] * smem + [vmem] * (len(operands) - smem),
        out_specs=tuple(vmem for _ in out_shape),
        scratch_shapes=scratch,
        compiler_params=pltpu.CompilerParams(vmem_limit_bytes=VMEM_LIMIT),
        cost_estimate=pl.CostEstimate(flops=flops, bytes_accessed=size, transcendentals=0),
    )(*operands)


def encode_kernel(z_ref, weight_ref, latent_ref, wt, wf):
    for a in range(3):
        wf[...] = jnp.zeros(wf.shape, F32)
        for b in range(3):
            wf[b * PAD:b * PAD + CIN, :] = weight_ref[3 * a + b].astype(F32)
        wt[a] = wf[...].T.astype(BF16)

    def encode_step(k, carry):
        rows = pl.ds(pl.multiple_of(k * 2 * PAD, 16), 3 * PAD)
        total = dot(wt[0], z_ref[0, rows, :])
        total += dot(wt[1], z_ref[1, rows, :])
        total += dot(wt[2], z_ref[2, rows, :])
        latent_ref[pl.ds(k, COUT, stride=16), :] = total
        return carry

    lax.fori_loop(0, 16, encode_step, 0)


def encode(z, weight):
    return vmem_call(
        encode_kernel,
        (jax.ShapeDtypeStruct((WIDTH, TOK), F32),),
        [pltpu.VMEM((3, COUT, 3 * PAD), BF16), pltpu.VMEM((3 * PAD, COUT), F32)],
        2 * 720 * 256 * 2048, 4 * 10**6, z, weight,
    )[0]


def first_column(east_ref, west_ref, a):
    lane = lax.broadcasted_iota(jnp.int32, (PAD, 128), 1)
    own = pltpu.roll(east_ref[a * PAD:(a + 1) * PAD, :].astype(F32), 1, 1)
    other = pltpu.roll(west_ref[a * PAD:(a + 1) * PAD, :].astype(F32), 128 - 7, 1)
    return jnp.where((lane & 7) == 0, other, own).astype(BF16)


def hot_codes(codes_ref, t):
    code = lax.broadcasted_iota(jnp.int32, (NCODE, TOK), 0)
    return (code == codes_ref[t:t + 1, :]).astype(BF16)


def operator_step(coords_ref, low_first, own_ref, other_ref, pull_from, push_from, aa, sa):
    def body(group, carry):
        items = []
        for u in range(UNROLL):
            n = group * UNROLL + u
            i, j = coords_ref[n, 0], coords_ref[n, 1]
            own, other = own_ref[n, 0:64, :], other_ref[n, 0:64, :]
            block = jnp.concatenate(
                [jnp.where(low_first, own, other), jnp.where(low_first, other, own)], axis=0
            )
            items.append((i, j, dot(pull_from(j), block), dot(block, push_from(i))))
        for i, j, pulled, pushed in items:
            aa[i] = aa[i] + pulled
            sa[rows_of(j), :] = sa[rows_of(j), :] + pushed
        return carry

    lax.fori_loop(0, NNZ // UNROLL, body, 0)


UNROLL = 8


def first_kernel(
    coords_ref, core_ref, own_ref, other_ref, latent_ref, east_ref, west_ref, weight_ref,
    table_ref, codes_ref, cot_ref,
    state_ref, adjoint_ref, keep_ref, send_ref,
    sa, sb, aa, ab, wf,
):
    low_first = core_ref[0] == 0
    extra = jnp.zeros((COUT, TOK), F32)
    wf[...] = jnp.zeros(wf.shape, F32)
    for a in range(3):
        wf[0:CIN, :] = weight_ref[3 * a].astype(F32)
        extra += lax.dot_general(
            wf[...].astype(BF16), first_column(east_ref, west_ref, a), OVER_ROWS,
            preferred_element_type=F32,
        )
    sa[...] = latent_ref[...]
    at = pl.ds(0, COUT, stride=16)
    sa[at, :] = sa[at, :] + extra
    hot = hot_codes(codes_ref, 0)

    def begin(b, carry):
        rows = rows_of(b)
        state = sa[rows, :].astype(BF16)
        sb[rows, 0:128] = state
        forcing = lax.dot_general(table_ref[:, rows], hot, OVER_ROWS, preferred_element_type=F32)
        sa[rows, :] = state.astype(F32) + forcing
        cot = cot_ref[:, rows]
        ab[b, 128:256, :] = cot
        aa[b] = cot.astype(F32)
        return carry

    lax.fori_loop(0, NBLK, begin, 0)
    operator_step(
        coords_ref, low_first, own_ref, other_ref,
        lambda j: ab[j, 128:256, :], lambda i: sb[rows_of(i), 0:128], aa, sa,
    )

    def end(b, carry):
        rows = rows_of(b)
        state = sa[rows, :].astype(BF16)
        sb[rows, 128:256] = state
        state_ref[rows, :] = state
        adjoint = aa[b].astype(BF16)
        ab[b, 0:128, :] = adjoint
        adjoint_ref[b] = adjoint
        return carry

    lax.fori_loop(0, NBLK, end, 0)

    def block_grads(group, carry):
        for u in range(UNROLL):
            n = group * UNROLL + u
            i, j = coords_ref[n, 0], coords_ref[n, 1]
            grad = dot(sb[rows_of(i), :], ab[j])
            low, high = grad[0:64], grad[64:128]
            keep = jnp.where(low_first, low, high)
            send = jnp.where(low_first, high, low).astype(BF16)
            for x in range(2):
                keep_ref[x, n] = keep[x * 32:(x + 1) * 32]
                send_ref[x, n] = send[x * 32:(x + 1) * 32]
        return carry

    lax.fori_loop(0, NNZ // UNROLL, block_grads, 0)


def run_first(coords, core, own, other, latent, east, west, weight, table, codes, cot):
    return vmem_call(
        first_kernel,
        (
            jax.ShapeDtypeStruct((WIDTH, TOK), BF16),
            jax.ShapeDtypeStruct((NBLK, TOK, 128), BF16),
            jax.ShapeDtypeStruct((2, NNZ, 32, 128), F32),
            jax.ShapeDtypeStruct((2, NNZ, 32, 128), BF16),
        ),
        [
            pltpu.VMEM((WIDTH, TOK), F32),
            pltpu.VMEM((WIDTH, 2 * TOK), BF16),
            pltpu.VMEM((NBLK, TOK, 128), F32),
            pltpu.VMEM((NBLK, 2 * TOK, 128), BF16),
            pltpu.VMEM((PAD, COUT), F32),
        ],
        10**9, 12 * 10**6,
        coords, core, own, other, latent, east, west, weight, table, codes, cot, smem=2,
    )


def second_kernel(
    coords_ref, core_ref, own_ref, other_ref, state_ref, adjoint_ref, z_ref, east_ref, west_ref,
    table_ref, codes_ref, cot_ref,
    next_ref, out_ref,
    sa, aa, at0, gc, left,
):
    low_first = core_ref[0] == 0
    hot0, hot1 = hot_codes(codes_ref, 0), hot_codes(codes_ref, 1)

    def begin(b, carry):
        rows = rows_of(b)
        forcing = lax.dot_general(table_ref[:, rows], hot1, OVER_ROWS, preferred_element_type=F32)
        sa[rows, :] = state_ref[rows, :].astype(F32) + forcing
        aa[b] = adjoint_ref[b].astype(F32)
        return carry

    lax.fori_loop(0, NBLK, begin, 0)
    operator_step(
        coords_ref, low_first, own_ref, other_ref,
        lambda j: adjoint_ref[j], lambda i: state_ref[rows_of(i), :], aa, sa,
    )

    def end(b, carry):
        rows = rows_of(b)
        next_ref[:, rows] = sa[rows, :].T.astype(BF16)
        at0[rows, :] = aa[b].T
        return carry

    lax.fori_loop(0, NBLK, end, 0)

    for j in range(NBLK):
        term = dot(hot0, adjoint_ref[j]) + dot(hot1, cot_ref[:, j * 128:(j + 1) * 128])
        for third in range(3):
            out_ref[3 * j + third] = term[third * 8:(third + 1) * 8, :]

    gc[...] = jnp.zeros(gc.shape, F32)

    def conv_grads(k, carry):
        adjoint = at0[pl.ds(k, COUT, stride=16), :].astype(BF16)
        rows = pl.ds(pl.multiple_of(k * 2 * PAD, 16), 3 * PAD)
        for a in range(3):
            gc[a] = gc[a] + lax.dot_general(
                z_ref[a, rows, :], adjoint, OVER_LANES, preferred_element_type=F32
            )
        return carry

    lax.fori_loop(0, 16, conv_grads, 0)
    adjoint = at0[pl.ds(0, COUT, stride=16), :].astype(BF16)
    for a in range(3):
        gc[a, 0:PAD, :] = gc[a, 0:PAD, :] + lax.dot_general(
            first_column(east_ref, west_ref, a), adjoint, OVER_LANES, preferred_element_type=F32
        )
    left[...] = jnp.zeros(left.shape, F32)
    for tap in range(9):
        a, b = divmod(tap, 3)
        for half in range(2):
            lanes = slice(half * 128, (half + 1) * 128)
            for g in range(8):
                out_ref[96 + (tap * 8 + g) * 2 + half] = (
                    gc[a, b * PAD + g * 8:b * PAD + g * 8 + 8, lanes]
                )
            at = 5 * (2 * tap + half)
            left[at:at + 5, :] = gc[a, b * PAD + 64:b * PAD + CIN, lanes]
    for m in range(16):
        out_ref[240 + m] = left[m * 8:(m + 1) * 8, :]


def run_second(coords, core, own, other, state, adjoint, z, east, west, table, codes, cot):
    return vmem_call(
        second_kernel,
        (
            jax.ShapeDtypeStruct((TOK, WIDTH), BF16),
            jax.ShapeDtypeStruct((256, 8, 128), F32),
        ),
        [
            pltpu.VMEM((WIDTH, TOK), F32),
            pltpu.VMEM((NBLK, TOK, 128), F32),
            pltpu.VMEM((WIDTH, TOK), F32),
            pltpu.VMEM((3, 3 * PAD, COUT), F32),
            pltpu.VMEM((128, 128), F32),
        ],
        2 * 10**9, 12 * 10**6,
        coords, core, own, other, state, adjoint, z, east, west, table, codes, cot, smem=2,
    )


def unpack_kernel(sums_ref, conv_ref, forcing_ref, left):
    for j in range(NBLK):
        for third in range(3):
            forcing_ref[third * 8:(third + 1) * 8, j * 128:(j + 1) * 128] = sums_ref[3 * j + third]
    for m in range(12):
        left[m * 8:(m + 1) * 8, :] = sums_ref[240 + m]
    for tap in range(9):
        for half in range(2):
            lanes = slice(half * 128, (half + 1) * 128)
            for g in range(8):
                conv_ref[tap, g * 8:(g + 1) * 8, lanes] = sums_ref[96 + (tap * 8 + g) * 2 + half]
            at = 5 * (2 * tap + half)
            conv_ref[tap, 64:CIN, lanes] = left[at:at + 5, :]


def unpack(sums):
    vmem = pl.BlockSpec(memory_space=pltpu.VMEM)
    return pl.pallas_call(
        unpack_kernel,
        out_shape=(
            jax.ShapeDtypeStruct((9, CIN, COUT), F32),
            jax.ShapeDtypeStruct((NCODE, WIDTH), F32),
        ),
        in_specs=[vmem],
        out_specs=(vmem, vmem),
        scratch_shapes=[pltpu.VMEM((96, 128), F32)],
        compiler_params=pltpu.CompilerParams(vmem_limit_bytes=VMEM_LIMIT),
    )(sums)


def per_device(
    fields, conv_weight, kernel_blocks, block_coords, forcing_table, forcing_codes, cotangent
):
    core = lax.axis_index("core")
    top = jnp.pad(fields[:, :, 7, :], ((0, 0), (0, PAD - CIN), (0, 0))).reshape(4 * PAD, 256)
    north = lax.ppermute(top, BAND, [(i, i + 1) for i in range(63)])

    turned = kernel_blocks[0].T
    half = jnp.where(core == 0, turned[0:64], turned[64:128])
    marks = jnp.pad(block_coords.astype(BF16), ((0, 7), (0, 126)))
    payload = jnp.concatenate([half, marks], axis=0)
    spread = jnp.broadcast_to(payload[None], (NNZ,) + payload.shape)
    spread, north = lax.optimization_barrier((spread, north))
    own = lax.all_to_all(spread, BAND, 0, 0, tiled=True)
    z, east = make_patches(fields.reshape(-1, 256), north)
    west = lax.ppermute(east, SECTION, [(i, (i + 1) % 4) for i in range(4)])
    latent = encode(z, conv_weight)
    other = lax.ppermute(own, "core", [(0, 1), (1, 0)])
    coords = own[:, 64, 0:2].astype(jnp.int32)
    codes = forcing_codes.reshape(2, TOK)
    cot = cotangent.reshape(TOK, WIDTH)
    which = core.astype(jnp.int32).reshape(1)

    state, adjoint, keep, send = run_first(
        coords, which, own, other, latent, east, west, conv_weight, forcing_table, codes, cot
    )
    received = lax.ppermute(send, "core", [(0, 1), (1, 0)])
    latent_next, partial = run_second(
        coords, which, own, other, state, adjoint, z, east, west, forcing_table, codes, cot
    )
    terms = lax.all_to_all(partial.astype(BF16), ALL, 0, 0, tiled=True)
    chip = (keep + received.astype(F32)).astype(BF16)
    parts = lax.all_to_all(chip.reshape(128, 32, 128), ("xl",) + BAND, 0, 0, tiled=True)
    shared = jnp.sum(terms.astype(F32), axis=0).astype(BF16)
    everyone = lax.all_to_all(
        jnp.broadcast_to(shared[None], (256, 8, 128)), ALL, 0, 0, tiled=True
    )
    grad_conv, grad_forcing = unpack(everyone.astype(F32))
    quarter = jnp.sum(parts.astype(F32), axis=0)
    others = [
        lax.ppermute(quarter, SECTION, [(i, i ^ flip) for i in range(4)]) for flip in (1, 2, 3)
    ]
    section = 2 * lax.axis_index("xl") + core
    quarters = jnp.stack([quarter] + others)
    order = jnp.stack([section ^ (2 * (q % 2) + q // 2) for q in range(4)])
    grad_blocks = jnp.take(quarters, order, axis=0).reshape(1, 128, 128)
    return (latent_next.reshape(cotangent.shape), grad_conv, grad_blocks, grad_forcing)


def solution(mesh):
    fine = Mesh(mesh.devices.reshape(2, 2, 4, 2, 8), ALL)
    return jax.shard_map(
        per_device,
        mesh=fine,
        in_specs=(
            P(None, None, BAND, SECTION),
            P(),
            P(BAND, None, None),
            P(BAND, None),
            P(),
            P(None, None, BAND, SECTION),
            P(None, BAND, SECTION, None),
        ),
        out_specs=(P(None, BAND, SECTION, None), P(), P(BAND, None, None), P()),
        check_vma=False,
    )
```

time: 246 us -> 218 us (0.89)
  waiting for transfers between devices: 85.7 us -> 63.3 us
  between operations: 14.1 us -> 0.8 us
  Pallas kernels: 50.8 us -> 57.9 us
  blocking collectives: 49.9 us -> 44.8 us
  starting transfers between devices: 31.4 us -> 35.8 us
  other arithmetic: 6.24 us -> 9.46 us
    all_to_all x2 -> x3, waiting for transfers between devices: 12.5 us -> 62.3 us  [the longest x1 29.2 us: per_device(): lax.all_to_all(chip.reshape(128, 32, 128), ('xl',) + BAND, 0, 0, tiled=True)]
    ppermute x1, waiting for transfers between devices: 47.6 us -> 0.96 us  [per_device(): north = lax.ppermute(top, BAND, [(i, i + 1) for i in range(63)])]
    reduce_scatter x1 -> x0, waiting for transfers between devices: 22.7 us -> none  [per_device(): chip = lax.psum_scatter(partial, 'core', scatter_dimension=0, tiled=True)]
    pallas_call x1 -> x3, Pallas kernels: 38.9 us -> 46 us  [vmem_call(): pl.pallas_call(kernel, out_shape=out_shape, in_specs=[scalar] * smem + [v...]
    ppermute x3 -> x5, starting transfers between devices: 4.1 us -> 9.46 us  [the longest x1 5.19 us: per_device(): other = lax.ppermute(own, 'core', [(0, 1), (1, 0)])]
    all_to_all x1, blocking collectives: 49.9 us -> 44.8 us  [per_device(): own = lax.all_to_all(spread, BAND, 0, 0, tiled=True)]
    convert_element_type x3 -> x4, other arithmetic: 3.29 us -> 6.05 us  [the longest x1 2.53 us: per_device(): chip = (keep + received.astype(F32)).astype(BF16)]
    all_to_all x2 -> x3, starting transfers between devices: 22.3 us -> 21.6 us  [the longest x1 8.6 us: per_device(): lax.all_to_all(jnp.broadcast_to(shared[None], (256, 8, 128)), ALL, 0, 0,...]
  transfers between devices with their start and end apart: 8 -> 10, of which waited for: 6 -> 4; matrix products, arithmetic and copies ran while one was open for 2% -> 5% of each run, Pallas kernels for 4% -> 19%
where the time goes in v2:
time: 218 us; the launch traced here: 217 us
  waiting for transfers between devices  63.3 us (29%)
  Pallas kernels  57.9 us (27%)
  blocking collectives  44.8 us (21%)
  starting transfers between devices  35.8 us (16%)
  other arithmetic  9.46 us (4%)
  local copies, waits for them, and re-layouts  5.36 us (2%)
    pallas_call x3, Pallas kernels, vmem_call(): pl.pallas_call(kernel, out_shape=out_shape, in_specs=[scalar] * smem + [v...  46 us
    all_to_all x1, blocking collectives, per_device(): own = lax.all_to_all(spread, BAND, 0, 0, tiled=True)  44.8 us
    all_to_all x1, waiting for transfers between devices, per_device(): lax.all_to_all(chip.reshape(128, 32, 128), ('xl',) + BAND, 0, 0, tiled=True)  29.2 us
    all_to_all x1, waiting for transfers between devices, per_device(): terms = lax.all_to_all(partial.astype(BF16), ALL, 0, 0, tiled=True)  17.5 us
    all_to_all x1, waiting for transfers between devices, per_device(): lax.all_to_all(jnp.broadcast_to(shared[None], (256, 8, 128)), ALL, 0, 0,...  15.6 us
    pallas_call x1, Pallas kernels, make_patches(): pl.pallas_call(patches_kernel, out_shape=(jax.ShapeDtypeStruct((3, 33 * P...  9.59 us
    all_to_all x1, starting transfers between devices, per_device(): lax.all_to_all(jnp.broadcast_to(shared[None], (256, 8, 128)), ALL, 0, 0,...  8.6 us
    all_to_all x1, starting transfers between devices, per_device(): terms = lax.all_to_all(partial.astype(BF16), ALL, 0, 0, tiled=True)  6.6 us
  transfers between devices with their start and end apart: 10, of which 4 were waited for; matrix products, arithmetic and copies ran while one was open for 5% of the time, Pallas kernels for 19%

profile of v2, /device:TPU:1, one launch (start us, length us, event | category | flops | bytes accessed | tf_op | source)
XLA Modules:
  0.0 217.4 jit_solution(4859305205867626853)
XLA Ops:
  0.6 1.5 slice.14
  2.2 4.4 %collective-permute-start = (bf16[320,256]{1,0:T(8,128)(2,1)S(1)}, bf16[320,256]{1,0:T(8,128)(2,1)S(1)}, u32[]{:S(2)}, u32[]{:S(2)}) collective-permute-start(bf16[320,256]{1,0:T(8,128)(2,1)S(1)} %bitcast.37), channel_id=1, source_target_pairs={{0,1},{1,2},{2,3},{3,4},{4,5},{5,6},{6,7},{7,8},{8,9},{9,10},{10,1... | collective-permute-start | bytes 491528 | tf_op jit(solution)/shard_map/ppermute | solution.py:387
  6.6 0.9 slice_select_fusion
  7.6 0.7 convert_element_type.29
  8.5 1.0 collective-permute-done.north_ref
  9.6 44.8 %all_to_all.20.own_ref = bf16[64,72,128]{2,1,0:T(8,128)(2,1)S(1)} all-to-all(bf16[64,72,128]{2,1,0:T(8,128)(2,1)S(1)} %broadcast_in_dim.26), channel_id=1, replica_groups=mesh['xl'=2,'core'=2,'y'=4,'xh'=2,'z'=8] {'y','xh','z'}, dimensions={0} | all-to-all | bytes 2359296 | tf_op jit(solution)/shard_map/all_to_all | solution.py:395
  54.5 5.2 %collective-permute-start.1 = (bf16[64,72,128]{2,1,0:T(8,128)(2,1)S(1)}, bf16[64,72,128]{2,1,0:T(8,128)(2,1)S(1)}, u32[]{:S(2)}, u32[]{:S(2)}) collective-permute-start(bf16[64,72,128]{2,1,0:T(8,128)(2,1)S(1)} %all_to_all.20.own_ref), channel_id=1, source_target_pairs={{0,64},{64,0},{1,65},{65,1},{2,66},{66,2},{3,67},{67,3},{4,68},{68... | collective-permute-start | bytes 3538952 | tf_op jit(solution)/shard_map/ppermute | solution.py:399
  59.7 0.7 reshape.250.codes_ref
  60.3 9.6 %shard_map.102 = (bf16[3,2640,128]{2,1,0:T(8,128)(2,1)}, bf16[240,128]{1,0:T(8,128)(2,1)}) custom-call(bf16[2208,256]{1,0:T(8,128)(2,1)} %bitcast.32, bf16[320,256]{1,0:T(8,128)(2,1)} %copy-done.4), custom_call_target="tpu_custom_call" | custom-call | flops 331350016 | bytes 4000000 | tf_op jit(solution)/shard_map/pallas_call | solution.py:78
  69.9 0.3 collective-permute-start.2
  70.3 7.6 %shard_map.103.latent_ref = f32[4096,128]{1,0:T(8,128)} custom-call(bf16[3,2640,128]{2,1,0:T(8,128)(2,1)} %get-tuple-element.18.z_ref, bf16[9,69,256]{2,1,0:T(8,128)(2,1)} %weight_ref.3), custom_call_target="tpu_custom_call" | custom-call | flops 754974720 | bytes 4000000 | tf_op jit(solution)/shard_map/pallas_call | solution.py:108
  77.9 0.6 slice_convert_fusion
  78.6 0.6 copy-done.3
  79.2 0.5 copy-done.1
  79.7 16.7 %shard_map.104 = (bf16[4096,128]{1,0:T(8,128)(2,1)}, bf16[32,128,128]{2,1,0:T(8,128)(2,1)}, f32[2,64,32,128]{3,2,1,0:T(8,128)}, bf16[2,64,32,128]{3,2,1,0:T(8,128)(2,1)}) custom-call(s32[64,2]{1,0:T(8,128)} %bitcast.34, s32[1]{0:T(128)} %bitcast.6.core_ref, bf16[64,72,128]{2,1,0:T(8,128)(2,1)} %copy-done, bf16[64,72,128]{2,1,0:T(8,128)(2,1)} %copy-done.1, ...), custom_call_target="tpu_custom_call" | custom-call | flops 1000000000 | bytes 12000000 | tf_op jit(solution)/shard_map/pallas_call | solution.py:108
  96.6 21.7 %shard_map.105 = (bf16[128,4096]{1,0:T(8,128)(2,1)}, f32[256,8,128]{2,1,0:T(8,128)}) custom-call(s32[64,2]{1,0:T(8,128)} %bitcast.35, s32[1]{0:T(128)} %bitcast.6.core_ref, bf16[64,72,128]{2,1,0:T(8,128)(2,1)} %copy-done, bf16[64,72,128]{2,1,0:T(8,128)(2,1)} %copy-done.1, bf16[4096,128]{1,0:T(8,128)(2,1)} %get-tuple-element.20.state_ref, ...), custom_call_target="tpu_custom_call" | custom-call | flops 2000000000 | bytes 12000000 | tf_op jit(solution)/shard_map/pallas_call | solution.py:108
  118.3 2.2 %convert_element_type.32 = bf16[256,8,128]{2,1,0:T(8,128)(2,1)} convert(f32[256,8,128]{2,1,0:T(8,128)} %get-tuple-element.23) | non-fusion elementwise | flops 262144 | bytes 1572864 | tf_op jit(solution)/shard_map/convert_element_type | solution.py:412
  120.5 6.6 %all-to-all-start.1 = ((bf16[256,8,128]{2,1,0:T(8,128)(2,1)}), bf16[256,8,128]{2,1,0:T(8,128)(2,1)S(1)}, u32[]{:S(2)}, u32[]{:S(2)}) async-start(bf16[256,8,128]{2,1,0:T(8,128)(2,1)} %convert_element_type.32), calls=%async_computation.1 | async-start | bytes 1048576 | tf_op jit(solution)/shard_map/all_to_all | solution.py:412
  127.1 2.5 %add_convert_fusion = bf16[2,64,32,128]{3,2,1,0:T(8,128)(2,1)} fusion(f32[2,64,32,128]{3,2,1,0:T(8,128)S(1)} %copy-done.2, bf16[2,64,32,128]{3,2,1,0:T(8,128)(2,1)} %collective-permute-done.3), kind=kLoop, calls=%fused_computation.2 | loop fusion | flops 1572864 | bytes 4194304 | tf_op jit(solution)/shard_map/convert_element_type | solution.py:413
  129.7 17.5 %all-to-all-done.1 = bf16[256,8,128]{2,1,0:T(8,128)(2,1)S(1)} async-done(((bf16[256,8,128]{2,1,0:T(8,128)(2,1)}), bf16[256,8,128]{2,1,0:T(8,128)(2,1)S(1)}, u32[]{:S(2)}, u32[]{:S(2)}) %all-to-all-start.1) | async-done | bytes 524320 | tf_op jit(solution)/shard_map/all_to_all | solution.py:412
  147.2 6.4 %all-to-all-start.3 = ((bf16[128,32,128]{2,1,0:T(8,128)(2,1)}), bf16[128,32,128]{2,1,0:T(8,128)(2,1)S(1)}, u32[]{:S(2)}, u32[]{:S(2)}) async-start(bf16[128,32,128]{2,1,0:T(8,128)(2,1)} %bitcast.14), calls=%async_computation.3 | async-start | bytes 2097152 | tf_op jit(solution)/shard_map/all_to_all | solution.py:414
  153.6 0.3 reduce_sum.21
  153.9 29.2 %all-to-all-done.3 = bf16[128,32,128]{2,1,0:T(8,128)(2,1)S(1)} async-done(((bf16[128,32,128]{2,1,0:T(8,128)(2,1)}), bf16[128,32,128]{2,1,0:T(8,128)(2,1)S(1)}, u32[]{:S(2)}, u32[]{:S(2)}) %all-to-all-start.3) | async-done | bytes 1048608 | tf_op jit(solution)/shard_map/all_to_all | solution.py:414
  183.1 0.9 broadcast_in_dim.27
  184.0 8.6 %all-to-all-start.2 = ((bf16[256,8,128]{2,1,0:T(8,128)(2,1)}), bf16[256,8,128]{2,1,0:T(8,128)(2,1)S(1)}, u32[]{:S(2)}, u32[]{:S(2)}) async-start(bf16[256,8,128]{2,1,0:T(8,128)(2,1)} %broadcast_in_dim.27), calls=%async_computation.2 | async-start | bytes 1048576 | tf_op jit(solution)/shard_map/all_to_all | solution.py:416
  192.9 2.4 %collective-permute-start.4 = (f32[32,128]{1,0:T(8,128)S(1)}, f32[32,128]{1,0:T(8,128)S(1)}, u32[]{:S(2)}, u32[]{:S(2)}) collective-permute-start(f32[32,128]{1,0:T(8,128)S(1)} %convert_reduce_fusion), channel_id=1, source_target_pairs={{0,64},{64,0},{128,192},{192,128},{1,65},{65,1},{129,193},{193,129... | collective-permute-start | bytes 49160 | tf_op jit(solution)/shard_map/ppermute | solution.py:422
  195.3 1.7 collective-permute-start.6
  197.2 15.6 %all-to-all-done.2 = bf16[256,8,128]{2,1,0:T(8,128)(2,1)S(1)} async-done(((bf16[256,8,128]{2,1,0:T(8,128)(2,1)}), bf16[256,8,128]{2,1,0:T(8,128)(2,1)S(1)}, u32[]{:S(2)}, u32[]{:S(2)}) %all-to-all-start.2) | async-done | bytes 524320 | tf_op jit(solution)/shard_map/all_to_all | solution.py:416
  212.8 1.1 convert_element_type.33.sums_ref
  213.9 2.2 %shard_map.106 = (f32[9,69,256]{2,1,0:T(8,128)}, f32[24,4096]{1,0:T(8,128)}) custom-call(f32[256,8,128]{2,1,0:T(8,128)} %convert_element_type.33.sums_ref), custom_call_target="tpu_custom_call" | custom-call | tf_op jit(solution)/shard_map/pallas_call | solution.py:369
  216.1 0.6 gather_fusion
  216.7 0.7 bitcast_select_fusion
  (31 shorter events, 1.2 us)
Async XLA Ops:
  2.2 57.4 %copy-start.5 = (s32[2,4,4,8]{3,2,1,0:T(4,128)S(1)}, s32[2,4,4,8]{3,2,1,0:T(4,128)}, u32[]{:S(2)}) copy-start(s32[2,4,4,8]{3,2,1,0:T(4,128)} %param.12) | copy-start | bytes 3076
  2.2 7.2 %collective-permute-start = (bf16[320,256]{1,0:T(8,128)(2,1)S(1)}, bf16[320,256]{1,0:T(8,128)(2,1)S(1)}, u32[]{:S(2)}, u32[]{:S(2)}) collective-permute-start(bf16[320,256]{1,0:T(8,128)(2,1)S(1)} %bitcast.37), channel_id=1, source_target_pairs={{0,1},{1,2},{2,3},{3,4},{4,5},{5,6},{6,7},{7,8},{8,9},{9,10},{10,1... | collective-permute-start | bytes 491528 | tf_op jit(solution)/shard_map/ppermute | solution.py:387
  9.5 50.9 %copy-start.4 = (bf16[320,256]{1,0:T(8,128)(2,1)}, bf16[320,256]{1,0:T(8,128)(2,1)S(1)}, u32[]{:S(2)}) copy-start(bf16[320,256]{1,0:T(8,128)(2,1)S(1)} %collective-permute-done.north_ref) | copy-start | bytes 491524
  54.5 23.4 %copy-start = (bf16[64,72,128]{2,1,0:T(8,128)(2,1)}, bf16[64,72,128]{2,1,0:T(8,128)(2,1)S(1)}, u32[]{:S(2)}) copy-start(bf16[64,72,128]{2,1,0:T(8,128)(2,1)S(1)} %all_to_all.20.own_ref) | copy-start | bytes 3538948
  54.5 24.1 %collective-permute-start.1 = (bf16[64,72,128]{2,1,0:T(8,128)(2,1)S(1)}, bf16[64,72,128]{2,1,0:T(8,128)(2,1)S(1)}, u32[]{:S(2)}, u32[]{:S(2)}) collective-permute-start(bf16[64,72,128]{2,1,0:T(8,128)(2,1)S(1)} %all_to_all.20.own_ref), channel_id=1, source_target_pairs={{0,64},{64,0},{1,65},{65,1},{2,66},{66,2},{3,67},{67,3},{4,68},{68... | collective-permute-start | bytes 3538952 | tf_op jit(solution)/shard_map/ppermute | solution.py:399
  69.9 8.6 %collective-permute-start.2 = (bf16[240,128]{1,0:T(8,128)(2,1)}, bf16[240,128]{1,0:T(8,128)(2,1)S(1)}, u32[]{:S(2)}, u32[]{:S(2)}) collective-permute-start(bf16[240,128]{1,0:T(8,128)(2,1)} %get-tuple-element.19.east_ref), channel_id=1, source_target_pairs={{0,64},{64,128},{128,192},{192,0},{1,65},{65,129},{129,193},{193,1... | collective-permute-start | bytes 184328 | tf_op jit(solution)/shard_map/ppermute | solution.py:397
  78.5 0.6 copy-start.3
  78.6 1.1 copy-start.1
  96.4 30.7 %collective-permute-start.3 = (bf16[2,64,32,128]{3,2,1,0:T(8,128)(2,1)}, bf16[2,64,32,128]{3,2,1,0:T(8,128)(2,1)}, u32[]{:S(2)}, u32[]{:S(2)}) collective-permute-start(bf16[2,64,32,128]{3,2,1,0:T(8,128)(2,1)} %get-tuple-element.26), channel_id=1, source_target_pairs={{0,64},{64,0},{1,65},{65,1},{2,66},{66,2},{3,67},{67,3},{4,68},{68... | collective-permute-start | bytes 3145736 | tf_op jit(solution)/shard_map/ppermute | solution.py:408
  118.3 8.8 %copy-start.2 = (f32[2,64,32,128]{3,2,1,0:T(8,128)S(1)}, f32[2,64,32,128]{3,2,1,0:T(8,128)}, u32[]{:S(2)}) copy-start(f32[2,64,32,128]{3,2,1,0:T(8,128)} %get-tuple-element.25) | copy-start | bytes 6291460
  120.5 26.7 %all-to-all-start.1 = ((bf16[256,8,128]{2,1,0:T(8,128)(2,1)}), bf16[256,8,128]{2,1,0:T(8,128)(2,1)S(1)}, u32[]{:S(2)}, u32[]{:S(2)}) async-start(bf16[256,8,128]{2,1,0:T(8,128)(2,1)} %convert_element_type.32), calls=%async_computation.1 | async-start | bytes 1048576 | tf_op jit(solution)/shard_map/all_to_all | solution.py:412
  147.2 35.9 %all-to-all-start.3 = ((bf16[128,32,128]{2,1,0:T(8,128)(2,1)}), bf16[128,32,128]{2,1,0:T(8,128)(2,1)S(1)}, u32[]{:S(2)}, u32[]{:S(2)}) async-start(bf16[128,32,128]{2,1,0:T(8,128)(2,1)} %bitcast.14), calls=%async_computation.3 | async-start | bytes 2097152 | tf_op jit(solution)/shard_map/all_to_all | solution.py:414
  184.0 28.8 %all-to-all-start.2 = ((bf16[256,8,128]{2,1,0:T(8,128)(2,1)}), bf16[256,8,128]{2,1,0:T(8,128)(2,1)S(1)}, u32[]{:S(2)}, u32[]{:S(2)}) async-start(bf16[256,8,128]{2,1,0:T(8,128)(2,1)} %broadcast_in_dim.27), calls=%async_computation.2 | async-start | bytes 1048576 | tf_op jit(solution)/shard_map/all_to_all | solution.py:416
  192.9 23.2 %collective-permute-start.4 = (f32[32,128]{1,0:T(8,128)S(1)}, f32[32,128]{1,0:T(8,128)S(1)}, u32[]{:S(2)}, u32[]{:S(2)}) collective-permute-start(f32[32,128]{1,0:T(8,128)S(1)} %convert_reduce_fusion), channel_id=1, source_target_pairs={{0,64},{64,0},{128,192},{192,128},{1,65},{65,1},{129,193},{193,129... | collective-permute-start | bytes 49160 | tf_op jit(solution)/shard_map/ppermute | solution.py:422
  195.3 20.9 %collective-permute-start.5 = (f32[32,128]{1,0:T(8,128)S(1)}, f32[32,128]{1,0:T(8,128)S(1)}, u32[]{:S(2)}, u32[]{:S(2)}) collective-permute-start(f32[32,128]{1,0:T(8,128)S(1)} %convert_reduce_fusion), channel_id=1, source_target_pairs={{0,128},{64,192},{128,0},{192,64},{1,129},{65,193},{129,1},{193,65... | collective-permute-start | bytes 49160 | tf_op jit(solution)/shard_map/ppermute | solution.py:422
  195.3 20.9 %collective-permute-start.6 = (f32[32,128]{1,0:T(8,128)S(1)}, f32[32,128]{1,0:T(8,128)S(1)}, u32[]{:S(2)}, u32[]{:S(2)}) collective-permute-start(f32[32,128]{1,0:T(8,128)S(1)} %convert_reduce_fusion), channel_id=1, source_target_pairs={{0,192},{64,128},{128,64},{192,0},{1,193},{65,129},{129,65},{193,1... | collective-permute-start | bytes 49160 | tf_op jit(solution)/shard_map/ppermute | solution.py:422

commit v3 on v2

v3 whole, which is shorter than its diff:
```python
import jax
import jax.numpy as jnp
from jax import lax
from jax.experimental import pallas as pl
from jax.experimental.pallas import tpu as pltpu
from jax.sharding import Mesh, PartitionSpec as P

BAND = ("y", "xh", "z")
SECTION = ("xl", "core")
ALL = ("xl", "core", "y", "xh", "z")
CIN, COUT, ROWS, PAD = 69, 256, 16, 80
TOK, WIDTH, NBLK, NNZ, NCODE = 128, 4096, 32, 64, 24
F32, BF16 = jnp.float32, jnp.bfloat16
VMEM_LIMIT = 56 * 1024 * 1024


def dot(a, b):
    return jnp.dot(a, b, preferred_element_type=F32)


def patches_kernel(fields_ref, north_ref, z_ref, east_ref, y0, y1, n0, n1):
    row = lax.broadcasted_iota(jnp.int32, (256, 256), 0)
    col = lax.broadcasted_iota(jnp.int32, (256, 256), 1)
    order = (row == (col & 7) * 32 + (col >> 3)).astype(BF16)

    def spread(step, carry):
        rows = pl.ds(pl.multiple_of(step * 368, 16), 368)
        mixed = dot(fields_ref[rows, :], order)
        y0[rows, :] = mixed[:, :128]
        y1[rows, :] = mixed[:, 128:]
        return carry

    lax.fori_loop(0, 6, spread, 0)
    y0[2208:2304, :] = jnp.zeros((96, 128), F32)
    y1[2208:2304, :] = jnp.zeros((96, 128), F32)
    mixed = dot(north_ref[...], order)
    n0[...] = mixed[:, :128]
    n1[...] = mixed[:, 128:]
    lane = lax.broadcasted_iota(jnp.int32, (16, 128), 1)

    def chunk(step, carry):
        for half, (rows_ref, top_ref) in enumerate(((y0, n0), (y1, n1))):
            for a in range(3):
                parts = []
                for s in range(4):
                    for r in range(4):
                        lat = 2 * r + a - 1
                        if lat < 0:
                            at = pl.ds(pl.multiple_of(s * PAD + step * 16, 16), 16)
                            parts.append(top_ref[at, :])
                        else:
                            at = pl.ds(s * CIN * 8 + lat + step * 128, 16, stride=8)
                            parts.append(rows_ref[at, :])
                for bit in (1, 2, 4, 8):
                    high = (lane & (8 * bit)) != 0
                    for i in range(16):
                        if i & bit:
                            continue
                        low_part, high_part = parts[i], parts[i | bit]
                        parts[i] = jnp.where(high, pltpu.roll(high_part, 8 * bit, 1), low_part)
                        parts[i | bit] = jnp.where(
                            high, high_part, pltpu.roll(low_part, 128 - 8 * bit, 1)
                        )
                for q in range(16):
                    at = pl.multiple_of((half * 16 + q + 1) * PAD + step * 16, 16)
                    z_ref[a, pl.ds(at, 16), :] = parts[q].astype(BF16)
                if half == 1:
                    at = pl.multiple_of(a * PAD + step * 16, 16)
                    east_ref[pl.ds(at, 16), :] = parts[15].astype(BF16)
        return carry

    lax.fori_loop(0, PAD // 16, chunk, 0)
    for a in range(3):
        z_ref[a, 0:PAD, :] = jnp.zeros((PAD, 128), BF16)


def make_patches(fields, north):
    return pl.pallas_call(
        patches_kernel,
        out_shape=(
            jax.ShapeDtypeStruct((3, 33 * PAD, 128), BF16),
            jax.ShapeDtypeStruct((3 * PAD, 128), BF16),
        ),
        in_specs=[pl.BlockSpec(memory_space=pltpu.VMEM)] * 2,
        out_specs=(pl.BlockSpec(memory_space=pltpu.VMEM),) * 2,
        scratch_shapes=[
            pltpu.VMEM((2304, 128), F32),
            pltpu.VMEM((2304, 128), F32),
            pltpu.VMEM((320, 128), F32),
            pltpu.VMEM((320, 128), F32),
        ],
        compiler_params=pltpu.CompilerParams(vmem_limit_bytes=VMEM_LIMIT),
        cost_estimate=pl.CostEstimate(flops=2 * 2528 * 256 * 256, bytes_accessed=4000000, transcendentals=0),
    )(fields, north)


OVER_ROWS = (((0,), (0,)), ((), ()))
OVER_LANES = (((1,), (1,)), ((), ()))


def rows_of(b):
    return pl.ds(pl.multiple_of(b * 128, 128), 128)


def vmem_call(kernel, out_shape, scratch, flops, size, *operands, smem=0):
    vmem = pl.BlockSpec(memory_space=pltpu.VMEM)
    scalar = pl.BlockSpec(memory_space=pltpu.SMEM)
    return pl.pallas_call(
        kernel,
        out_shape=out_shape,
        in_specs=[scalar] * smem + [vmem] * (len(operands) - smem),
        out_specs=tuple(vmem for _ in out_shape),
        scratch_shapes=scratch,
        compiler_params=pltpu.CompilerParams(vmem_limit_bytes=VMEM_LIMIT),
        cost_estimate=pl.CostEstimate(flops=flops, bytes_accessed=size, transcendentals=0),
    )(*operands)


def encode_kernel(z_ref, weight_ref, latent_ref, wt, wf):
    for a in range(3):
        wf[...] = jnp.zeros(wf.shape, F32)
        for b in range(3):
            wf[b * PAD:b * PAD + CIN, :] = weight_ref[3 * a + b].astype(F32)
        wt[a] = wf[...].T.astype(BF16)

    def encode_step(k, carry):
        rows = pl.ds(pl.multiple_of(k * 2 * PAD, 16), 3 * PAD)
        total = dot(wt[0], z_ref[0, rows, :])
        total += dot(wt[1], z_ref[1, rows, :])
        total += dot(wt[2], z_ref[2, rows, :])
        latent_ref[pl.ds(k, COUT, stride=16), :] = total
        return carry

    lax.fori_loop(0, 16, encode_step, 0)


def encode(z, weight):
    return vmem_call(
        encode_kernel,
        (jax.ShapeDtypeStruct((WIDTH, TOK), F32),),
        [pltpu.VMEM((3, COUT, 3 * PAD), BF16), pltpu.VMEM((3 * PAD, COUT), F32)],
        2 * 720 * 256 * 2048, 4 * 10**6, z, weight,
    )[0]


def first_column(east_ref, west_ref, a):
    lane = lax.broadcasted_iota(jnp.int32, (PAD, 128), 1)
    own = pltpu.roll(east_ref[a * PAD:(a + 1) * PAD, :].astype(F32), 1, 1)
    other = pltpu.roll(west_ref[a * PAD:(a + 1) * PAD, :].astype(F32), 128 - 7, 1)
    return jnp.where((lane & 7) == 0, other, own).astype(BF16)


def hot_codes(codes_ref, t):
    code = lax.broadcasted_iota(jnp.int32, (NCODE, TOK), 0)
    return (code == codes_ref[t:t + 1, :]).astype(BF16)


def block_of(n, low_first, own_ref, other_ref):
    own, other = own_ref[n, 0:64, :], other_ref[n, 0:64, :]
    return jnp.concatenate(
        [jnp.where(low_first, own, other), jnp.where(low_first, other, own)], axis=0
    )


def pull(coords_ref, low_first, own_ref, other_ref, source, target):
    def body(group, carry):
        items = []
        for u in range(UNROLL):
            n = group * UNROLL + u
            block = block_of(n, low_first, own_ref, other_ref)
            items.append((coords_ref[n, 0], dot(source(coords_ref[n, 1]), block)))
        for i, term in items:
            target[i] = target[i] + term
        return carry

    lax.fori_loop(0, NNZ // UNROLL, body, 0)


def push(coords_ref, low_first, own_ref, other_ref, source, target):
    def body(group, carry):
        items = []
        for u in range(UNROLL):
            n = group * UNROLL + u
            block = block_of(n, low_first, own_ref, other_ref)
            items.append((coords_ref[n, 1], dot(block, source(coords_ref[n, 0]))))
        for j, term in items:
            target[rows_of(j), :] = target[rows_of(j), :] + term
        return carry

    lax.fori_loop(0, NNZ // UNROLL, body, 0)


UNROLL = 8


def adjoint_kernel(
    coords_ref, core_ref, own_ref, other_ref, z_ref, east_ref, west_ref, codes_ref, cot_ref,
    adjoint_ref, out_ref,
    later, sums, turned, gc, left,
):
    low_first = core_ref[0] == 0
    for b in range(NBLK):
        cot = cot_ref[:, b * 128:(b + 1) * 128]
        later[b] = cot
        sums[b] = cot.astype(F32)
    pull(coords_ref, low_first, own_ref, other_ref, lambda j: later[j], sums)

    def between(b, carry):
        adjoint = sums[b].astype(BF16)
        adjoint_ref[b] = adjoint
        sums[b] = adjoint.astype(F32)
        return carry

    lax.fori_loop(0, NBLK, between, 0, unroll=4)
    pull(coords_ref, low_first, own_ref, other_ref, lambda j: adjoint_ref[j], sums)

    def end(b, carry):
        turned[rows_of(b), :] = sums[b].T
        return carry

    lax.fori_loop(0, NBLK, end, 0, unroll=4)
    hot = jnp.concatenate([hot_codes(codes_ref, 0), hot_codes(codes_ref, 1)], axis=1)
    for j in range(NBLK):
        both = jnp.concatenate([adjoint_ref[j], later[j]], axis=0)
        term = dot(hot, both).astype(BF16)
        for third in range(3):
            out_ref[3 * j + third] = term[third * 8:(third + 1) * 8, :]

    def conv_grads(pair, carry):
        adjoint, rows = [], []
        for u in range(2):
            k = 2 * pair + u
            adjoint.append(turned[pl.ds(k, COUT, stride=16), :].astype(BF16))
            rows.append(pl.ds(pl.multiple_of(k * 2 * PAD, 16), 3 * PAD))
        adjoint = jnp.concatenate(adjoint, axis=1)
        for a in range(3):
            patches = jnp.concatenate([z_ref[a, rows[0], :], z_ref[a, rows[1], :]], axis=1)
            gc[a] = gc[a] + lax.dot_general(
                patches, adjoint, OVER_LANES, preferred_element_type=F32
            )
        return carry

    gc[...] = jnp.zeros(gc.shape, F32)
    adjoint = turned[pl.ds(0, COUT, stride=16), :].astype(BF16)
    for a in range(3):
        gc[a, 0:PAD, :] = lax.dot_general(
            first_column(east_ref, west_ref, a), adjoint, OVER_LANES, preferred_element_type=F32
        )
    lax.fori_loop(0, 8, conv_grads, 0)
    left[...] = jnp.zeros(left.shape, F32)
    for tap in range(9):
        a, b = divmod(tap, 3)
        for half in range(2):
            lanes = slice(half * 128, (half + 1) * 128)
            for g in range(8):
                out_ref[96 + (tap * 8 + g) * 2 + half] = (
                    gc[a, b * PAD + g * 8:b * PAD + g * 8 + 8, lanes].astype(BF16)
                )
            at = 5 * (2 * tap + half)
            left[at:at + 5, :] = gc[a, b * PAD + 64:b * PAD + CIN, lanes]
    for m in range(16):
        out_ref[240 + m] = left[m * 8:(m + 1) * 8, :].astype(BF16)


def run_adjoint(coords, core, own, other, z, east, west, codes, cot):
    return vmem_call(
        adjoint_kernel,
        (
            jax.ShapeDtypeStruct((NBLK, TOK, 128), BF16),
            jax.ShapeDtypeStruct((256, 8, 128), BF16),
        ),
        [
            pltpu.VMEM((NBLK, TOK, 128), BF16),
            pltpu.VMEM((NBLK, TOK, 128), F32),
            pltpu.VMEM((WIDTH, TOK), F32),
            pltpu.VMEM((3, 3 * PAD, COUT), F32),
            pltpu.VMEM((128, 128), F32),
        ],
        1500 * 10**6, 8 * 10**6,
        coords, core, own, other, z, east, west, codes, cot, smem=2,
    )


def forward_kernel(
    coords_ref, core_ref, own_ref, other_ref, latent_ref, east_ref, west_ref, weight_ref,
    table_ref, codes_ref, adjoint_ref, cot_ref,
    state_ref, keep_ref, send_ref,
    sums, states, adjoints, wf,
):
    low_first = core_ref[0] == 0
    extra = jnp.zeros((COUT, TOK), F32)
    wf[...] = jnp.zeros(wf.shape, F32)
    for a in range(3):
        wf[0:CIN, :] = weight_ref[3 * a].astype(F32)
        extra += lax.dot_general(
            wf[...].astype(BF16), first_column(east_ref, west_ref, a), OVER_ROWS,
            preferred_element_type=F32,
        )
    at = pl.ds(0, COUT, stride=16)
    sums[...] = latent_ref[...]
    sums[at, :] = sums[at, :] + extra
    hot = hot_codes(codes_ref, 0)
    for b in range(NBLK):
        rows = slice(b * 128, (b + 1) * 128)
        state = sums[rows, :].astype(BF16)
        states[rows, 0:128] = state
        forcing = lax.dot_general(table_ref[:, rows], hot, OVER_ROWS, preferred_element_type=F32)
        sums[rows, :] = state.astype(F32) + forcing
        adjoints[b, 0:128, :] = adjoint_ref[b]
        adjoints[b, 128:256, :] = cot_ref[:, rows]
    push(
        coords_ref, low_first, own_ref, other_ref,
        lambda i: states[rows_of(i), 0:128], sums,
    )

    def end(b, carry):
        rows = rows_of(b)
        state = sums[rows, :].astype(BF16)
        states[rows, 128:256] = state
        state_ref[rows, :] = state
        return carry

    lax.fori_loop(0, NBLK, end, 0, unroll=4)

    def block_grads(group, carry):
        for u in range(UNROLL):
            n = group * UNROLL + u
            i, j = coords_ref[n, 0], coords_ref[n, 1]
            grad = dot(states[rows_of(i), :], adjoints[j])
            low, high = grad[0:64], grad[64:128]
            keep = jnp.where(low_first, low, high)
            send = jnp.where(low_first, high, low).astype(BF16)
            for x in range(2):
                keep_ref[x, n] = keep[x * 32:(x + 1) * 32]
                send_ref[x, n] = send[x * 32:(x + 1) * 32]
        return carry

    lax.fori_loop(0, NNZ // UNROLL, block_grads, 0)


def run_forward(coords, core, own, other, latent, east, west, weight, table, codes, adjoint, cot):
    return vmem_call(
        forward_kernel,
        (
            jax.ShapeDtypeStruct((WIDTH, TOK), BF16),
            jax.ShapeDtypeStruct((2, NNZ, 32, 128), F32),
            jax.ShapeDtypeStruct((2, NNZ, 32, 128), BF16),
        ),
        [
            pltpu.VMEM((WIDTH, TOK), F32),
            pltpu.VMEM((WIDTH, 2 * TOK), BF16),
            pltpu.VMEM((NBLK, 2 * TOK, 128), BF16),
            pltpu.VMEM((PAD, COUT), F32),
        ],
        1000, 1000,
        coords, core, own, other, latent, east, west, weight, table, codes, adjoint, cot, smem=2,
    )


def last_kernel(
    coords_ref, core_ref, own_ref, other_ref, state_ref, table_ref, codes_ref, next_ref, sums,
):
    low_first = core_ref[0] == 0
    hot = hot_codes(codes_ref, 1)
    for b in range(NBLK):
        rows = slice(b * 128, (b + 1) * 128)
        forcing = lax.dot_general(table_ref[:, rows], hot, OVER_ROWS, preferred_element_type=F32)
        sums[rows, :] = state_ref[rows, :].astype(F32) + forcing
    push(coords_ref, low_first, own_ref, other_ref, lambda i: state_ref[rows_of(i), :], sums)
    for b in range(NBLK):
        rows = slice(b * 128, (b + 1) * 128)
        next_ref[:, rows] = sums[rows, :].T.astype(BF16)


def run_last(coords, core, own, other, state, table, codes):
    return vmem_call(
        last_kernel,
        (jax.ShapeDtypeStruct((TOK, WIDTH), BF16),),
        [pltpu.VMEM((WIDTH, TOK), F32)],
        1000, 1000,
        coords, core, own, other, state, table, codes, smem=2,
    )[0]


def unpack_kernel(plane_ref, conv_ref, forcing_ref, left):
    tiles = {}
    for p in range(16):
        for pair in range(8):
            rows = plane_ref[p, 256 + pair * 16:256 + pair * 16 + 16, :].astype(F32)
            for z in range(2):
                xl, yx = divmod(p, 8)
                core, pair_z = divmod(pair, 4)
                m = xl * 128 + core * 64 + yx * 8 + pair_z * 2 + z
                tiles[m] = rows[z * 8:z * 8 + 8]
    for j in range(NBLK):
        for third in range(3):
            forcing_ref[third * 8:(third + 1) * 8, j * 128:(j + 1) * 128] = tiles[3 * j + third]
    for m in range(12):
        left[m * 8:(m + 1) * 8, :] = tiles[240 + m]
    for tap in range(9):
        for half in range(2):
            lanes = slice(half * 128, (half + 1) * 128)
            for g in range(8):
                conv_ref[tap, g * 8:(g + 1) * 8, lanes] = tiles[96 + (tap * 8 + g) * 2 + half]
            at = 5 * (2 * tap + half)
            conv_ref[tap, 64:CIN, lanes] = left[at:at + 5, :]


def unpack(plane):
    return vmem_call(
        unpack_kernel,
        (
            jax.ShapeDtypeStruct((9, CIN, COUT), F32),
            jax.ShapeDtypeStruct((NCODE, WIDTH), F32),
        ),
        [pltpu.VMEM((96, 128), F32)],
        1000, 3 * 10**6, plane,
    )


def per_device(
    fields, conv_weight, kernel_blocks, block_coords, forcing_table, forcing_codes, cotangent
):
    core = lax.axis_index("core")
    top = jnp.pad(fields[:, :, 7, :], ((0, 0), (0, PAD - CIN), (0, 0))).reshape(4 * PAD, 256)

    turned = kernel_blocks[0].T
    half = jnp.where(core == 0, turned[0:64], turned[64:128])
    marks = jnp.pad(block_coords.astype(BF16), ((0, 7), (0, 126)))
    payload = jnp.concatenate([half, marks], axis=0)
    north = lax.ppermute(top, BAND, [(i, i + 1) for i in range(63)])
    column = lax.all_to_all(
        jnp.broadcast_to(payload[None], (8,) + payload.shape), "z", 0, 0, tiled=True
    )
    column, north = lax.optimization_barrier((column, north))
    own = lax.all_to_all(
        jnp.broadcast_to(column[None], (8,) + column.shape), ("y", "xh"), 0, 0, tiled=True
    ).reshape((NNZ,) + payload.shape)
    z, east = make_patches(fields.reshape(-1, 256), north)
    west = lax.ppermute(east, SECTION, [(i, (i + 1) % 4) for i in range(4)])
    latent = encode(z, conv_weight)
    own, latent = lax.optimization_barrier((own, latent))
    other = lax.ppermute(own, "core", [(0, 1), (1, 0)])
    coords = own[:, 64, 0:2].astype(jnp.int32)
    codes = forcing_codes.reshape(2, TOK)
    cot = cotangent.reshape(TOK, WIDTH)
    which = core.astype(jnp.int32).reshape(1)

    adjoint, partial = run_adjoint(coords, which, own, other, z, east, west, codes, cot)
    terms = lax.all_to_all(partial, ALL, 0, 0, tiled=True)
    state, keep, send = run_forward(
        coords, which, own, other, latent, east, west, conv_weight, forcing_table, codes,
        adjoint, cot,
    )
    received = lax.ppermute(send, "core", [(0, 1), (1, 0)])
    latent_next = run_last(coords, which, own, other, state, forcing_table, codes)
    shared = jnp.sum(terms.astype(F32), axis=0).astype(BF16)
    column = lax.all_to_all(
        jnp.broadcast_to(shared[None], (16, 8, 128)), ("core", "z"), 0, 0, tiled=True
    ).reshape(128, 128)
    column, received, latent_next = lax.optimization_barrier((column, received, latent_next))
    chip = (keep + received.astype(F32)).astype(BF16).reshape(16, 256, 128)
    plane = lax.all_to_all(
        jnp.concatenate([chip, jnp.broadcast_to(column[None], (16, 128, 128))], axis=1),
        ("xl", "y", "xh"), 0, 0, tiled=True,
    )
    grad_conv, grad_forcing = unpack(plane)
    quarter = jnp.sum(plane[:, 0:256].astype(F32), axis=0).astype(BF16).reshape(8, 32, 128)
    parts = lax.all_to_all(
        jnp.broadcast_to(quarter[None], (4, 8, 32, 128)).reshape(32, 32, 128),
        ("xl", "core", "z"), 0, 0, tiled=True,
    )
    quarters = jnp.sum(parts.reshape(2, 2, 8, 32, 128).astype(F32), axis=2)
    grad_blocks = jnp.transpose(quarters, (1, 0, 2, 3)).reshape(1, 128, 128)
    return (latent_next.reshape(cotangent.shape), grad_conv, grad_blocks, grad_forcing)


def solution(mesh):
    fine = Mesh(mesh.devices.reshape(2, 2, 4, 2, 8), ALL)
    return jax.shard_map(
        per_device,
        mesh=fine,
        in_specs=(
            P(None, None, BAND, SECTION),
            P(),
            P(BAND, None, None),
            P(BAND, None),
            P(),
            P(None, None, BAND, SECTION),
            P(None, BAND, SECTION, None),
        ),
        out_specs=(P(None, BAND, SECTION, None), P(), P(BAND, None, None), P()),
        check_vma=False,
    )
```

time: 218 us -> 158 us (0.72)
  waiting for transfers between devices: 63.3 us -> 21.4 us
  blocking collectives: 44.8 us -> 24.2 us
  starting transfers between devices: 35.8 us -> 52.9 us
  Pallas kernels: 57.9 us -> 47.6 us
  other arithmetic: 9.46 us -> 3.19 us
  local copies, waits for them, and re-layouts: 5.36 us -> 7.59 us
    all_to_all x3 -> x5, waiting for transfers between devices: 62.3 us -> 17.6 us  [the longest x1 8.74 us: per_device(): lax.all_to_all(jnp.broadcast_to(quarter[None], (4, 8, 32, 128)).reshape(3...]
    all_to_all x3 -> x5, starting transfers between devices: 21.6 us -> 44.7 us  [the longest x1 11.9 us: per_device(): terms = lax.all_to_all(partial, ALL, 0, 0, tiled=True)]
    all_to_all x1, blocking collectives: 44.8 us -> 24.2 us  [per_device(): lax.all_to_all(jnp.concatenate([chip, jnp.broadcast_to(column[None], (16,...]
    pallas_call x3 -> x5, Pallas kernels: 46 us -> 38 us  [vmem_call(): pl.pallas_call(kernel, out_shape=out_shape, in_specs=[scalar] * smem + [v...]
    convert_element_type x3 -> x1, other arithmetic: 5.8 us -> 0.32 us  [per_device(): chip = (keep + received.astype(F32)).astype(BF16).reshape(16, 256, 128)]
    ppermute x3 -> x0, starting transfers between devices: 4.1 us -> none  [per_device(): lax.ppermute(quarter, SECTION, [(i, i ^ flip) for i in range(4)])]
    ppermute x1, starting transfers between devices: 5.19 us -> 2.31 us  [per_device(): other = lax.ppermute(own, 'core', [(0, 1), (1, 0)])]
    broadcast_in_dim x4 -> x5, local copies, waits for them, and re-layouts: 1.18 us -> 3.47 us  [the longest x1 1.17 us: per_device(): jnp.broadcast_to(column[None], (8,) + column.shape)]
  transfers between devices with their start and end apart: 10 -> 9, of which waited for: 4 -> 5; matrix products, arithmetic and copies ran while one was open for 5% -> 2% of each run, Pallas kernels for 19% -> 23%
where the time goes in v3:
time: 158 us
  starting transfers between devices  52.9 us (33%)
  Pallas kernels  47.6 us (30%)
  blocking collectives  24.2 us (15%)
  waiting for transfers between devices  21.4 us (14%)
  local copies, waits for them, and re-layouts  7.59 us (5%)
  other arithmetic  3.19 us (2%)
    pallas_call x5, Pallas kernels, vmem_call(): pl.pallas_call(kernel, out_shape=out_shape, in_specs=[scalar] * smem + [v...  38 us
    all_to_all x1, blocking collectives, per_device(): lax.all_to_all(jnp.concatenate([chip, jnp.broadcast_to(column[None], (16,...  24.2 us
    all_to_all x1, starting transfers between devices, per_device(): terms = lax.all_to_all(partial, ALL, 0, 0, tiled=True)  11.9 us
    all_to_all x1, starting transfers between devices, per_device(): lax.all_to_all(jnp.broadcast_to(column[None], (8,) + column.shape), ('y',...  10.9 us
    pallas_call x1, Pallas kernels, make_patches(): pl.pallas_call(patches_kernel, out_shape=(jax.ShapeDtypeStruct((3, 33 * P...  9.58 us
    all_to_all x1, starting transfers between devices, per_device(): lax.all_to_all(jnp.broadcast_to(payload[None], (8,) + payload.shape), 'z'...  9.01 us
    all_to_all x1, starting transfers between devices, per_device(): lax.all_to_all(jnp.broadcast_to(quarter[None], (4, 8, 32, 128)).reshape(3...  8.75 us
    all_to_all x1, waiting for transfers between devices, per_device(): lax.all_to_all(jnp.broadcast_to(quarter[None], (4, 8, 32, 128)).reshape(3...  8.74 us
  transfers between devices with their start and end apart: 9, of which 5 were waited for; matrix products, arithmetic and copies ran while one was open for 2% of the time, Pallas kernels for 23%

profile of v3, /device:TPU:1, one launch (start us, length us, event | category | flops | bytes accessed | tf_op | source)
XLA Modules:
  0.0 157.6 jit_solution(7726206027947892285)
XLA Ops:
  0.6 0.7 convert_element_type.28
  1.4 0.9 slice_select_fusion
  2.5 0.7 broadcast_in_dim.12
  3.2 9.0 %all-to-all-start = ((bf16[8,72,128]{2,1,0:T(8,128)(2,1)}), bf16[8,72,128]{2,1,0:T(8,128)(2,1)S(1)}, u32[]{:S(2)}, u32[]{:S(2)}) async-start(bf16[8,72,128]{2,1,0:T(8,128)(2,1)} %broadcast_in_dim.12), calls=%async_computation | async-start | bytes 294912 | tf_op jit(solution)/shard_map/all_to_all | solution.py:432
  12.2 1.5 slice.17
  13.8 3.4 %collective-permute-start = (bf16[320,256]{1,0:T(8,128)(2,1)S(1)}, bf16[320,256]{1,0:T(8,128)(2,1)S(1)}, u32[]{:S(2)}, u32[]{:S(2)}) collective-permute-start(bf16[320,256]{1,0:T(8,128)(2,1)S(1)} %bitcast.38), channel_id=1, source_target_pairs={{0,1},{1,2},{2,3},{3,4},{4,5},{5,6},{6,7},{7,8},{8,9},{9,10},{10,1... | collective-permute-start | bytes 491528 | tf_op jit(solution)/shard_map/ppermute | solution.py:431
  17.2 2.9 %collective-permute-done.north_ref = bf16[320,256]{1,0:T(8,128)(2,1)S(1)} collective-permute-done((bf16[320,256]{1,0:T(8,128)(2,1)S(1)}, bf16[320,256]{1,0:T(8,128)(2,1)S(1)}, u32[]{:S(2)}, u32[]{:S(2)}) %collective-permute-start) | collective-permute-done | bytes 163872 | tf_op jit(solution)/shard_map/ppermute | solution.py:431
  20.1 1.2 broadcast_in_dim.13
  21.3 10.9 %all-to-all-start.1 = ((bf16[8,8,72,128]{3,2,1,0:T(8,128)(2,1)}), bf16[8,8,72,128]{3,2,1,0:T(8,128)(2,1)S(1)}, u32[]{:S(2)}, u32[]{:S(2)}) async-start(bf16[8,8,72,128]{3,2,1,0:T(8,128)(2,1)} %broadcast_in_dim.13), calls=%async_computation.1 | async-start | bytes 2359296 | tf_op jit(solution)/shard_map/all_to_all | solution.py:436
  32.2 9.6 %shard_map.102 = (bf16[3,2640,128]{2,1,0:T(8,128)(2,1)}, bf16[240,128]{1,0:T(8,128)(2,1)}) custom-call(bf16[2208,256]{1,0:T(8,128)(2,1)} %bitcast.30, bf16[320,256]{1,0:T(8,128)(2,1)} %copy-done.6), custom_call_target="tpu_custom_call" | custom-call | flops 331350016 | bytes 4000000 | tf_op jit(solution)/shard_map/pallas_call | solution.py:78
  41.8 7.7 %shard_map.103.latent_ref = f32[4096,128]{1,0:T(8,128)} custom-call(bf16[3,2640,128]{2,1,0:T(8,128)(2,1)} %get-tuple-element.22.z_ref, bf16[9,69,256]{2,1,0:T(8,128)(2,1)} %weight_ref.3), custom_call_target="tpu_custom_call" | custom-call | flops 754974720 | bytes 4000000 | tf_op jit(solution)/shard_map/pallas_call | solution.py:108
  49.5 2.3 %collective-permute-start.1 = (bf16[64,72,128]{2,1,0:T(8,128)(2,1)S(1)}, bf16[64,72,128]{2,1,0:T(8,128)(2,1)S(1)}, u32[]{:S(2)}, u32[]{:S(2)}) collective-permute-start(bf16[64,72,128]{2,1,0:T(8,128)(2,1)S(1)} %bitcast.22), channel_id=1, source_target_pairs={{0,64},{64,0},{1,65},{65,1},{2,66},{66,2},{3,67},{67,3},{4,68},{68... | collective-permute-start | bytes 3538952 | tf_op jit(solution)/shard_map/ppermute | solution.py:443
  51.8 0.6 reshape.55.codes_ref
  52.8 0.6 slice_convert_fusion
  53.4 0.8 collective-permute-done.2.west_ref
  54.3 0.6 copy-done.5
  54.8 0.5 copy-done.2
  55.3 11.8 %shard_map.104 = (bf16[32,128,128]{2,1,0:T(8,128)(2,1)}, bf16[256,8,128]{2,1,0:T(8,128)(2,1)}) custom-call(s32[64,2]{1,0:T(8,128)} %bitcast.33, s32[1]{0:T(128)} %bitcast.8.core_ref, bf16[64,72,128]{2,1,0:T(8,128)(2,1)} %bitcast.24, bf16[64,72,128]{2,1,0:T(8,128)(2,1)} %copy-done.2, bf16[3,2640,128]{2,1,0:T(8,128)(2,1)} %get-tuple-element.22.z_ref, ...), custom_call_target="tpu_custom_call" | custom-call | flops 1500000000 | bytes 8000000 | tf_op jit(solution)/shard_map/pallas_call | solution.py:108
  67.1 11.9 %all-to-all-start.2 = ((bf16[256,8,128]{2,1,0:T(8,128)(2,1)}), bf16[256,8,128]{2,1,0:T(8,128)(2,1)S(1)}, u32[]{:S(2)}, u32[]{:S(2)}) async-start(bf16[256,8,128]{2,1,0:T(8,128)(2,1)} %get-tuple-element.25), calls=%async_computation.2 | async-start | bytes 1048576 | tf_op jit(solution)/shard_map/all_to_all | solution.py:450
  79.1 10.3 %shard_map.105 = (bf16[4096,128]{1,0:T(8,128)(2,1)}, f32[2,64,32,128]{3,2,1,0:T(8,128)}, bf16[2,64,32,128]{3,2,1,0:T(8,128)(2,1)}) custom-call(s32[64,2]{1,0:T(8,128)} %bitcast.34, s32[1]{0:T(128)} %bitcast.8.core_ref, bf16[64,72,128]{2,1,0:T(8,128)(2,1)} %bitcast.25, bf16[64,72,128]{2,1,0:T(8,128)(2,1)} %copy-done.2, f32[4096,128]{1,0:T(8,128)} %shard_map.103.latent_ref, ...), custom_call_target="tpu_custom_call" | custom-call | flops 1000 | bytes 1000 | tf_op jit(solution)/shard_map/pallas_call | solution.py:108
  89.3 2.1 %collective-permute-start.3 = (bf16[2,64,32,128]{3,2,1,0:T(8,128)(2,1)}, bf16[2,64,32,128]{3,2,1,0:T(8,128)(2,1)S(1)}, u32[]{:S(2)}, u32[]{:S(2)}) collective-permute-start(bf16[2,64,32,128]{3,2,1,0:T(8,128)(2,1)} %get-tuple-element.28), channel_id=1, source_target_pairs={{0,64},{64,0},{1,65},{65,1},{2,66},{66,2},{3,67},{67,3},{4,68},{68... | collective-permute-start | bytes 3145736 | tf_op jit(solution)/shard_map/ppermute | solution.py:455
  91.5 7.7 %all-to-all-done.2 = bf16[256,8,128]{2,1,0:T(8,128)(2,1)S(1)} async-done(((bf16[256,8,128]{2,1,0:T(8,128)(2,1)}), bf16[256,8,128]{2,1,0:T(8,128)(2,1)S(1)}, u32[]{:S(2)}, u32[]{:S(2)}) %all-to-all-start.2) | async-done | bytes 524320 | tf_op jit(solution)/shard_map/all_to_all | solution.py:450
  99.4 0.6 broadcast_in_dim.14
  100.0 4.1 %all-to-all-start.3 = ((bf16[16,8,128]{2,1,0:T(8,128)(2,1)}), bf16[16,8,128]{2,1,0:T(8,128)(2,1)S(1)}, u32[]{:S(2)}, u32[]{:S(2)}) async-start(bf16[16,8,128]{2,1,0:T(8,128)(2,1)} %broadcast_in_dim.14), calls=%async_computation.3 | async-start | bytes 65536 | tf_op jit(solution)/shard_map/all_to_all | solution.py:458
  104.1 5.8 %shard_map.106 = bf16[128,4096]{1,0:T(8,128)(2,1)} custom-call(s32[64,2]{1,0:T(8,128)} %bitcast.35, s32[1]{0:T(128)} %bitcast.8.core_ref, bf16[64,72,128]{2,1,0:T(8,128)(2,1)} %bitcast.26, bf16[64,72,128]{2,1,0:T(8,128)(2,1)} %copy-done.2, bf16[4096,128]{1,0:T(8,128)(2,1)} %get-tuple-element.29.state_ref, bf16[24,4096]{1,0:T(8,128)(2,1)} %table_ref.3, ...), custom_call_target="tpu_custom_call" | custom-call | flops 1000 | bytes 1000 | tf_op jit(solution)/shard_map/pallas_call | solution.py:108
  110.0 1.2 all-to-all-done.3
  111.7 24.2 %all_to_all.30.plane_ref = bf16[16,384,128]{2,1,0:T(8,128)(2,1)S(1)} all-to-all(bf16[16,384,128]{2,1,0:T(8,128)(2,1)S(1)} %pad_maximum_fusion), channel_id=1, replica_groups=mesh['xl'=2,'core'=2,'y'=4,'xh'=2,'z'=8] {'xl','y','xh'}, dimensions={0} | all-to-all | bytes 3145728 | tf_op jit(solution)/shard_map/all_to_all | solution.py:463
  136.1 0.9 broadcast_in_dim.17
  137.0 8.8 %all-to-all-start.5 = ((bf16[32,32,128]{2,1,0:T(8,128)(2,1)}), bf16[32,32,128]{2,1,0:T(8,128)(2,1)S(1)}, u32[]{:S(2)}, u32[]{:S(2)}) async-start(bf16[32,32,128]{2,1,0:T(8,128)(2,1)} %bitcast.14), calls=%async_computation.5 | async-start | bytes 524288 | tf_op jit(solution)/shard_map/all_to_all | solution.py:469
  145.8 2.4 %shard_map.107 = (f32[9,69,256]{2,1,0:T(8,128)}, f32[24,4096]{1,0:T(8,128)}) custom-call(bf16[16,384,128]{2,1,0:T(8,128)(2,1)} %copy-done.1), custom_call_target="tpu_custom_call" | custom-call | flops 1000 | bytes 3000000 | tf_op jit(solution)/shard_map/pallas_call | solution.py:108
  148.2 8.7 %all-to-all-done.5 = bf16[32,32,128]{2,1,0:T(8,128)(2,1)S(1)} async-done(((bf16[32,32,128]{2,1,0:T(8,128)(2,1)}), bf16[32,32,128]{2,1,0:T(8,128)(2,1)S(1)}, u32[]{:S(2)}, u32[]{:S(2)}) %all-to-all-start.5) | async-done | bytes 262176 | tf_op jit(solution)/shard_map/all_to_all | solution.py:469
  157.0 0.6 copy.46
  (30 shorter events, 1.8 us)
Async XLA Ops:
  3.2 16.9 %all-to-all-start = ((bf16[8,72,128]{2,1,0:T(8,128)(2,1)}), bf16[8,72,128]{2,1,0:T(8,128)(2,1)S(1)}, u32[]{:S(2)}, u32[]{:S(2)}) async-start(bf16[8,72,128]{2,1,0:T(8,128)(2,1)} %broadcast_in_dim.12), calls=%async_computation | async-start | bytes 294912 | tf_op jit(solution)/shard_map/all_to_all | solution.py:432
  13.8 6.3 %collective-permute-start = (bf16[320,256]{1,0:T(8,128)(2,1)S(1)}, bf16[320,256]{1,0:T(8,128)(2,1)S(1)}, u32[]{:S(2)}, u32[]{:S(2)}) collective-permute-start(bf16[320,256]{1,0:T(8,128)(2,1)S(1)} %bitcast.38), channel_id=1, source_target_pairs={{0,1},{1,2},{2,3},{3,4},{4,5},{5,6},{6,7},{7,8},{8,9},{9,10},{10,1... | collective-permute-start | bytes 491528 | tf_op jit(solution)/shard_map/ppermute | solution.py:431
  20.1 1.2 copy-start.6
  21.3 28.2 %all-to-all-start.1 = ((bf16[8,8,72,128]{3,2,1,0:T(8,128)(2,1)}), bf16[8,8,72,128]{3,2,1,0:T(8,128)(2,1)S(1)}, u32[]{:S(2)}, u32[]{:S(2)}) async-start(bf16[8,8,72,128]{3,2,1,0:T(8,128)(2,1)} %broadcast_in_dim.13), calls=%async_computation.1 | async-start | bytes 2359296 | tf_op jit(solution)/shard_map/all_to_all | solution.py:436
  41.8 10.0 %copy-start.7 = (s32[2,4,4,8]{3,2,1,0:T(4,128)S(1)}, s32[2,4,4,8]{3,2,1,0:T(4,128)}, u32[]{:S(2)}) copy-start(s32[2,4,4,8]{3,2,1,0:T(4,128)} %param.12) | copy-start | bytes 3076
  41.8 10.6 %copy-start.4 = (bf16[240,128]{1,0:T(8,128)(2,1)S(1)}, bf16[240,128]{1,0:T(8,128)(2,1)}, u32[]{:S(2)}) copy-start(bf16[240,128]{1,0:T(8,128)(2,1)} %get-tuple-element.24.east_ref) | copy-start | bytes 184324
  49.5 4.8 %copy-start = (bf16[8,8,72,128]{3,2,1,0:T(8,128)(2,1)}, bf16[8,8,72,128]{3,2,1,0:T(8,128)(2,1)S(1)}, u32[]{:S(2)}) copy-start(bf16[8,8,72,128]{3,2,1,0:T(8,128)(2,1)S(1)} %all-to-all-done.1) | copy-start | bytes 3538948
  49.5 4.8 %collective-permute-start.1 = (bf16[64,72,128]{2,1,0:T(8,128)(2,1)S(1)}, bf16[64,72,128]{2,1,0:T(8,128)(2,1)S(1)}, u32[]{:S(2)}, u32[]{:S(2)}) collective-permute-start(bf16[64,72,128]{2,1,0:T(8,128)(2,1)S(1)} %bitcast.22), channel_id=1, source_target_pairs={{0,64},{64,0},{1,65},{65,1},{2,66},{66,2},{3,67},{67,3},{4,68},{68... | collective-permute-start | bytes 3538952 | tf_op jit(solution)/shard_map/ppermute | solution.py:443
  52.4 1.8 %collective-permute-start.2 = (bf16[240,128]{1,0:T(8,128)(2,1)S(1)}, bf16[240,128]{1,0:T(8,128)(2,1)S(1)}, u32[]{:S(2)}, u32[]{:S(2)}) collective-permute-start(bf16[240,128]{1,0:T(8,128)(2,1)S(1)} %copy-done.4), channel_id=1, source_target_pairs={{0,64},{64,128},{128,192},{192,0},{1,65},{65,129},{129,193},{193,1... | collective-permute-start | bytes 184328 | tf_op jit(solution)/shard_map/ppermute | solution.py:440
  54.2 0.6 copy-start.5
  54.3 1.1 copy-start.2
  67.1 32.0 %all-to-all-start.2 = ((bf16[256,8,128]{2,1,0:T(8,128)(2,1)}), bf16[256,8,128]{2,1,0:T(8,128)(2,1)S(1)}, u32[]{:S(2)}, u32[]{:S(2)}) async-start(bf16[256,8,128]{2,1,0:T(8,128)(2,1)} %get-tuple-element.25), calls=%async_computation.2 | async-start | bytes 1048576 | tf_op jit(solution)/shard_map/all_to_all | solution.py:450
  89.3 20.6 %collective-permute-start.3 = (bf16[2,64,32,128]{3,2,1,0:T(8,128)(2,1)}, bf16[2,64,32,128]{3,2,1,0:T(8,128)(2,1)S(1)}, u32[]{:S(2)}, u32[]{:S(2)}) collective-permute-start(bf16[2,64,32,128]{3,2,1,0:T(8,128)(2,1)} %get-tuple-element.28), channel_id=1, source_target_pairs={{0,64},{64,0},{1,65},{65,1},{2,66},{66,2},{3,67},{67,3},{4,68},{68... | collective-permute-start | bytes 3145736 | tf_op jit(solution)/shard_map/ppermute | solution.py:455
  100.0 11.1 %all-to-all-start.3 = ((bf16[16,8,128]{2,1,0:T(8,128)(2,1)}), bf16[16,8,128]{2,1,0:T(8,128)(2,1)S(1)}, u32[]{:S(2)}, u32[]{:S(2)}) async-start(bf16[16,8,128]{2,1,0:T(8,128)(2,1)} %broadcast_in_dim.14), calls=%async_computation.3 | async-start | bytes 65536 | tf_op jit(solution)/shard_map/all_to_all | solution.py:458
  104.1 7.0 %copy-start.3 = (f32[2,64,32,128]{3,2,1,0:T(8,128)S(1)}, f32[2,64,32,128]{3,2,1,0:T(8,128)}, u32[]{:S(2)}) copy-start(f32[2,64,32,128]{3,2,1,0:T(8,128)} %get-tuple-element.31) | copy-start | bytes 6291460
  135.9 9.8 %copy-start.1 = (bf16[16,384,128]{2,1,0:T(8,128)(2,1)}, bf16[16,384,128]{2,1,0:T(8,128)(2,1)S(1)}, u32[]{:S(2)}) copy-start(bf16[16,384,128]{2,1,0:T(8,128)(2,1)S(1)} %all_to_all.30.plane_ref) | copy-start | bytes 4718596
  137.0 19.9 %all-to-all-start.5 = ((bf16[32,32,128]{2,1,0:T(8,128)(2,1)}), bf16[32,32,128]{2,1,0:T(8,128)(2,1)S(1)}, u32[]{:S(2)}, u32[]{:S(2)}) async-start(bf16[32,32,128]{2,1,0:T(8,128)(2,1)} %bitcast.14), calls=%async_computation.5 | async-start | bytes 524288 | tf_op jit(solution)/shard_map/all_to_all | solution.py:469

commit v4 on v3

--- a/solution.py
+++ b/solution.py
@@ -382,16 +382,19 @@
     )[0]
 
 
-def unpack_kernel(plane_ref, conv_ref, forcing_ref, left):
+def unpack_kernel(core_ref, own_ref, other_ref, conv_ref, forcing_ref, left):
+    low_first = core_ref[0] == 0
     tiles = {}
     for p in range(16):
-        for pair in range(8):
-            rows = plane_ref[p, 256 + pair * 16:256 + pair * 16 + 16, :].astype(F32)
-            for z in range(2):
-                xl, yx = divmod(p, 8)
-                core, pair_z = divmod(pair, 4)
-                m = xl * 128 + core * 64 + yx * 8 + pair_z * 2 + z
-                tiles[m] = rows[z * 8:z * 8 + 8]
+        for pair in range(4):
+            own = own_ref[p, pair * 16:pair * 16 + 16, :].astype(F32)
+            other = other_ref[p, pair * 16:pair * 16 + 16, :].astype(F32)
+            both = (jnp.where(low_first, own, other), jnp.where(low_first, other, own))
+            xl, yx = divmod(p, 8)
+            for core in range(2):
+                for z in range(2):
+                    m = xl * 128 + core * 64 + yx * 8 + pair * 2 + z
+                    tiles[m] = both[core][z * 8:z * 8 + 8]
     for j in range(NBLK):
         for third in range(3):
             forcing_ref[third * 8:(third + 1) * 8, j * 128:(j + 1) * 128] = tiles[3 * j + third]
@@ -406,7 +409,7 @@
             conv_ref[tap, 64:CIN, lanes] = left[at:at + 5, :]
 
 
-def unpack(plane):
+def unpack(core, own, other):
     return vmem_call(
         unpack_kernel,
         (
@@ -414,7 +417,7 @@
             jax.ShapeDtypeStruct((NCODE, WIDTH), F32),
         ),
         [pltpu.VMEM((96, 128), F32)],
-        1000, 3 * 10**6, plane,
+        1000, 1000, core, own, other, smem=1,
     )
 
 
@@ -428,6 +431,7 @@
     half = jnp.where(core == 0, turned[0:64], turned[64:128])
     marks = jnp.pad(block_coords.astype(BF16), ((0, 7), (0, 126)))
     payload = jnp.concatenate([half, marks], axis=0)
+    payload, top = lax.optimization_barrier((payload, top))
     north = lax.ppermute(top, BAND, [(i, i + 1) for i in range(63)])
     column = lax.all_to_all(
         jnp.broadcast_to(payload[None], (8,) + payload.shape), "z", 0, 0, tiled=True
@@ -447,24 +451,30 @@
     which = core.astype(jnp.int32).reshape(1)
 
     adjoint, partial = run_adjoint(coords, which, own, other, z, east, west, codes, cot)
-    terms = lax.all_to_all(partial, ALL, 0, 0, tiled=True)
+    terms = lax.all_to_all(
+        partial.reshape(32, 64, 128), ("xl", "core", "y", "xh"), 0, 0, tiled=True
+    )
     state, keep, send = run_forward(
         coords, which, own, other, latent, east, west, conv_weight, forcing_table, codes,
         adjoint, cot,
     )
+    terms, send = lax.optimization_barrier((terms, send))
     received = lax.ppermute(send, "core", [(0, 1), (1, 0)])
     latent_next = run_last(coords, which, own, other, state, forcing_table, codes)
     shared = jnp.sum(terms.astype(F32), axis=0).astype(BF16)
-    column = lax.all_to_all(
-        jnp.broadcast_to(shared[None], (16, 8, 128)), ("core", "z"), 0, 0, tiled=True
-    ).reshape(128, 128)
+    spread = lax.all_to_all(
+        jnp.broadcast_to(shared[None], (8, 64, 128)), "z", 0, 0, tiled=True
+    )
+    column = jnp.sum(spread.astype(F32), axis=0).astype(BF16)
     column, received, latent_next = lax.optimization_barrier((column, received, latent_next))
     chip = (keep + received.astype(F32)).astype(BF16).reshape(16, 256, 128)
     plane = lax.all_to_all(
-        jnp.concatenate([chip, jnp.broadcast_to(column[None], (16, 128, 128))], axis=1),
+        jnp.concatenate([chip, jnp.broadcast_to(column[None], (16, 64, 128))], axis=1),
         ("xl", "y", "xh"), 0, 0, tiled=True,
     )
-    grad_conv, grad_forcing = unpack(plane)
+    half_sums = plane[:, 256:320]
+    other_sums = lax.ppermute(half_sums, "core", [(0, 1), (1, 0)])
+    grad_conv, grad_forcing = unpack(which, half_sums, other_sums)
     quarter = jnp.sum(plane[:, 0:256].astype(F32), axis=0).astype(BF16).reshape(8, 32, 128)
     parts = lax.all_to_all(
         jnp.broadcast_to(quarter[None], (4, 8, 32, 128)).reshape(32, 32, 128),

time: 158 us -> 146 us (0.924)
  starting transfers between devices: 52.9 us -> 45.6 us
  waiting for transfers between devices: 21.4 us -> 16.7 us
    all_to_all x2, waiting for transfers between devices: 8.89 us -> 3.47 us  [the longest x1 1.92 us: per_device(): lax.all_to_all(jnp.broadcast_to(shared[None], (8, 64, 128)), 'z', 0, 0, t...]
    all_to_all x2, starting transfers between devices: 16 us -> 12.2 us  [the longest x1 8.47 us: per_device(): lax.all_to_all(partial.reshape(32, 64, 128), ('xl', 'core', 'y', 'xh'), 0...]
    ppermute x1, starting transfers between devices: 2.14 us -> 0.01 us  [per_device(): received = lax.ppermute(send, 'core', [(0, 1), (1, 0)])]
    all_to_all x1, waiting for transfers between devices: 8.74 us -> 6.76 us  [per_device(): lax.all_to_all(jnp.broadcast_to(quarter[None], (4, 8, 32, 128)).reshape(3...]
    all_to_all x1, starting transfers between devices: 10.9 us -> 9.28 us  [per_device(): lax.all_to_all(jnp.broadcast_to(column[None], (8,) + column.shape), ('y',...]
  transfers between devices with their start and end apart: 9 -> 10, of which waited for: 5 -> 7; matrix products, arithmetic and copies ran while one was open for 2% -> 1% of each run, Pallas kernels for 23% -> 24%
where the time goes in v4:
time: 146 us; the launch traced here: 145 us
  Pallas kernels  47.2 us (32%)
  starting transfers between devices  45.6 us (31%)
  blocking collectives  23.5 us (16%)
  waiting for transfers between devices  16.7 us (11%)
  local copies, waits for them, and re-layouts  8.2 us (6%)
  other arithmetic  3 us (2%)
    pallas_call x5, Pallas kernels, vmem_call(): pl.pallas_call(kernel, out_shape=out_shape, in_specs=[scalar] * smem + [v...  37.6 us
    all_to_all x1, blocking collectives, per_device(): lax.all_to_all(jnp.concatenate([chip, jnp.broadcast_to(column[None], (16,...  23.5 us
    pallas_call x1, Pallas kernels, make_patches(): pl.pallas_call(patches_kernel, out_shape=(jax.ShapeDtypeStruct((3, 33 * P...  9.58 us
    all_to_all x1, starting transfers between devices, per_device(): lax.all_to_all(jnp.broadcast_to(column[None], (8,) + column.shape), ('y',...  9.28 us
    all_to_all x1, starting transfers between devices, per_device(): lax.all_to_all(jnp.broadcast_to(payload[None], (8,) + payload.shape), 'z'...  9.01 us
    all_to_all x1, starting transfers between devices, per_device(): lax.all_to_all(partial.reshape(32, 64, 128), ('xl', 'core', 'y', 'xh'), 0...  8.47 us
    all_to_all x1, starting transfers between devices, per_device(): lax.all_to_all(jnp.broadcast_to(quarter[None], (4, 8, 32, 128)).reshape(3...  7.71 us
    all_to_all x1, waiting for transfers between devices, per_device(): lax.all_to_all(jnp.broadcast_to(quarter[None], (4, 8, 32, 128)).reshape(3...  6.76 us
  transfers between devices with their start and end apart: 10, of which 7 were waited for; matrix products, arithmetic and copies ran while one was open for 1% of the time, Pallas kernels for 24%

profile of v4, /device:TPU:1, one launch (start us, length us, event | category | flops | bytes accessed | tf_op | source)
XLA Modules:
  0.0 145.0 jit_solution(2416486797263206688)
XLA Ops:
  0.6 0.7 convert_element_type.30
  1.4 1.5 %slice.20 = bf16[4,69,1,256]{3,2,1,0:T(2,128)(2,1)S(1)} slice(bf16[4,69,8,256]{3,2,1,0:T(8,128)(2,1)} %param.7), slice={[0:4], [0:69], [7:8], [0:256]} | slice | bytes 282624 | tf_op jit(solution)/shard_map/slice | solution.py:428
  3.0 0.9 slice_select_fusion
  4.1 0.7 broadcast_in_dim.12
  4.8 9.0 %all-to-all-start = ((bf16[8,72,128]{2,1,0:T(8,128)(2,1)}), bf16[8,72,128]{2,1,0:T(8,128)(2,1)S(1)}, u32[]{:S(2)}, u32[]{:S(2)}) async-start(bf16[8,72,128]{2,1,0:T(8,128)(2,1)} %broadcast_in_dim.12), calls=%async_computation | async-start | bytes 294912 | tf_op jit(solution)/shard_map/all_to_all | solution.py:436
  13.8 3.4 %collective-permute-start = (bf16[320,256]{1,0:T(8,128)(2,1)S(1)}, bf16[320,256]{1,0:T(8,128)(2,1)S(1)}, u32[]{:S(2)}, u32[]{:S(2)}) collective-permute-start(bf16[320,256]{1,0:T(8,128)(2,1)S(1)} %bitcast.39), channel_id=1, source_target_pairs={{0,1},{1,2},{2,3},{3,4},{4,5},{5,6},{6,7},{7,8},{8,9},{9,10},{10,1... | collective-permute-start | bytes 491528 | tf_op jit(solution)/shard_map/ppermute | solution.py:435
  17.2 4.2 %collective-permute-done.north_ref = bf16[320,256]{1,0:T(8,128)(2,1)S(1)} collective-permute-done((bf16[320,256]{1,0:T(8,128)(2,1)S(1)}, bf16[320,256]{1,0:T(8,128)(2,1)S(1)}, u32[]{:S(2)}, u32[]{:S(2)}) %collective-permute-start) | collective-permute-done | bytes 163872 | tf_op jit(solution)/shard_map/ppermute | solution.py:435
  21.7 1.2 broadcast_in_dim.13
  22.9 9.3 %all-to-all-start.1 = ((bf16[8,8,72,128]{3,2,1,0:T(8,128)(2,1)}), bf16[8,8,72,128]{3,2,1,0:T(8,128)(2,1)S(1)}, u32[]{:S(2)}, u32[]{:S(2)}) async-start(bf16[8,8,72,128]{3,2,1,0:T(8,128)(2,1)} %broadcast_in_dim.13), calls=%async_computation.1 | async-start | bytes 2359296 | tf_op jit(solution)/shard_map/all_to_all | solution.py:440
  32.2 9.6 %shard_map.102 = (bf16[3,2640,128]{2,1,0:T(8,128)(2,1)}, bf16[240,128]{1,0:T(8,128)(2,1)}) custom-call(bf16[2208,256]{1,0:T(8,128)(2,1)} %bitcast.30, bf16[320,256]{1,0:T(8,128)(2,1)} %copy-done.7), custom_call_target="tpu_custom_call" | custom-call | flops 331350016 | bytes 4000000 | tf_op jit(solution)/shard_map/pallas_call | solution.py:78
  41.8 7.6 %shard_map.103.latent_ref = f32[4096,128]{1,0:T(8,128)} custom-call(bf16[3,2640,128]{2,1,0:T(8,128)(2,1)} %get-tuple-element.28.z_ref, bf16[9,69,256]{2,1,0:T(8,128)(2,1)} %weight_ref.3), custom_call_target="tpu_custom_call" | custom-call | flops 754974720 | bytes 4000000 | tf_op jit(solution)/shard_map/pallas_call | solution.py:108
  49.4 2.3 %collective-permute-start.1 = (bf16[64,72,128]{2,1,0:T(8,128)(2,1)S(1)}, bf16[64,72,128]{2,1,0:T(8,128)(2,1)S(1)}, u32[]{:S(2)}, u32[]{:S(2)}) collective-permute-start(bf16[64,72,128]{2,1,0:T(8,128)(2,1)S(1)} %bitcast.22), channel_id=1, source_target_pairs={{0,64},{64,0},{1,65},{65,1},{2,66},{66,2},{3,67},{67,3},{4,68},{68... | collective-permute-start | bytes 3538952 | tf_op jit(solution)/shard_map/ppermute | solution.py:447
  51.7 0.7 reshape.55.codes_ref
  52.4 1.4 collective-permute-start.2
  53.8 0.6 slice_convert_fusion
  54.5 0.7 collective-permute-done.2.west_ref
  56.2 11.8 %shard_map.104 = (bf16[32,128,128]{2,1,0:T(8,128)(2,1)}, bf16[256,8,128]{2,1,0:T(8,128)(2,1)}) custom-call(s32[64,2]{1,0:T(8,128)} %bitcast.33, s32[1]{0:T(128)} %bitcast.8.core_ref, bf16[64,72,128]{2,1,0:T(8,128)(2,1)} %bitcast.24, bf16[64,72,128]{2,1,0:T(8,128)(2,1)} %copy-done.1, bf16[3,2640,128]{2,1,0:T(8,128)(2,1)} %get-tuple-element.28.z_ref, ...), custom_call_target="tpu_custom_call" | custom-call | flops 1500000000 | bytes 8000000 | tf_op jit(solution)/shard_map/pallas_call | solution.py:108
  68.0 8.5 %all-to-all-start.2 = ((bf16[32,64,128]{2,1,0:T(8,128)(2,1)}), bf16[32,64,128]{2,1,0:T(8,128)(2,1)S(1)}, u32[]{:S(2)}, u32[]{:S(2)}) async-start(bf16[32,64,128]{2,1,0:T(8,128)(2,1)} %bitcast.36), calls=%async_computation.2 | async-start | bytes 1048576 | tf_op jit(solution)/shard_map/all_to_all | solution.py:454
  76.5 10.2 %shard_map.105 = (bf16[4096,128]{1,0:T(8,128)(2,1)}, f32[2,64,32,128]{3,2,1,0:T(8,128)}, bf16[2,64,32,128]{3,2,1,0:T(8,128)(2,1)}) custom-call(s32[64,2]{1,0:T(8,128)} %bitcast.34, s32[1]{0:T(128)} %bitcast.8.core_ref, bf16[64,72,128]{2,1,0:T(8,128)(2,1)} %bitcast.25, bf16[64,72,128]{2,1,0:T(8,128)(2,1)} %copy-done.1, f32[4096,128]{1,0:T(8,128)} %shard_map.103.latent_ref, ...), custom_call_target="tpu_custom_call" | custom-call | flops 1000 | bytes 1000 | tf_op jit(solution)/shard_map/pallas_call | solution.py:108
  86.7 1.6 %all-to-all-done.2 = bf16[32,64,128]{2,1,0:T(8,128)(2,1)S(1)} async-done(((bf16[32,64,128]{2,1,0:T(8,128)(2,1)}), bf16[32,64,128]{2,1,0:T(8,128)(2,1)S(1)}, u32[]{:S(2)}, u32[]{:S(2)}) %all-to-all-start.2) | async-done | bytes 524320 | tf_op jit(solution)/shard_map/all_to_all | solution.py:454
  88.4 0.7 broadcast_in_dim.14
  89.0 3.7 %all-to-all-start.3 = ((bf16[8,64,128]{2,1,0:T(8,128)(2,1)}), bf16[8,64,128]{2,1,0:T(8,128)(2,1)S(1)}, u32[]{:S(2)}, u32[]{:S(2)}) async-start(bf16[8,64,128]{2,1,0:T(8,128)(2,1)} %broadcast_in_dim.14), calls=%async_computation.3 | async-start | bytes 262144 | tf_op jit(solution)/shard_map/all_to_all | solution.py:465
  92.8 5.8 %shard_map.106 = bf16[128,4096]{1,0:T(8,128)(2,1)} custom-call(s32[64,2]{1,0:T(8,128)} %bitcast.35, s32[1]{0:T(128)} %bitcast.8.core_ref, bf16[64,72,128]{2,1,0:T(8,128)(2,1)} %bitcast.26, bf16[64,72,128]{2,1,0:T(8,128)(2,1)} %copy-done.1, bf16[4096,128]{1,0:T(8,128)(2,1)} %get-tuple-element.37.state_ref, bf16[24,4096]{1,0:T(8,128)(2,1)} %table_ref.3, ...), custom_call_target="tpu_custom_call" | custom-call | flops 1000 | bytes 1000 | tf_op jit(solution)/shard_map/pallas_call | solution.py:108
  98.6 1.9 %all-to-all-done.3 = bf16[8,64,128]{2,1,0:T(8,128)(2,1)S(1)} async-done(((bf16[8,64,128]{2,1,0:T(8,128)(2,1)}), bf16[8,64,128]{2,1,0:T(8,128)(2,1)S(1)}, u32[]{:S(2)}, u32[]{:S(2)}) %all-to-all-start.3) | async-done | bytes 131104 | tf_op jit(solution)/shard_map/all_to_all | solution.py:465
  101.1 23.5 %all_to_all.30 = bf16[16,320,128]{2,1,0:T(8,128)(2,1)S(1)} all-to-all(bf16[16,320,128]{2,1,0:T(8,128)(2,1)S(1)} %pad_maximum_fusion), channel_id=1, replica_groups=mesh['xl'=2,'core'=2,'y'=4,'xh'=2,'z'=8] {'xl','y','xh'}, dimensions={0} | all-to-all | bytes 2621440 | tf_op jit(solution)/shard_map/all_to_all | solution.py:471
  124.8 0.7 broadcast_in_dim.17
  125.5 7.7 %all-to-all-start.5 = ((bf16[32,32,128]{2,1,0:T(8,128)(2,1)}), bf16[32,32,128]{2,1,0:T(8,128)(2,1)S(1)}, u32[]{:S(2)}, u32[]{:S(2)}) async-start(bf16[32,32,128]{2,1,0:T(8,128)(2,1)} %bitcast.14), calls=%async_computation.5 | async-start | bytes 524288 | tf_op jit(solution)/shard_map/all_to_all | solution.py:479
  133.6 1.3 collective-permute-done.4.other_ref
  134.9 0.7 copy-done.4
  135.6 2.0 %shard_map.107 = (f32[9,69,256]{2,1,0:T(8,128)}, f32[24,4096]{1,0:T(8,128)}) custom-call(s32[1]{0:T(128)} %bitcast.8.core_ref, bf16[16,64,128]{2,1,0:T(8,128)(2,1)} %copy-done.3, bf16[16,64,128]{2,1,0:T(8,128)(2,1)} %copy-done.4), custom_call_target="tpu_custom_call" | custom-call | flops 1000 | bytes 1000 | tf_op jit(solution)/shard_map/pallas_call | solution.py:108
  137.6 6.8 %all-to-all-done.5 = bf16[32,32,128]{2,1,0:T(8,128)(2,1)S(1)} async-done(((bf16[32,32,128]{2,1,0:T(8,128)(2,1)}), bf16[32,32,128]{2,1,0:T(8,128)(2,1)S(1)}, u32[]{:S(2)}, u32[]{:S(2)}) %all-to-all-start.5) | async-done | bytes 262176 | tf_op jit(solution)/shard_map/all_to_all | solution.py:479
  144.4 0.6 copy.46
  (36 shorter events, 2.9 us)
Async XLA Ops:
  4.8 16.9 %all-to-all-start = ((bf16[8,72,128]{2,1,0:T(8,128)(2,1)}), bf16[8,72,128]{2,1,0:T(8,128)(2,1)S(1)}, u32[]{:S(2)}, u32[]{:S(2)}) async-start(bf16[8,72,128]{2,1,0:T(8,128)(2,1)} %broadcast_in_dim.12), calls=%async_computation | async-start | bytes 294912 | tf_op jit(solution)/shard_map/all_to_all | solution.py:436
  13.8 7.5 %collective-permute-start = (bf16[320,256]{1,0:T(8,128)(2,1)S(1)}, bf16[320,256]{1,0:T(8,128)(2,1)S(1)}, u32[]{:S(2)}, u32[]{:S(2)}) collective-permute-start(bf16[320,256]{1,0:T(8,128)(2,1)S(1)} %bitcast.39), channel_id=1, source_target_pairs={{0,1},{1,2},{2,3},{3,4},{4,5},{5,6},{6,7},{7,8},{8,9},{9,10},{10,1... | collective-permute-start | bytes 491528 | tf_op jit(solution)/shard_map/ppermute | solution.py:435
  21.3 1.6 %copy-start.7 = (bf16[320,256]{1,0:T(8,128)(2,1)}, bf16[320,256]{1,0:T(8,128)(2,1)S(1)}, u32[]{:S(2)}) copy-start(bf16[320,256]{1,0:T(8,128)(2,1)S(1)} %collective-permute-done.north_ref) | copy-start | bytes 491524
  22.9 26.5 %all-to-all-start.1 = ((bf16[8,8,72,128]{3,2,1,0:T(8,128)(2,1)}), bf16[8,8,72,128]{3,2,1,0:T(8,128)(2,1)S(1)}, u32[]{:S(2)}, u32[]{:S(2)}) async-start(bf16[8,8,72,128]{3,2,1,0:T(8,128)(2,1)} %broadcast_in_dim.13), calls=%async_computation.1 | async-start | bytes 2359296 | tf_op jit(solution)/shard_map/all_to_all | solution.py:440
  41.8 10.0 %copy-start.8 = (s32[2,4,4,8]{3,2,1,0:T(4,128)S(1)}, s32[2,4,4,8]{3,2,1,0:T(4,128)}, u32[]{:S(2)}) copy-start(s32[2,4,4,8]{3,2,1,0:T(4,128)} %param.12) | copy-start | bytes 3076
  41.8 10.7 %copy-start.5 = (bf16[240,128]{1,0:T(8,128)(2,1)S(1)}, bf16[240,128]{1,0:T(8,128)(2,1)}, u32[]{:S(2)}) copy-start(bf16[240,128]{1,0:T(8,128)(2,1)} %get-tuple-element.30.east_ref) | copy-start | bytes 184324
  49.4 5.7 %copy-start = (bf16[8,8,72,128]{3,2,1,0:T(8,128)(2,1)}, bf16[8,8,72,128]{3,2,1,0:T(8,128)(2,1)S(1)}, u32[]{:S(2)}) copy-start(bf16[8,8,72,128]{3,2,1,0:T(8,128)(2,1)S(1)} %all-to-all-done.1) | copy-start | bytes 3538948
  49.4 5.7 %collective-permute-start.1 = (bf16[64,72,128]{2,1,0:T(8,128)(2,1)S(1)}, bf16[64,72,128]{2,1,0:T(8,128)(2,1)S(1)}, u32[]{:S(2)}, u32[]{:S(2)}) collective-permute-start(bf16[64,72,128]{2,1,0:T(8,128)(2,1)S(1)} %bitcast.22), channel_id=1, source_target_pairs={{0,64},{64,0},{1,65},{65,1},{2,66},{66,2},{3,67},{67,3},{4,68},{68... | collective-permute-start | bytes 3538952 | tf_op jit(solution)/shard_map/ppermute | solution.py:447
  52.4 2.7 %collective-permute-start.2 = (bf16[240,128]{1,0:T(8,128)(2,1)S(1)}, bf16[240,128]{1,0:T(8,128)(2,1)S(1)}, u32[]{:S(2)}, u32[]{:S(2)}) collective-permute-start(bf16[240,128]{1,0:T(8,128)(2,1)S(1)} %copy-done.5), channel_id=1, source_target_pairs={{0,64},{64,128},{128,192},{192,0},{1,65},{65,129},{129,193},{193,1... | collective-permute-start | bytes 184328 | tf_op jit(solution)/shard_map/ppermute | solution.py:444
  55.1 0.6 copy-start.6
  55.1 1.1 copy-start.1
  68.0 20.3 %all-to-all-start.2 = ((bf16[32,64,128]{2,1,0:T(8,128)(2,1)}), bf16[32,64,128]{2,1,0:T(8,128)(2,1)S(1)}, u32[]{:S(2)}, u32[]{:S(2)}) async-start(bf16[32,64,128]{2,1,0:T(8,128)(2,1)} %bitcast.36), calls=%async_computation.2 | async-start | bytes 1048576 | tf_op jit(solution)/shard_map/all_to_all | solution.py:454
  88.3 12.3 %collective-permute-start.3 = (bf16[2,64,32,128]{3,2,1,0:T(8,128)(2,1)}, bf16[2,64,32,128]{3,2,1,0:T(8,128)(2,1)S(1)}, u32[]{:S(2)}, u32[]{:S(2)}) collective-permute-start(bf16[2,64,32,128]{3,2,1,0:T(8,128)(2,1)} %get-tuple-element.36), channel_id=1, source_target_pairs={{0,64},{64,0},{1,65},{65,1},{2,66},{66,2},{3,67},{67,3},{4,68},{68... | collective-permute-start | bytes 3145736 | tf_op jit(solution)/shard_map/ppermute | solution.py:462
  89.0 11.5 %all-to-all-start.3 = ((bf16[8,64,128]{2,1,0:T(8,128)(2,1)}), bf16[8,64,128]{2,1,0:T(8,128)(2,1)S(1)}, u32[]{:S(2)}, u32[]{:S(2)}) async-start(bf16[8,64,128]{2,1,0:T(8,128)(2,1)} %broadcast_in_dim.14), calls=%async_computation.3 | async-start | bytes 262144 | tf_op jit(solution)/shard_map/all_to_all | solution.py:465
  92.8 7.8 %copy-start.2 = (f32[2,64,32,128]{3,2,1,0:T(8,128)S(1)}, f32[2,64,32,128]{3,2,1,0:T(8,128)}, u32[]{:S(2)}) copy-start(f32[2,64,32,128]{3,2,1,0:T(8,128)} %get-tuple-element.39) | copy-start | bytes 6291460
  125.5 18.9 %all-to-all-start.5 = ((bf16[32,32,128]{2,1,0:T(8,128)(2,1)}), bf16[32,32,128]{2,1,0:T(8,128)(2,1)S(1)}, u32[]{:S(2)}, u32[]{:S(2)}) async-start(bf16[32,32,128]{2,1,0:T(8,128)(2,1)} %bitcast.14), calls=%async_computation.5 | async-start | bytes 524288 | tf_op jit(solution)/shard_map/all_to_all | solution.py:479
  133.2 1.6 %copy-start.3 = (bf16[16,64,128]{2,1,0:T(8,128)(2,1)}, bf16[16,64,128]{2,1,0:T(8,128)(2,1)S(1)}, u32[]{:S(2)}) copy-start(bf16[16,64,128]{2,1,0:T(8,128)(2,1)S(1)} %slice.26.own_ref) | copy-start | bytes 786436
  133.2 1.6 %collective-permute-start.4 = (bf16[16,64,128]{2,1,0:T(8,128)(2,1)S(1)}, bf16[16,64,128]{2,1,0:T(8,128)(2,1)S(1)}, u32[]{:S(2)}, u32[]{:S(2)}) collective-permute-start(bf16[16,64,128]{2,1,0:T(8,128)(2,1)S(1)} %slice.26.own_ref), channel_id=1, source_target_pairs={{0,64},{64,0},{1,65},{65,1},{2,66},{66,2},{3,67},{67,3},{4,68},{68... | collective-permute-start | bytes 786440 | tf_op jit(solution)/shard_map/ppermute | solution.py:476
  134.9 0.7 copy-start.4

commit v5 on v4

--- a/solution.py
+++ b/solution.py
@@ -30,7 +30,7 @@
         y1[rows, :] = mixed[:, 128:]
         return carry
 
-    lax.fori_loop(0, 6, spread, 0)
+    lax.fori_loop(0, 6, spread, 0, unroll=3)
     y0[2208:2304, :] = jnp.zeros((96, 128), F32)
     y1[2208:2304, :] = jnp.zeros((96, 128), F32)
     mixed = dot(north_ref[...], order)
@@ -47,10 +47,10 @@
                         lat = 2 * r + a - 1
                         if lat < 0:
                             at = pl.ds(pl.multiple_of(s * PAD + step * 16, 16), 16)
-                            parts.append(top_ref[at, :])
+                            parts.append(top_ref[at, :].astype(BF16))
                         else:
                             at = pl.ds(s * CIN * 8 + lat + step * 128, 16, stride=8)
-                            parts.append(rows_ref[at, :])
+                            parts.append(rows_ref[at, :].astype(BF16))
                 for bit in (1, 2, 4, 8):
                     high = (lane & (8 * bit)) != 0
                     for i in range(16):
@@ -123,15 +123,19 @@
             wf[b * PAD:b * PAD + CIN, :] = weight_ref[3 * a + b].astype(F32)
         wt[a] = wf[...].T.astype(BF16)
 
-    def encode_step(k, carry):
-        rows = pl.ds(pl.multiple_of(k * 2 * PAD, 16), 3 * PAD)
-        total = dot(wt[0], z_ref[0, rows, :])
-        total += dot(wt[1], z_ref[1, rows, :])
-        total += dot(wt[2], z_ref[2, rows, :])
-        latent_ref[pl.ds(k, COUT, stride=16), :] = total
-        return carry
-
-    lax.fori_loop(0, 16, encode_step, 0)
+    def encode_step(pair, carry):
+        ks = [2 * pair, 2 * pair + 1]
+        rows = [pl.ds(pl.multiple_of(k * 2 * PAD, 16), 3 * PAD) for k in ks]
+        total = None
+        for a in range(3):
+            both = jnp.concatenate([z_ref[a, rows[0], :], z_ref[a, rows[1], :]], axis=1)
+            term = dot(wt[a], both)
+            total = term if a == 0 else total + term
+        for u in range(2):
+            latent_ref[pl.ds(ks[u], COUT, stride=16), :] = total[:, u * 128:(u + 1) * 128]
+        return carry
+
+    lax.fori_loop(0, 8, encode_step, 0, unroll=4)
 
 
 def encode(z, weight):
@@ -190,7 +194,7 @@
     lax.fori_loop(0, NNZ // UNROLL, body, 0)
 
 
-UNROLL = 8
+UNROLL = 64
 
 
 def adjoint_kernel(
@@ -246,7 +250,7 @@
         gc[a, 0:PAD, :] = lax.dot_general(
             first_column(east_ref, west_ref, a), adjoint, OVER_LANES, preferred_element_type=F32
         )
-    lax.fori_loop(0, 8, conv_grads, 0)
+    lax.fori_loop(0, 8, conv_grads, 0, unroll=4)
     left[...] = jnp.zeros(left.shape, F32)
     for tap in range(9):
         a, b = divmod(tap, 3)
@@ -465,13 +469,14 @@
     spread = lax.all_to_all(
         jnp.broadcast_to(shared[None], (8, 64, 128)), "z", 0, 0, tiled=True
     )
+    chip = (keep + received.astype(F32)).astype(BF16).reshape(16, 256, 128)
+    spread, chip = lax.optimization_barrier((spread, chip))
     column = jnp.sum(spread.astype(F32), axis=0).astype(BF16)
-    column, received, latent_next = lax.optimization_barrier((column, received, latent_next))
-    chip = (keep + received.astype(F32)).astype(BF16).reshape(16, 256, 128)
     plane = lax.all_to_all(
         jnp.concatenate([chip, jnp.broadcast_to(column[None], (16, 64, 128))], axis=1),
         ("xl", "y", "xh"), 0, 0, tiled=True,
     )
+    plane, latent_next = lax.optimization_barrier((plane, latent_next))
     half_sums = plane[:, 256:320]
     other_sums = lax.ppermute(half_sums, "core", [(0, 1), (1, 0)])
     grad_conv, grad_forcing = unpack(which, half_sums, other_sums)

time: 146 us -> 137 us (0.938)
  blocking collectives: 23.5 us -> 0 us
  waiting for transfers between devices: 16.7 us -> 39.7 us
  Pallas kernels: 47.2 us -> 35.1 us
  other arithmetic: 3 us -> 5.67 us
    all_to_all x1 -> x0, blocking collectives: 23.5 us -> none  [per_device(): lax.all_to_all(jnp.concatenate([chip, jnp.broadcast_to(column[None], (16,...]
    all_to_all x0 -> x1, waiting for transfers between devices: none -> 12.5 us  [per_device(): lax.all_to_all(jnp.concatenate([chip, jnp.broadcast_to(column[None], (16,...]
    pallas_call x5, Pallas kernels: 37.6 us -> 27.8 us  [vmem_call(): pl.pallas_call(kernel, out_shape=out_shape, in_specs=[scalar] * smem + [v...]
    all_to_all x1, waiting for transfers between devices: 0.01 us -> 4.46 us  [per_device(): lax.all_to_all(jnp.broadcast_to(column[None], (8,) + column.shape), ('y',...]
    all_to_all x0 -> x1, starting transfers between devices: none -> 4.43 us  [per_device(): lax.all_to_all(jnp.concatenate([chip, jnp.broadcast_to(column[None], (16,...]
    all_to_all x1, waiting for transfers between devices: 1.92 us -> 5.85 us  [per_device(): lax.all_to_all(jnp.broadcast_to(shared[None], (8, 64, 128)), 'z', 0, 0, t...]
    all_to_all x1, starting transfers between devices: 8.47 us -> 4.79 us  [per_device(): lax.all_to_all(partial.reshape(32, 64, 128), ('xl', 'core', 'y', 'xh'), 0...]
    pallas_call x1, Pallas kernels: 9.58 us -> 7.23 us  [make_patches(): pl.pallas_call(patches_kernel, out_shape=(jax.ShapeDtypeStruct((3, 33 * P...]
  transfers between devices with their start and end apart: 10 -> 11, of which waited for: 7 -> 9; matrix products, arithmetic and copies ran while one was open for 1% -> 3% of each run, Pallas kernels for 24% -> 19%
where the time goes in v5:
time: 137 us; the launch traced here: 136 us
  starting transfers between devices  46.8 us (34%)
  waiting for transfers between devices  39.7 us (29%)
  Pallas kernels  35.1 us (26%)
  local copies, waits for them, and re-layouts  8.15 us (6%)
  other arithmetic  5.67 us (4%)
    pallas_call x5, Pallas kernels, vmem_call(): pl.pallas_call(kernel, out_shape=out_shape, in_specs=[scalar] * smem + [v...  27.8 us
    all_to_all x1, waiting for transfers between devices, per_device(): lax.all_to_all(jnp.concatenate([chip, jnp.broadcast_to(column[None], (16,...  12.5 us
    all_to_all x1, starting transfers between devices, per_device(): lax.all_to_all(jnp.broadcast_to(column[None], (8,) + column.shape), ('y',...  9.28 us
    all_to_all x1, starting transfers between devices, per_device(): lax.all_to_all(jnp.broadcast_to(payload[None], (8,) + payload.shape), 'z'...  9.01 us
    pallas_call x1, Pallas kernels, make_patches(): pl.pallas_call(patches_kernel, out_shape=(jax.ShapeDtypeStruct((3, 33 * P...  7.23 us
    all_to_all x1, starting transfers between devices, per_device(): lax.all_to_all(jnp.broadcast_to(quarter[None], (4, 8, 32, 128)).reshape(3...  7.04 us
    all_to_all x1, waiting for transfers between devices, per_device(): lax.all_to_all(jnp.broadcast_to(quarter[None], (4, 8, 32, 128)).reshape(3...  6.82 us
    all_to_all x1, waiting for transfers between devices, per_device(): lax.all_to_all(jnp.broadcast_to(shared[None], (8, 64, 128)), 'z', 0, 0, t...  5.85 us
  transfers between devices with their start and end apart: 11, of which 9 were waited for; matrix products, arithmetic and copies ran while one was open for 3% of the time, Pallas kernels for 19%

profile of v5, /device:TPU:1, one launch (start us, length us, event | category | flops | bytes accessed | tf_op | source)
XLA Modules:
  0.0 136.2 jit_solution(1535431561745398619)
XLA Ops:
  1.4 1.5 %slice.20 = bf16[4,69,1,256]{3,2,1,0:T(2,128)(2,1)S(1)} slice(bf16[4,69,8,256]{3,2,1,0:T(8,128)(2,1)} %param.7), slice={[0:4], [0:69], [7:8], [0:256]} | slice | bytes 282624 | tf_op jit(solution)/shard_map/slice | solution.py:432
  3.0 0.9 slice_select_fusion
  4.1 0.7 broadcast_in_dim.12
  4.8 9.0 %all-to-all-start = ((bf16[8,72,128]{2,1,0:T(8,128)(2,1)}), bf16[8,72,128]{2,1,0:T(8,128)(2,1)S(1)}, u32[]{:S(2)}, u32[]{:S(2)}) async-start(bf16[8,72,128]{2,1,0:T(8,128)(2,1)} %broadcast_in_dim.12), calls=%async_computation | async-start | bytes 294912 | tf_op jit(solution)/shard_map/all_to_all | solution.py:440
  13.8 3.4 %collective-permute-start = (bf16[320,256]{1,0:T(8,128)(2,1)S(1)}, bf16[320,256]{1,0:T(8,128)(2,1)S(1)}, u32[]{:S(2)}, u32[]{:S(2)}) collective-permute-start(bf16[320,256]{1,0:T(8,128)(2,1)S(1)} %bitcast.39), channel_id=1, source_target_pairs={{0,1},{1,2},{2,3},{3,4},{4,5},{5,6},{6,7},{7,8},{8,9},{9,10},{10,1... | collective-permute-start | bytes 491528 | tf_op jit(solution)/shard_map/ppermute | solution.py:439
  17.2 4.2 %collective-permute-done.north_ref = bf16[320,256]{1,0:T(8,128)(2,1)S(1)} collective-permute-done((bf16[320,256]{1,0:T(8,128)(2,1)S(1)}, bf16[320,256]{1,0:T(8,128)(2,1)S(1)}, u32[]{:S(2)}, u32[]{:S(2)}) %collective-permute-start) | collective-permute-done | bytes 163872 | tf_op jit(solution)/shard_map/ppermute | solution.py:439
  21.7 1.2 broadcast_in_dim.13
  22.9 9.3 %all-to-all-start.1 = ((bf16[8,8,72,128]{3,2,1,0:T(8,128)(2,1)}), bf16[8,8,72,128]{3,2,1,0:T(8,128)(2,1)S(1)}, u32[]{:S(2)}, u32[]{:S(2)}) async-start(bf16[8,8,72,128]{3,2,1,0:T(8,128)(2,1)} %broadcast_in_dim.13), calls=%async_computation.1 | async-start | bytes 2359296 | tf_op jit(solution)/shard_map/all_to_all | solution.py:444
  32.2 7.2 %shard_map.102 = (bf16[3,2640,128]{2,1,0:T(8,128)(2,1)}, bf16[240,128]{1,0:T(8,128)(2,1)}) custom-call(bf16[2208,256]{1,0:T(8,128)(2,1)} %bitcast.30, bf16[320,256]{1,0:T(8,128)(2,1)} %copy-done.6), custom_call_target="tpu_custom_call" | custom-call | flops 331350016 | bytes 4000000 | tf_op jit(solution)/shard_map/pallas_call | solution.py:78
  39.4 4.6 %shard_map.103.latent_ref = f32[4096,128]{1,0:T(8,128)} custom-call(bf16[3,2640,128]{2,1,0:T(8,128)(2,1)} %get-tuple-element.29.z_ref, bf16[9,69,256]{2,1,0:T(8,128)(2,1)} %weight_ref.3), custom_call_target="tpu_custom_call" | custom-call | flops 754974720 | bytes 4000000 | tf_op jit(solution)/shard_map/pallas_call | solution.py:108
  44.0 4.5 %all-to-all-done.1 = bf16[8,8,72,128]{3,2,1,0:T(8,128)(2,1)S(1)} async-done(((bf16[8,8,72,128]{3,2,1,0:T(8,128)(2,1)}), bf16[8,8,72,128]{3,2,1,0:T(8,128)(2,1)S(1)}, u32[]{:S(2)}, u32[]{:S(2)}) %all-to-all-start.1) | async-done | bytes 1179680 | tf_op jit(solution)/shard_map/all_to_all | solution.py:444
  48.4 3.3 %collective-permute-start.1 = (bf16[64,72,128]{2,1,0:T(8,128)(2,1)S(1)}, bf16[64,72,128]{2,1,0:T(8,128)(2,1)S(1)}, u32[]{:S(2)}, u32[]{:S(2)}) collective-permute-start(bf16[64,72,128]{2,1,0:T(8,128)(2,1)S(1)} %bitcast.22), channel_id=1, source_target_pairs={{0,64},{64,0},{1,65},{65,1},{2,66},{66,2},{3,67},{67,3},{4,68},{68... | collective-permute-start | bytes 3538952 | tf_op jit(solution)/shard_map/ppermute | solution.py:451
  52.4 1.4 %collective-permute-start.2 = (bf16[240,128]{1,0:T(8,128)(2,1)S(1)}, bf16[240,128]{1,0:T(8,128)(2,1)S(1)}, u32[]{:S(2)}, u32[]{:S(2)}) collective-permute-start(bf16[240,128]{1,0:T(8,128)(2,1)S(1)} %copy-done.4), channel_id=1, source_target_pairs={{0,64},{64,128},{128,192},{192,0},{1,65},{65,129},{129,193},{193,1... | collective-permute-start | bytes 184328 | tf_op jit(solution)/shard_map/ppermute | solution.py:448
  54.4 0.7 collective-permute-done.2.west_ref
  56.1 8.7 %shard_map.104 = (bf16[32,128,128]{2,1,0:T(8,128)(2,1)}, bf16[256,8,128]{2,1,0:T(8,128)(2,1)}) custom-call(s32[64,2]{1,0:T(8,128)} %bitcast.33, s32[1]{0:T(128)} %bitcast.8.core_ref, bf16[64,72,128]{2,1,0:T(8,128)(2,1)} %bitcast.24, bf16[64,72,128]{2,1,0:T(8,128)(2,1)} %copy-done.1, bf16[3,2640,128]{2,1,0:T(8,128)(2,1)} %get-tuple-element.29.z_ref, ...), custom_call_target="tpu_custom_call" | custom-call | flops 1500000000 | bytes 8000000 | tf_op jit(solution)/shard_map/pallas_call | solution.py:108
  64.8 4.8 %all-to-all-start.2 = ((bf16[32,64,128]{2,1,0:T(8,128)(2,1)}), bf16[32,64,128]{2,1,0:T(8,128)(2,1)S(1)}, u32[]{:S(2)}, u32[]{:S(2)}) async-start(bf16[32,64,128]{2,1,0:T(8,128)(2,1)} %bitcast.36), calls=%async_computation.2 | async-start | bytes 1048576 | tf_op jit(solution)/shard_map/all_to_all | solution.py:458
  69.6 8.1 %shard_map.105 = (bf16[4096,128]{1,0:T(8,128)(2,1)}, f32[2,64,32,128]{3,2,1,0:T(8,128)}, bf16[2,64,32,128]{3,2,1,0:T(8,128)(2,1)}) custom-call(s32[64,2]{1,0:T(8,128)} %bitcast.34, s32[1]{0:T(128)} %bitcast.8.core_ref, bf16[64,72,128]{2,1,0:T(8,128)(2,1)} %bitcast.25, bf16[64,72,128]{2,1,0:T(8,128)(2,1)} %copy-done.1, f32[4096,128]{1,0:T(8,128)} %shard_map.103.latent_ref, ...), custom_call_target="tpu_custom_call" | custom-call | flops 1000 | bytes 1000 | tf_op jit(solution)/shard_map/pallas_call | solution.py:108
  77.7 3.7 %all-to-all-done.2 = bf16[32,64,128]{2,1,0:T(8,128)(2,1)S(1)} async-done(((bf16[32,64,128]{2,1,0:T(8,128)(2,1)}), bf16[32,64,128]{2,1,0:T(8,128)(2,1)S(1)}, u32[]{:S(2)}, u32[]{:S(2)}) %all-to-all-start.2) | async-done | bytes 524320 | tf_op jit(solution)/shard_map/all_to_all | solution.py:458
  81.5 0.7 broadcast_in_dim.14
  82.1 3.8 %all-to-all-start.3 = ((bf16[8,64,128]{2,1,0:T(8,128)(2,1)}), bf16[8,64,128]{2,1,0:T(8,128)(2,1)S(1)}, u32[]{:S(2)}, u32[]{:S(2)}) async-start(bf16[8,64,128]{2,1,0:T(8,128)(2,1)} %broadcast_in_dim.14), calls=%async_computation.3 | async-start | bytes 262144 | tf_op jit(solution)/shard_map/all_to_all | solution.py:469
  86.0 1.9 %add_convert_fusion = bf16[2,64,32,128]{3,2,1,0:T(8,128)(2,1)S(1)} fusion(f32[2,64,32,128]{3,2,1,0:T(8,128)} %get-tuple-element.37, bf16[2,64,32,128]{3,2,1,0:T(8,128)(2,1)S(1)} %collective-permute-done.3), kind=kLoop, calls=%fused_computation | loop fusion | flops 1572864 | bytes 4194304 | tf_op jit(solution)/shard_map/convert_element_type | solution.py:472
  87.9 5.8 %all-to-all-done.3 = bf16[8,64,128]{2,1,0:T(8,128)(2,1)S(1)} async-done(((bf16[8,64,128]{2,1,0:T(8,128)(2,1)}), bf16[8,64,128]{2,1,0:T(8,128)(2,1)S(1)}, u32[]{:S(2)}, u32[]{:S(2)}) %all-to-all-start.3) | async-done | bytes 131104 | tf_op jit(solution)/shard_map/all_to_all | solution.py:469
  93.8 1.2 pad_maximum_fusion
  95.0 4.4 %all-to-all-start.4 = ((bf16[16,320,128]{2,1,0:T(8,128)(2,1)}), bf16[16,320,128]{2,1,0:T(8,128)(2,1)S(1)}, u32[]{:S(2)}, u32[]{:S(2)}) async-start(bf16[16,320,128]{2,1,0:T(8,128)(2,1)} %pad_maximum_fusion), calls=%async_computation.4 | async-start | bytes 2621440 | tf_op jit(solution)/shard_map/all_to_all | solution.py:475
  99.4 4.5 %shard_map.106 = bf16[128,4096]{1,0:T(8,128)(2,1)} custom-call(s32[64,2]{1,0:T(8,128)} %bitcast.35, s32[1]{0:T(128)} %bitcast.8.core_ref, bf16[64,72,128]{2,1,0:T(8,128)(2,1)} %bitcast.26, bf16[64,72,128]{2,1,0:T(8,128)(2,1)} %copy-done.1, bf16[4096,128]{1,0:T(8,128)(2,1)} %get-tuple-element.41.state_ref, bf16[24,4096]{1,0:T(8,128)(2,1)} %table_ref.3, ...), custom_call_target="tpu_custom_call" | custom-call | flops 1000 | bytes 1000 | tf_op jit(solution)/shard_map/pallas_call | solution.py:108
  103.9 12.5 %all-to-all-done.4 = bf16[16,320,128]{2,1,0:T(8,128)(2,1)S(1)} async-done(((bf16[16,320,128]{2,1,0:T(8,128)(2,1)}), bf16[16,320,128]{2,1,0:T(8,128)(2,1)S(1)}, u32[]{:S(2)}, u32[]{:S(2)}) %all-to-all-start.4) | async-done | bytes 1310752 | tf_op jit(solution)/shard_map/all_to_all | solution.py:475
  116.5 0.7 broadcast_in_dim.17
  117.2 7.0 %all-to-all-start.5 = ((bf16[32,32,128]{2,1,0:T(8,128)(2,1)}), bf16[32,32,128]{2,1,0:T(8,128)(2,1)S(1)}, u32[]{:S(2)}, u32[]{:S(2)}) async-start(bf16[32,32,128]{2,1,0:T(8,128)(2,1)} %bitcast.14), calls=%async_computation.5 | async-start | bytes 524288 | tf_op jit(solution)/shard_map/all_to_all | solution.py:484
  124.7 1.2 collective-permute-done.4.other_ref
  126.0 0.7 copy-done.3
  126.7 2.0 %shard_map.107 = (f32[9,69,256]{2,1,0:T(8,128)}, f32[24,4096]{1,0:T(8,128)}) custom-call(s32[1]{0:T(128)} %bitcast.8.core_ref, bf16[16,64,128]{2,1,0:T(8,128)(2,1)} %copy-done.2, bf16[16,64,128]{2,1,0:T(8,128)(2,1)} %copy-done.3), custom_call_target="tpu_custom_call" | custom-call | flops 1000 | bytes 1000 | tf_op jit(solution)/shard_map/pallas_call | solution.py:108
  128.7 6.8 %all-to-all-done.5 = bf16[32,32,128]{2,1,0:T(8,128)(2,1)S(1)} async-done(((bf16[32,32,128]{2,1,0:T(8,128)(2,1)}), bf16[32,32,128]{2,1,0:T(8,128)(2,1)S(1)}, u32[]{:S(2)}, u32[]{:S(2)}) %all-to-all-start.5) | async-done | bytes 262176 | tf_op jit(solution)/shard_map/all_to_all | solution.py:484
  (35 shorter events, 5.1 us)
Async XLA Ops:
  4.8 16.9 %all-to-all-start = ((bf16[8,72,128]{2,1,0:T(8,128)(2,1)}), bf16[8,72,128]{2,1,0:T(8,128)(2,1)S(1)}, u32[]{:S(2)}, u32[]{:S(2)}) async-start(bf16[8,72,128]{2,1,0:T(8,128)(2,1)} %broadcast_in_dim.12), calls=%async_computation | async-start | bytes 294912 | tf_op jit(solution)/shard_map/all_to_all | solution.py:440
  13.8 7.5 %collective-permute-start = (bf16[320,256]{1,0:T(8,128)(2,1)S(1)}, bf16[320,256]{1,0:T(8,128)(2,1)S(1)}, u32[]{:S(2)}, u32[]{:S(2)}) collective-permute-start(bf16[320,256]{1,0:T(8,128)(2,1)S(1)} %bitcast.39), channel_id=1, source_target_pairs={{0,1},{1,2},{2,3},{3,4},{4,5},{5,6},{6,7},{7,8},{8,9},{9,10},{10,1... | collective-permute-start | bytes 491528 | tf_op jit(solution)/shard_map/ppermute | solution.py:439
  21.3 1.6 %copy-start.6 = (bf16[320,256]{1,0:T(8,128)(2,1)}, bf16[320,256]{1,0:T(8,128)(2,1)S(1)}, u32[]{:S(2)}) copy-start(bf16[320,256]{1,0:T(8,128)(2,1)S(1)} %collective-permute-done.north_ref) | copy-start | bytes 491524
  22.9 25.5 %all-to-all-start.1 = ((bf16[8,8,72,128]{3,2,1,0:T(8,128)(2,1)}), bf16[8,8,72,128]{3,2,1,0:T(8,128)(2,1)S(1)}, u32[]{:S(2)}, u32[]{:S(2)}) async-start(bf16[8,8,72,128]{3,2,1,0:T(8,128)(2,1)} %broadcast_in_dim.13), calls=%async_computation.1 | async-start | bytes 2359296 | tf_op jit(solution)/shard_map/all_to_all | solution.py:444
  39.4 12.3 %copy-start.7 = (s32[2,4,4,8]{3,2,1,0:T(4,128)S(1)}, s32[2,4,4,8]{3,2,1,0:T(4,128)}, u32[]{:S(2)}) copy-start(s32[2,4,4,8]{3,2,1,0:T(4,128)} %param.12) | copy-start | bytes 3076
  39.4 13.0 %copy-start.4 = (bf16[240,128]{1,0:T(8,128)(2,1)S(1)}, bf16[240,128]{1,0:T(8,128)(2,1)}, u32[]{:S(2)}) copy-start(bf16[240,128]{1,0:T(8,128)(2,1)} %get-tuple-element.31.east_ref) | copy-start | bytes 184324
  48.4 6.6 %copy-start = (bf16[8,8,72,128]{3,2,1,0:T(8,128)(2,1)}, bf16[8,8,72,128]{3,2,1,0:T(8,128)(2,1)S(1)}, u32[]{:S(2)}) copy-start(bf16[8,8,72,128]{3,2,1,0:T(8,128)(2,1)S(1)} %all-to-all-done.1) | copy-start | bytes 3538948
  48.4 6.6 %collective-permute-start.1 = (bf16[64,72,128]{2,1,0:T(8,128)(2,1)S(1)}, bf16[64,72,128]{2,1,0:T(8,128)(2,1)S(1)}, u32[]{:S(2)}, u32[]{:S(2)}) collective-permute-start(bf16[64,72,128]{2,1,0:T(8,128)(2,1)S(1)} %bitcast.22), channel_id=1, source_target_pairs={{0,64},{64,0},{1,65},{65,1},{2,66},{66,2},{3,67},{67,3},{4,68},{68... | collective-permute-start | bytes 3538952 | tf_op jit(solution)/shard_map/ppermute | solution.py:451
  52.4 2.7 %collective-permute-start.2 = (bf16[240,128]{1,0:T(8,128)(2,1)S(1)}, bf16[240,128]{1,0:T(8,128)(2,1)S(1)}, u32[]{:S(2)}, u32[]{:S(2)}) collective-permute-start(bf16[240,128]{1,0:T(8,128)(2,1)S(1)} %copy-done.4), channel_id=1, source_target_pairs={{0,64},{64,128},{128,192},{192,0},{1,65},{65,129},{129,193},{193,1... | collective-permute-start | bytes 184328 | tf_op jit(solution)/shard_map/ppermute | solution.py:448
  55.1 0.6 copy-start.5
  55.1 1.1 copy-start.1
  64.8 16.6 %all-to-all-start.2 = ((bf16[32,64,128]{2,1,0:T(8,128)(2,1)}), bf16[32,64,128]{2,1,0:T(8,128)(2,1)S(1)}, u32[]{:S(2)}, u32[]{:S(2)}) async-start(bf16[32,64,128]{2,1,0:T(8,128)(2,1)} %bitcast.36), calls=%async_computation.2 | async-start | bytes 1048576 | tf_op jit(solution)/shard_map/all_to_all | solution.py:458
  81.4 4.6 %collective-permute-start.3 = (bf16[2,64,32,128]{3,2,1,0:T(8,128)(2,1)}, bf16[2,64,32,128]{3,2,1,0:T(8,128)(2,1)S(1)}, u32[]{:S(2)}, u32[]{:S(2)}) collective-permute-start(bf16[2,64,32,128]{3,2,1,0:T(8,128)(2,1)} %get-tuple-element.38), channel_id=1, source_target_pairs={{0,64},{64,0},{1,65},{65,1},{2,66},{66,2},{3,67},{67,3},{4,68},{68... | collective-permute-start | bytes 3145736 | tf_op jit(solution)/shard_map/ppermute | solution.py:466
  82.1 11.6 %all-to-all-start.3 = ((bf16[8,64,128]{2,1,0:T(8,128)(2,1)}), bf16[8,64,128]{2,1,0:T(8,128)(2,1)S(1)}, u32[]{:S(2)}, u32[]{:S(2)}) async-start(bf16[8,64,128]{2,1,0:T(8,128)(2,1)} %broadcast_in_dim.14), calls=%async_computation.3 | async-start | bytes 262144 | tf_op jit(solution)/shard_map/all_to_all | solution.py:469
  95.0 21.4 %all-to-all-start.4 = ((bf16[16,320,128]{2,1,0:T(8,128)(2,1)}), bf16[16,320,128]{2,1,0:T(8,128)(2,1)S(1)}, u32[]{:S(2)}, u32[]{:S(2)}) async-start(bf16[16,320,128]{2,1,0:T(8,128)(2,1)} %pad_maximum_fusion), calls=%async_computation.4 | async-start | bytes 2621440 | tf_op jit(solution)/shard_map/all_to_all | solution.py:475
  117.2 18.3 %all-to-all-start.5 = ((bf16[32,32,128]{2,1,0:T(8,128)(2,1)}), bf16[32,32,128]{2,1,0:T(8,128)(2,1)S(1)}, u32[]{:S(2)}, u32[]{:S(2)}) async-start(bf16[32,32,128]{2,1,0:T(8,128)(2,1)} %bitcast.14), calls=%async_computation.5 | async-start | bytes 524288 | tf_op jit(solution)/shard_map/all_to_all | solution.py:484
  124.3 1.6 %copy-start.2 = (bf16[16,64,128]{2,1,0:T(8,128)(2,1)}, bf16[16,64,128]{2,1,0:T(8,128)(2,1)S(1)}, u32[]{:S(2)}) copy-start(bf16[16,64,128]{2,1,0:T(8,128)(2,1)S(1)} %slice.22.own_ref) | copy-start | bytes 786436
  124.3 1.6 %collective-permute-start.4 = (bf16[16,64,128]{2,1,0:T(8,128)(2,1)S(1)}, bf16[16,64,128]{2,1,0:T(8,128)(2,1)S(1)}, u32[]{:S(2)}, u32[]{:S(2)}) collective-permute-start(bf16[16,64,128]{2,1,0:T(8,128)(2,1)S(1)} %slice.22.own_ref), channel_id=1, source_target_pairs={{0,64},{64,0},{1,65},{65,1},{2,66},{66,2},{3,67},{67,3},{4,68},{68... | collective-permute-start | bytes 786440 | tf_op jit(solution)/shard_map/ppermute | solution.py:481
  125.9 0.7 copy-start.3

commit v6 on v5

--- a/solution.py
+++ b/solution.py
@@ -114,6 +114,25 @@
         compiler_params=pltpu.CompilerParams(vmem_limit_bytes=VMEM_LIMIT),
         cost_estimate=pl.CostEstimate(flops=flops, bytes_accessed=size, transcendentals=0),
     )(*operands)
+
+
+def prepare_kernel(coords_ref, core_ref, block_ref, copies_ref):
+    turned = block_ref[0].astype(F32).T
+    half = jnp.where(core_ref[0] == 0, turned[0:64], turned[64:128])
+    row = lax.broadcasted_iota(jnp.int32, (8, 128), 0)
+    lane = lax.broadcasted_iota(jnp.int32, (8, 128), 1)
+    mark = jnp.where(lane == 0, coords_ref[0, 0], jnp.where(lane == 1, coords_ref[0, 1], 0))
+    mark = jnp.where(row == 0, mark, 0).astype(F32)
+    payload = jnp.concatenate([half, mark], axis=0).astype(BF16)
+    for z in range(8):
+        copies_ref[z] = payload
+
+
+def prepare(coords, core, block):
+    return vmem_call(
+        prepare_kernel, (jax.ShapeDtypeStruct((8, 72, 128), BF16),), [], 1000, 1000,
+        coords, core, block, smem=2,
+    )[0]
 
 
 def encode_kernel(z_ref, weight_ref, latent_ref, wt, wf):
@@ -431,19 +450,15 @@
     core = lax.axis_index("core")
     top = jnp.pad(fields[:, :, 7, :], ((0, 0), (0, PAD - CIN), (0, 0))).reshape(4 * PAD, 256)
 
-    turned = kernel_blocks[0].T
-    half = jnp.where(core == 0, turned[0:64], turned[64:128])
-    marks = jnp.pad(block_coords.astype(BF16), ((0, 7), (0, 126)))
-    payload = jnp.concatenate([half, marks], axis=0)
-    payload, top = lax.optimization_barrier((payload, top))
+    which = core.astype(jnp.int32).reshape(1)
+    copies = prepare(block_coords, which, kernel_blocks)
+    copies, top = lax.optimization_barrier((copies, top))
     north = lax.ppermute(top, BAND, [(i, i + 1) for i in range(63)])
-    column = lax.all_to_all(
-        jnp.broadcast_to(payload[None], (8,) + payload.shape), "z", 0, 0, tiled=True
-    )
+    column = lax.all_to_all(copies, "z", 0, 0, tiled=True)
     column, north = lax.optimization_barrier((column, north))
     own = lax.all_to_all(
         jnp.broadcast_to(column[None], (8,) + column.shape), ("y", "xh"), 0, 0, tiled=True
-    ).reshape((NNZ,) + payload.shape)
+    ).reshape(NNZ, 72, 128)
     z, east = make_patches(fields.reshape(-1, 256), north)
     west = lax.ppermute(east, SECTION, [(i, (i + 1) % 4) for i in range(4)])
     latent = encode(z, conv_weight)
@@ -452,7 +467,6 @@
     coords = own[:, 64, 0:2].astype(jnp.int32)
     codes = forcing_codes.reshape(2, TOK)
     cot = cotangent.reshape(TOK, WIDTH)
-    which = core.astype(jnp.int32).reshape(1)
 
     adjoint, partial = run_adjoint(coords, which, own, other, z, east, west, codes, cot)
     terms = lax.all_to_all(

time: 137 us -> 136 us (level)
  other arithmetic: 5.67 us -> 4.01 us
  Pallas kernels: 35.1 us -> 36.6 us
    pallas_call x5 -> x6, Pallas kernels: 27.8 us -> 29.4 us  [vmem_call(): pl.pallas_call(kernel, out_shape=out_shape, in_specs=[scalar] * smem + [v...]
  transfers between devices with their start and end apart: 11 -> 11, of which waited for: 9 -> 9; matrix products, arithmetic and copies ran while one was open for 3% -> 3% of each run, Pallas kernels for 19% -> 20%
where the time goes in v6:
time: 136 us; the launch traced here: 135 us
  starting transfers between devices  46.7 us (34%)
  waiting for transfers between devices  39.6 us (29%)
  Pallas kernels  36.6 us (27%)
  local copies, waits for them, and re-layouts  7.26 us (5%)
  other arithmetic  4.01 us (3%)
    pallas_call x6, Pallas kernels, vmem_call(): pl.pallas_call(kernel, out_shape=out_shape, in_specs=[scalar] * smem + [v...  29.4 us
    all_to_all x1, waiting for transfers between devices, per_device(): lax.all_to_all(jnp.concatenate([chip, jnp.broadcast_to(column[None], (16,...  12.4 us
    all_to_all x1, starting transfers between devices, per_device(): lax.all_to_all(jnp.broadcast_to(column[None], (8,) + column.shape), ('y',...  9.28 us
    all_to_all x1, starting transfers between devices, per_device(): column = lax.all_to_all(copies, 'z', 0, 0, tiled=True)  9.01 us
    pallas_call x1, Pallas kernels, make_patches(): pl.pallas_call(patches_kernel, out_shape=(jax.ShapeDtypeStruct((3, 33 * P...  7.23 us
    all_to_all x1, starting transfers between devices, per_device(): lax.all_to_all(jnp.broadcast_to(quarter[None], (4, 8, 32, 128)).reshape(3...  7.13 us
    all_to_all x1, waiting for transfers between devices, per_device(): lax.all_to_all(jnp.broadcast_to(quarter[None], (4, 8, 32, 128)).reshape(3...  6.82 us
    all_to_all x1, waiting for transfers between devices, per_device(): lax.all_to_all(jnp.broadcast_to(shared[None], (8, 64, 128)), 'z', 0, 0, t...  5.85 us
  transfers between devices with their start and end apart: 11, of which 9 were waited for; matrix products, arithmetic and copies ran while one was open for 3% of the time, Pallas kernels for 20%

profile of v6, /device:TPU:1, one launch (start us, length us, event | category | flops | bytes accessed | tf_op | source)
XLA Modules:
  0.0 135.0 jit_solution(12983982887207818915)
XLA Ops:
  0.6 1.5 %slice.12 = bf16[4,69,1,256]{3,2,1,0:T(2,128)(2,1)S(1)} slice(bf16[4,69,8,256]{3,2,1,0:T(8,128)(2,1)} %param.7), slice={[0:4], [0:69], [7:8], [0:256]} | slice | bytes 282624 | tf_op jit(solution)/shard_map/slice | solution.py:451
  2.2 1.5 %shard_map.102 = bf16[8,72,128]{2,1,0:T(8,128)(2,1)} custom-call(s32[1,2]{1,0:T(1,128)} %coords_ref.1, s32[1]{0:T(128)} %bitcast.core_ref, bf16[1,128,128]{2,1,0:T(8,128)(2,1)} %block_ref.1), custom_call_target="tpu_custom_call" | custom-call | flops 1000 | bytes 1000 | tf_op jit(solution)/shard_map/pallas_call | solution.py:108
  3.8 9.0 %all-to-all-start = ((bf16[8,72,128]{2,1,0:T(8,128)(2,1)}), bf16[8,72,128]{2,1,0:T(8,128)(2,1)S(1)}, u32[]{:S(2)}, u32[]{:S(2)}) async-start(bf16[8,72,128]{2,1,0:T(8,128)(2,1)} %shard_map.102), calls=%async_computation | async-start | bytes 294912 | tf_op jit(solution)/shard_map/all_to_all | solution.py:457
  12.8 3.4 %collective-permute-start = (bf16[320,256]{1,0:T(8,128)(2,1)S(1)}, bf16[320,256]{1,0:T(8,128)(2,1)S(1)}, u32[]{:S(2)}, u32[]{:S(2)}) collective-permute-start(bf16[320,256]{1,0:T(8,128)(2,1)S(1)} %bitcast.36), channel_id=1, source_target_pairs={{0,1},{1,2},{2,3},{3,4},{4,5},{5,6},{6,7},{7,8},{8,9},{9,10},{10,1... | collective-permute-start | bytes 491528 | tf_op jit(solution)/shard_map/ppermute | solution.py:456
  16.2 4.2 %collective-permute-done.north_ref = bf16[320,256]{1,0:T(8,128)(2,1)S(1)} collective-permute-done((bf16[320,256]{1,0:T(8,128)(2,1)S(1)}, bf16[320,256]{1,0:T(8,128)(2,1)S(1)}, u32[]{:S(2)}, u32[]{:S(2)}) %collective-permute-start) | collective-permute-done | bytes 163872 | tf_op jit(solution)/shard_map/ppermute | solution.py:456
  20.7 1.2 broadcast_in_dim.10
  21.9 9.3 %all-to-all-start.1 = ((bf16[8,8,72,128]{3,2,1,0:T(8,128)(2,1)}), bf16[8,8,72,128]{3,2,1,0:T(8,128)(2,1)S(1)}, u32[]{:S(2)}, u32[]{:S(2)}) async-start(bf16[8,8,72,128]{3,2,1,0:T(8,128)(2,1)} %broadcast_in_dim.10), calls=%async_computation.1 | async-start | bytes 2359296 | tf_op jit(solution)/shard_map/all_to_all | solution.py:459
  31.1 7.2 %shard_map.103 = (bf16[3,2640,128]{2,1,0:T(8,128)(2,1)}, bf16[240,128]{1,0:T(8,128)(2,1)}) custom-call(bf16[2208,256]{1,0:T(8,128)(2,1)} %bitcast.27, bf16[320,256]{1,0:T(8,128)(2,1)} %copy-done.6), custom_call_target="tpu_custom_call" | custom-call | flops 331350016 | bytes 4000000 | tf_op jit(solution)/shard_map/pallas_call | solution.py:78
  38.4 4.6 %shard_map.104.latent_ref = f32[4096,128]{1,0:T(8,128)} custom-call(bf16[3,2640,128]{2,1,0:T(8,128)(2,1)} %get-tuple-element.29.z_ref, bf16[9,69,256]{2,1,0:T(8,128)(2,1)} %weight_ref.3), custom_call_target="tpu_custom_call" | custom-call | flops 754974720 | bytes 4000000 | tf_op jit(solution)/shard_map/pallas_call | solution.py:108
  43.0 4.5 %all-to-all-done.1 = bf16[8,8,72,128]{3,2,1,0:T(8,128)(2,1)S(1)} async-done(((bf16[8,8,72,128]{3,2,1,0:T(8,128)(2,1)}), bf16[8,8,72,128]{3,2,1,0:T(8,128)(2,1)S(1)}, u32[]{:S(2)}, u32[]{:S(2)}) %all-to-all-start.1) | async-done | bytes 1179680 | tf_op jit(solution)/shard_map/all_to_all | solution.py:459
  47.4 3.3 %collective-permute-start.1 = (bf16[64,72,128]{2,1,0:T(8,128)(2,1)S(1)}, bf16[64,72,128]{2,1,0:T(8,128)(2,1)S(1)}, u32[]{:S(2)}, u32[]{:S(2)}) collective-permute-start(bf16[64,72,128]{2,1,0:T(8,128)(2,1)S(1)} %bitcast.19), channel_id=1, source_target_pairs={{0,64},{64,0},{1,65},{65,1},{2,66},{66,2},{3,67},{67,3},{4,68},{68... | collective-permute-start | bytes 3538952 | tf_op jit(solution)/shard_map/ppermute | solution.py:466
  51.3 1.4 %collective-permute-start.2 = (bf16[240,128]{1,0:T(8,128)(2,1)S(1)}, bf16[240,128]{1,0:T(8,128)(2,1)S(1)}, u32[]{:S(2)}, u32[]{:S(2)}) collective-permute-start(bf16[240,128]{1,0:T(8,128)(2,1)S(1)} %copy-done.4), channel_id=1, source_target_pairs={{0,64},{64,128},{128,192},{192,0},{1,65},{65,129},{129,193},{193,1... | collective-permute-start | bytes 184328 | tf_op jit(solution)/shard_map/ppermute | solution.py:463
  53.4 0.7 collective-permute-done.2.west_ref
  55.1 8.7 %shard_map.105 = (bf16[32,128,128]{2,1,0:T(8,128)(2,1)}, bf16[256,8,128]{2,1,0:T(8,128)(2,1)}) custom-call(s32[64,2]{1,0:T(8,128)} %bitcast.30, s32[1]{0:T(128)} %bitcast.core_ref, bf16[64,72,128]{2,1,0:T(8,128)(2,1)} %bitcast.21, bf16[64,72,128]{2,1,0:T(8,128)(2,1)} %copy-done.1, bf16[3,2640,128]{2,1,0:T(8,128)(2,1)} %get-tuple-element.29.z_ref, ...), custom_call_target="tpu_custom_call" | custom-call | flops 1500000000 | bytes 8000000 | tf_op jit(solution)/shard_map/pallas_call | solution.py:108
  63.8 4.8 %all-to-all-start.2 = ((bf16[32,64,128]{2,1,0:T(8,128)(2,1)}), bf16[32,64,128]{2,1,0:T(8,128)(2,1)S(1)}, u32[]{:S(2)}, u32[]{:S(2)}) async-start(bf16[32,64,128]{2,1,0:T(8,128)(2,1)} %bitcast.33), calls=%async_computation.2 | async-start | bytes 1048576 | tf_op jit(solution)/shard_map/all_to_all | solution.py:472
  68.6 8.1 %shard_map.106 = (bf16[4096,128]{1,0:T(8,128)(2,1)}, f32[2,64,32,128]{3,2,1,0:T(8,128)}, bf16[2,64,32,128]{3,2,1,0:T(8,128)(2,1)}) custom-call(s32[64,2]{1,0:T(8,128)} %bitcast.31, s32[1]{0:T(128)} %bitcast.core_ref, bf16[64,72,128]{2,1,0:T(8,128)(2,1)} %bitcast.22, bf16[64,72,128]{2,1,0:T(8,128)(2,1)} %copy-done.1, f32[4096,128]{1,0:T(8,128)} %shard_map.104.latent_ref, ...), custom_call_target="tpu_custom_call" | custom-call | flops 1000 | bytes 1000 | tf_op jit(solution)/shard_map/pallas_call | solution.py:108
  76.7 3.7 %all-to-all-done.2 = bf16[32,64,128]{2,1,0:T(8,128)(2,1)S(1)} async-done(((bf16[32,64,128]{2,1,0:T(8,128)(2,1)}), bf16[32,64,128]{2,1,0:T(8,128)(2,1)S(1)}, u32[]{:S(2)}, u32[]{:S(2)}) %all-to-all-start.2) | async-done | bytes 524320 | tf_op jit(solution)/shard_map/all_to_all | solution.py:472
  80.4 0.7 broadcast_in_dim.11
  81.1 3.8 %all-to-all-start.3 = ((bf16[8,64,128]{2,1,0:T(8,128)(2,1)}), bf16[8,64,128]{2,1,0:T(8,128)(2,1)S(1)}, u32[]{:S(2)}, u32[]{:S(2)}) async-start(bf16[8,64,128]{2,1,0:T(8,128)(2,1)} %broadcast_in_dim.11), calls=%async_computation.3 | async-start | bytes 262144 | tf_op jit(solution)/shard_map/all_to_all | solution.py:483
  85.0 1.9 %add_convert_fusion = bf16[2,64,32,128]{3,2,1,0:T(8,128)(2,1)S(1)} fusion(f32[2,64,32,128]{3,2,1,0:T(8,128)} %get-tuple-element.37, bf16[2,64,32,128]{3,2,1,0:T(8,128)(2,1)S(1)} %collective-permute-done.3), kind=kLoop, calls=%fused_computation | loop fusion | flops 1572864 | bytes 4194304 | tf_op jit(solution)/shard_map/convert_element_type | solution.py:486
  86.9 5.8 %all-to-all-done.3 = bf16[8,64,128]{2,1,0:T(8,128)(2,1)S(1)} async-done(((bf16[8,64,128]{2,1,0:T(8,128)(2,1)}), bf16[8,64,128]{2,1,0:T(8,128)(2,1)S(1)}, u32[]{:S(2)}, u32[]{:S(2)}) %all-to-all-start.3) | async-done | bytes 131104 | tf_op jit(solution)/shard_map/all_to_all | solution.py:483
  92.8 1.2 pad_maximum_fusion
  94.0 4.3 %all-to-all-start.4 = ((bf16[16,320,128]{2,1,0:T(8,128)(2,1)}), bf16[16,320,128]{2,1,0:T(8,128)(2,1)S(1)}, u32[]{:S(2)}, u32[]{:S(2)}) async-start(bf16[16,320,128]{2,1,0:T(8,128)(2,1)} %pad_maximum_fusion), calls=%async_computation.4 | async-start | bytes 2621440 | tf_op jit(solution)/shard_map/all_to_all | solution.py:489
  98.2 4.5 %shard_map.107 = bf16[128,4096]{1,0:T(8,128)(2,1)} custom-call(s32[64,2]{1,0:T(8,128)} %bitcast.32, s32[1]{0:T(128)} %bitcast.core_ref, bf16[64,72,128]{2,1,0:T(8,128)(2,1)} %bitcast.23, bf16[64,72,128]{2,1,0:T(8,128)(2,1)} %copy-done.1, bf16[4096,128]{1,0:T(8,128)(2,1)} %get-tuple-element.41.state_ref, bf16[24,4096]{1,0:T(8,128)(2,1)} %table_ref.3, ...), custom_call_target="tpu_custom_call" | custom-call | flops 1000 | bytes 1000 | tf_op jit(solution)/shard_map/pallas_call | solution.py:108
  102.7 12.4 %all-to-all-done.4 = bf16[16,320,128]{2,1,0:T(8,128)(2,1)S(1)} async-done(((bf16[16,320,128]{2,1,0:T(8,128)(2,1)}), bf16[16,320,128]{2,1,0:T(8,128)(2,1)S(1)}, u32[]{:S(2)}, u32[]{:S(2)}) %all-to-all-start.4) | async-done | bytes 1310752 | tf_op jit(solution)/shard_map/all_to_all | solution.py:489
  115.2 0.7 broadcast_in_dim.14
  116.0 7.1 %all-to-all-start.5 = ((bf16[32,32,128]{2,1,0:T(8,128)(2,1)}), bf16[32,32,128]{2,1,0:T(8,128)(2,1)S(1)}, u32[]{:S(2)}, u32[]{:S(2)}) async-start(bf16[32,32,128]{2,1,0:T(8,128)(2,1)} %bitcast.11), calls=%async_computation.5 | async-start | bytes 524288 | tf_op jit(solution)/shard_map/all_to_all | solution.py:498
  123.5 1.2 collective-permute-done.4.other_ref
  124.8 0.7 copy-done.3
  125.5 2.0 %shard_map.108 = (f32[9,69,256]{2,1,0:T(8,128)}, f32[24,4096]{1,0:T(8,128)}) custom-call(s32[1]{0:T(128)} %bitcast.core_ref, bf16[16,64,128]{2,1,0:T(8,128)(2,1)} %copy-done.2, bf16[16,64,128]{2,1,0:T(8,128)(2,1)} %copy-done.3), custom_call_target="tpu_custom_call" | custom-call | flops 1000 | bytes 1000 | tf_op jit(solution)/shard_map/pallas_call | solution.py:108
  127.5 6.8 %all-to-all-done.5 = bf16[32,32,128]{2,1,0:T(8,128)(2,1)S(1)} async-done(((bf16[32,32,128]{2,1,0:T(8,128)(2,1)}), bf16[32,32,128]{2,1,0:T(8,128)(2,1)S(1)}, u32[]{:S(2)}, u32[]{:S(2)}) %all-to-all-start.5) | async-done | bytes 262176 | tf_op jit(solution)/shard_map/all_to_all | solution.py:498
  134.4 0.6 copy.36
  (30 shorter events, 3.5 us)
Async XLA Ops:
  3.8 16.9 %all-to-all-start = ((bf16[8,72,128]{2,1,0:T(8,128)(2,1)}), bf16[8,72,128]{2,1,0:T(8,128)(2,1)S(1)}, u32[]{:S(2)}, u32[]{:S(2)}) async-start(bf16[8,72,128]{2,1,0:T(8,128)(2,1)} %shard_map.102), calls=%async_computation | async-start | bytes 294912 | tf_op jit(solution)/shard_map/all_to_all | solution.py:457
  12.8 7.5 %collective-permute-start = (bf16[320,256]{1,0:T(8,128)(2,1)S(1)}, bf16[320,256]{1,0:T(8,128)(2,1)S(1)}, u32[]{:S(2)}, u32[]{:S(2)}) collective-permute-start(bf16[320,256]{1,0:T(8,128)(2,1)S(1)} %bitcast.36), channel_id=1, source_target_pairs={{0,1},{1,2},{2,3},{3,4},{4,5},{5,6},{6,7},{7,8},{8,9},{9,10},{10,1... | collective-permute-start | bytes 491528 | tf_op jit(solution)/shard_map/ppermute | solution.py:456
  20.3 1.6 %copy-start.6 = (bf16[320,256]{1,0:T(8,128)(2,1)}, bf16[320,256]{1,0:T(8,128)(2,1)S(1)}, u32[]{:S(2)}) copy-start(bf16[320,256]{1,0:T(8,128)(2,1)S(1)} %collective-permute-done.north_ref) | copy-start | bytes 491524
  21.9 25.5 %all-to-all-start.1 = ((bf16[8,8,72,128]{3,2,1,0:T(8,128)(2,1)}), bf16[8,8,72,128]{3,2,1,0:T(8,128)(2,1)S(1)}, u32[]{:S(2)}, u32[]{:S(2)}) async-start(bf16[8,8,72,128]{3,2,1,0:T(8,128)(2,1)} %broadcast_in_dim.10), calls=%async_computation.1 | async-start | bytes 2359296 | tf_op jit(solution)/shard_map/all_to_all | solution.py:459
  38.4 12.3 %copy-start.7 = (s32[2,4,4,8]{3,2,1,0:T(4,128)S(1)}, s32[2,4,4,8]{3,2,1,0:T(4,128)}, u32[]{:S(2)}) copy-start(s32[2,4,4,8]{3,2,1,0:T(4,128)} %param.12) | copy-start | bytes 3076
  38.4 13.0 %copy-start.4 = (bf16[240,128]{1,0:T(8,128)(2,1)S(1)}, bf16[240,128]{1,0:T(8,128)(2,1)}, u32[]{:S(2)}) copy-start(bf16[240,128]{1,0:T(8,128)(2,1)} %get-tuple-element.31.east_ref) | copy-start | bytes 184324
  47.4 6.6 %copy-start = (bf16[8,8,72,128]{3,2,1,0:T(8,128)(2,1)}, bf16[8,8,72,128]{3,2,1,0:T(8,128)(2,1)S(1)}, u32[]{:S(2)}) copy-start(bf16[8,8,72,128]{3,2,1,0:T(8,128)(2,1)S(1)} %all-to-all-done.1) | copy-start | bytes 3538948
  47.4 6.6 %collective-permute-start.1 = (bf16[64,72,128]{2,1,0:T(8,128)(2,1)S(1)}, bf16[64,72,128]{2,1,0:T(8,128)(2,1)S(1)}, u32[]{:S(2)}, u32[]{:S(2)}) collective-permute-start(bf16[64,72,128]{2,1,0:T(8,128)(2,1)S(1)} %bitcast.19), channel_id=1, source_target_pairs={{0,64},{64,0},{1,65},{65,1},{2,66},{66,2},{3,67},{67,3},{4,68},{68... | collective-permute-start | bytes 3538952 | tf_op jit(solution)/shard_map/ppermute | solution.py:466
  51.3 2.7 %collective-permute-start.2 = (bf16[240,128]{1,0:T(8,128)(2,1)S(1)}, bf16[240,128]{1,0:T(8,128)(2,1)S(1)}, u32[]{:S(2)}, u32[]{:S(2)}) collective-permute-start(bf16[240,128]{1,0:T(8,128)(2,1)S(1)} %copy-done.4), channel_id=1, source_target_pairs={{0,64},{64,128},{128,192},{192,0},{1,65},{65,129},{129,193},{193,1... | collective-permute-start | bytes 184328 | tf_op jit(solution)/shard_map/ppermute | solution.py:463
  54.0 0.6 copy-start.5
  54.1 1.1 copy-start.1
  63.8 16.6 %all-to-all-start.2 = ((bf16[32,64,128]{2,1,0:T(8,128)(2,1)}), bf16[32,64,128]{2,1,0:T(8,128)(2,1)S(1)}, u32[]{:S(2)}, u32[]{:S(2)}) async-start(bf16[32,64,128]{2,1,0:T(8,128)(2,1)} %bitcast.33), calls=%async_computation.2 | async-start | bytes 1048576 | tf_op jit(solution)/shard_map/all_to_all | solution.py:472
  80.3 4.6 %collective-permute-start.3 = (bf16[2,64,32,128]{3,2,1,0:T(8,128)(2,1)}, bf16[2,64,32,128]{3,2,1,0:T(8,128)(2,1)S(1)}, u32[]{:S(2)}, u32[]{:S(2)}) collective-permute-start(bf16[2,64,32,128]{3,2,1,0:T(8,128)(2,1)} %get-tuple-element.38), channel_id=1, source_target_pairs={{0,64},{64,0},{1,65},{65,1},{2,66},{66,2},{3,67},{67,3},{4,68},{68... | collective-permute-start | bytes 3145736 | tf_op jit(solution)/shard_map/ppermute | solution.py:480
  81.1 11.6 %all-to-all-start.3 = ((bf16[8,64,128]{2,1,0:T(8,128)(2,1)}), bf16[8,64,128]{2,1,0:T(8,128)(2,1)S(1)}, u32[]{:S(2)}, u32[]{:S(2)}) async-start(bf16[8,64,128]{2,1,0:T(8,128)(2,1)} %broadcast_in_dim.11), calls=%async_computation.3 | async-start | bytes 262144 | tf_op jit(solution)/shard_map/all_to_all | solution.py:483
  94.0 21.1 %all-to-all-start.4 = ((bf16[16,320,128]{2,1,0:T(8,128)(2,1)}), bf16[16,320,128]{2,1,0:T(8,128)(2,1)S(1)}, u32[]{:S(2)}, u32[]{:S(2)}) async-start(bf16[16,320,128]{2,1,0:T(8,128)(2,1)} %pad_maximum_fusion), calls=%async_computation.4 | async-start | bytes 2621440 | tf_op jit(solution)/shard_map/all_to_all | solution.py:489
  116.0 18.4 %all-to-all-start.5 = ((bf16[32,32,128]{2,1,0:T(8,128)(2,1)}), bf16[32,32,128]{2,1,0:T(8,128)(2,1)S(1)}, u32[]{:S(2)}, u32[]{:S(2)}) async-start(bf16[32,32,128]{2,1,0:T(8,128)(2,1)} %bitcast.11), calls=%async_computation.5 | async-start | bytes 524288 | tf_op jit(solution)/shard_map/all_to_all | solution.py:498
  123.1 1.6 %copy-start.2 = (bf16[16,64,128]{2,1,0:T(8,128)(2,1)}, bf16[16,64,128]{2,1,0:T(8,128)(2,1)S(1)}, u32[]{:S(2)}) copy-start(bf16[16,64,128]{2,1,0:T(8,128)(2,1)S(1)} %slice.14.own_ref) | copy-start | bytes 786436
  123.2 1.6 %collective-permute-start.4 = (bf16[16,64,128]{2,1,0:T(8,128)(2,1)S(1)}, bf16[16,64,128]{2,1,0:T(8,128)(2,1)S(1)}, u32[]{:S(2)}, u32[]{:S(2)}) collective-permute-start(bf16[16,64,128]{2,1,0:T(8,128)(2,1)S(1)} %slice.14.own_ref), channel_id=1, source_target_pairs={{0,64},{64,0},{1,65},{65,1},{2,66},{66,2},{3,67},{67,3},{4,68},{68... | collective-permute-start | bytes 786440 | tf_op jit(solution)/shard_map/ppermute | solution.py:495
  124.8 0.7 copy-start.3

commit v7 on v6

--- a/solution.py
+++ b/solution.py
@@ -102,13 +102,16 @@
     return pl.ds(pl.multiple_of(b * 128, 128), 128)
 
 
-def vmem_call(kernel, out_shape, scratch, flops, size, *operands, smem=0):
+def vmem_call(kernel, out_shape, scratch, flops, size, *operands, smem=0, hbm=()):
     vmem = pl.BlockSpec(memory_space=pltpu.VMEM)
     scalar = pl.BlockSpec(memory_space=pltpu.SMEM)
     return pl.pallas_call(
         kernel,
         out_shape=out_shape,
-        in_specs=[scalar] * smem + [vmem] * (len(operands) - smem),
+        in_specs=[
+            scalar if i < smem else pl.BlockSpec(memory_space=pl.ANY) if i in hbm else vmem
+            for i in range(len(operands))
+        ],
         out_specs=tuple(vmem for _ in out_shape),
         scratch_shapes=scratch,
         compiler_params=pltpu.CompilerParams(vmem_limit_bytes=VMEM_LIMIT),
@@ -217,10 +220,12 @@
 
 
 def adjoint_kernel(
-    coords_ref, core_ref, own_ref, other_ref, z_ref, east_ref, west_ref, codes_ref, cot_ref,
+    coords_ref, core_ref, own_ref, other_ref, z_hbm, east_ref, west_ref, codes_ref, cot_ref,
     adjoint_ref, out_ref,
-    later, sums, turned, gc, left,
+    later, sums, turned, gc, left, z_ref, z_sem,
 ):
+    z_copy = pltpu.make_async_copy(z_hbm, z_ref, z_sem)
+    z_copy.start()
     low_first = core_ref[0] == 0
     for b in range(NBLK):
         cot = cot_ref[:, b * 128:(b + 1) * 128]
@@ -269,6 +274,7 @@
         gc[a, 0:PAD, :] = lax.dot_general(
             first_column(east_ref, west_ref, a), adjoint, OVER_LANES, preferred_element_type=F32
         )
+    z_copy.wait()
     lax.fori_loop(0, 8, conv_grads, 0, unroll=4)
     left[...] = jnp.zeros(left.shape, F32)
     for tap in range(9):
@@ -298,9 +304,11 @@
             pltpu.VMEM((WIDTH, TOK), F32),
             pltpu.VMEM((3, 3 * PAD, COUT), F32),
             pltpu.VMEM((128, 128), F32),
+            pltpu.VMEM((3, 33 * PAD, 128), BF16),
+            pltpu.SemaphoreType.DMA,
         ],
         1500 * 10**6, 8 * 10**6,
-        coords, core, own, other, z, east, west, codes, cot, smem=2,
+        coords, core, own, other, z, east, west, codes, cot, smem=2, hbm=(4,),
     )
 
 

time: 136 us -> 135 us (level)
  no operation moved by 1% of the time
where the time goes in v7:
time: 135 us; the launch traced here: 134 us
  starting transfers between devices  46.7 us (35%)
  waiting for transfers between devices  39.6 us (29%)
  Pallas kernels  36 us (27%)
  local copies, waits for them, and re-layouts  7.26 us (5%)
  other arithmetic  4.01 us (3%)
    pallas_call x6, Pallas kernels, vmem_call(): pl.pallas_call(kernel, out_shape=out_shape, in_specs=[scalar if i < smem...  28.8 us
    all_to_all x1, waiting for transfers between devices, per_device(): lax.all_to_all(jnp.concatenate([chip, jnp.broadcast_to(column[None], (16,...  12.4 us
    all_to_all x1, starting transfers between devices, per_device(): lax.all_to_all(jnp.broadcast_to(column[None], (8,) + column.shape), ('y',...  9.28 us
    all_to_all x1, starting transfers between devices, per_device(): column = lax.all_to_all(copies, 'z', 0, 0, tiled=True)  9.01 us
    pallas_call x1, Pallas kernels, make_patches(): pl.pallas_call(patches_kernel, out_shape=(jax.ShapeDtypeStruct((3, 33 * P...  7.23 us
    all_to_all x1, starting transfers between devices, per_device(): lax.all_to_all(jnp.broadcast_to(quarter[None], (4, 8, 32, 128)).reshape(3...  7.13 us
    all_to_all x1, waiting for transfers between devices, per_device(): lax.all_to_all(jnp.broadcast_to(quarter[None], (4, 8, 32, 128)).reshape(3...  6.82 us
    all_to_all x1, waiting for transfers between devices, per_device(): lax.all_to_all(jnp.broadcast_to(shared[None], (8, 64, 128)), 'z', 0, 0, t...  5.85 us
  transfers between devices with their start and end apart: 11, of which 9 were waited for; matrix products, arithmetic and copies ran while one was open for 3% of the time, Pallas kernels for 20%

profile of v7, /device:TPU:1, one launch (start us, length us, event | category | flops | bytes accessed | tf_op | source)
XLA Modules:
  0.0 134.4 jit_solution(5075105857731332148)
XLA Ops:
  0.6 1.5 %slice.12 = bf16[4,69,1,256]{3,2,1,0:T(2,128)(2,1)S(1)} slice(bf16[4,69,8,256]{3,2,1,0:T(8,128)(2,1)} %param.7), slice={[0:4], [0:69], [7:8], [0:256]} | slice | bytes 282624 | tf_op jit(solution)/shard_map/slice | solution.py:459
  2.2 1.5 %shard_map.102 = bf16[8,72,128]{2,1,0:T(8,128)(2,1)} custom-call(s32[1,2]{1,0:T(1,128)} %coords_ref.1, s32[1]{0:T(128)} %bitcast.core_ref, bf16[1,128,128]{2,1,0:T(8,128)(2,1)} %block_ref.1), custom_call_target="tpu_custom_call" | custom-call | flops 1000 | bytes 1000 | tf_op jit(solution)/shard_map/pallas_call | solution.py:108
  3.8 9.0 %all-to-all-start = ((bf16[8,72,128]{2,1,0:T(8,128)(2,1)}), bf16[8,72,128]{2,1,0:T(8,128)(2,1)S(1)}, u32[]{:S(2)}, u32[]{:S(2)}) async-start(bf16[8,72,128]{2,1,0:T(8,128)(2,1)} %shard_map.102), calls=%async_computation | async-start | bytes 294912 | tf_op jit(solution)/shard_map/all_to_all | solution.py:465
  12.8 3.4 %collective-permute-start = (bf16[320,256]{1,0:T(8,128)(2,1)S(1)}, bf16[320,256]{1,0:T(8,128)(2,1)S(1)}, u32[]{:S(2)}, u32[]{:S(2)}) collective-permute-start(bf16[320,256]{1,0:T(8,128)(2,1)S(1)} %bitcast.36), channel_id=1, source_target_pairs={{0,1},{1,2},{2,3},{3,4},{4,5},{5,6},{6,7},{7,8},{8,9},{9,10},{10,1... | collective-permute-start | bytes 491528 | tf_op jit(solution)/shard_map/ppermute | solution.py:464
  16.2 4.2 %collective-permute-done.north_ref = bf16[320,256]{1,0:T(8,128)(2,1)S(1)} collective-permute-done((bf16[320,256]{1,0:T(8,128)(2,1)S(1)}, bf16[320,256]{1,0:T(8,128)(2,1)S(1)}, u32[]{:S(2)}, u32[]{:S(2)}) %collective-permute-start) | collective-permute-done | bytes 163872 | tf_op jit(solution)/shard_map/ppermute | solution.py:464
  20.7 1.2 broadcast_in_dim.10
  21.9 9.3 %all-to-all-start.1 = ((bf16[8,8,72,128]{3,2,1,0:T(8,128)(2,1)}), bf16[8,8,72,128]{3,2,1,0:T(8,128)(2,1)S(1)}, u32[]{:S(2)}, u32[]{:S(2)}) async-start(bf16[8,8,72,128]{3,2,1,0:T(8,128)(2,1)} %broadcast_in_dim.10), calls=%async_computation.1 | async-start | bytes 2359296 | tf_op jit(solution)/shard_map/all_to_all | solution.py:467
  31.1 7.2 %shard_map.103 = (bf16[3,2640,128]{2,1,0:T(8,128)(2,1)}, bf16[240,128]{1,0:T(8,128)(2,1)}) custom-call(bf16[2208,256]{1,0:T(8,128)(2,1)} %bitcast.27, bf16[320,256]{1,0:T(8,128)(2,1)} %copy-done.6), custom_call_target="tpu_custom_call" | custom-call | flops 331350016 | bytes 4000000 | tf_op jit(solution)/shard_map/pallas_call | solution.py:78
  38.4 4.6 %shard_map.104.latent_ref = f32[4096,128]{1,0:T(8,128)} custom-call(bf16[3,2640,128]{2,1,0:T(8,128)(2,1)} %get-tuple-element.29.z_ref.z_hbm, bf16[9,69,256]{2,1,0:T(8,128)(2,1)} %weight_ref.3), custom_call_target="tpu_custom_call" | custom-call | flops 754974720 | bytes 4000000 | tf_op jit(solution)/shard_map/pallas_call | solution.py:108
  43.0 4.5 %all-to-all-done.1 = bf16[8,8,72,128]{3,2,1,0:T(8,128)(2,1)S(1)} async-done(((bf16[8,8,72,128]{3,2,1,0:T(8,128)(2,1)}), bf16[8,8,72,128]{3,2,1,0:T(8,128)(2,1)S(1)}, u32[]{:S(2)}, u32[]{:S(2)}) %all-to-all-start.1) | async-done | bytes 1179680 | tf_op jit(solution)/shard_map/all_to_all | solution.py:467
  47.4 3.3 %collective-permute-start.1 = (bf16[64,72,128]{2,1,0:T(8,128)(2,1)S(1)}, bf16[64,72,128]{2,1,0:T(8,128)(2,1)S(1)}, u32[]{:S(2)}, u32[]{:S(2)}) collective-permute-start(bf16[64,72,128]{2,1,0:T(8,128)(2,1)S(1)} %bitcast.19), channel_id=1, source_target_pairs={{0,64},{64,0},{1,65},{65,1},{2,66},{66,2},{3,67},{67,3},{4,68},{68... | collective-permute-start | bytes 3538952 | tf_op jit(solution)/shard_map/ppermute | solution.py:474
  51.3 1.4 %collective-permute-start.2 = (bf16[240,128]{1,0:T(8,128)(2,1)S(1)}, bf16[240,128]{1,0:T(8,128)(2,1)S(1)}, u32[]{:S(2)}, u32[]{:S(2)}) collective-permute-start(bf16[240,128]{1,0:T(8,128)(2,1)S(1)} %copy-done.4), channel_id=1, source_target_pairs={{0,64},{64,128},{128,192},{192,0},{1,65},{65,129},{129,193},{193,1... | collective-permute-start | bytes 184328 | tf_op jit(solution)/shard_map/ppermute | solution.py:471
  53.4 0.7 collective-permute-done.2.west_ref
  55.1 8.1 %shard_map.105 = (bf16[32,128,128]{2,1,0:T(8,128)(2,1)}, bf16[256,8,128]{2,1,0:T(8,128)(2,1)}) custom-call(s32[64,2]{1,0:T(8,128)} %bitcast.30, s32[1]{0:T(128)} %bitcast.core_ref, bf16[64,72,128]{2,1,0:T(8,128)(2,1)} %bitcast.21, bf16[64,72,128]{2,1,0:T(8,128)(2,1)} %copy-done.1, bf16[3,2640,128]{2,1,0:T(8,128)(2,1)} %get-tuple-element.29.z_ref.z_hbm, ...), custom_call_target="tpu_custom_call" | custom-call | flops 1500000000 | bytes 8000000 | tf_op jit(solution)/shard_map/pallas_call | solution.py:108
  63.2 4.8 %all-to-all-start.2 = ((bf16[32,64,128]{2,1,0:T(8,128)(2,1)}), bf16[32,64,128]{2,1,0:T(8,128)(2,1)S(1)}, u32[]{:S(2)}, u32[]{:S(2)}) async-start(bf16[32,64,128]{2,1,0:T(8,128)(2,1)} %bitcast.33), calls=%async_computation.2 | async-start | bytes 1048576 | tf_op jit(solution)/shard_map/all_to_all | solution.py:480
  68.0 8.1 %shard_map.106 = (bf16[4096,128]{1,0:T(8,128)(2,1)}, f32[2,64,32,128]{3,2,1,0:T(8,128)}, bf16[2,64,32,128]{3,2,1,0:T(8,128)(2,1)}) custom-call(s32[64,2]{1,0:T(8,128)} %bitcast.31, s32[1]{0:T(128)} %bitcast.core_ref, bf16[64,72,128]{2,1,0:T(8,128)(2,1)} %bitcast.22, bf16[64,72,128]{2,1,0:T(8,128)(2,1)} %copy-done.1, f32[4096,128]{1,0:T(8,128)} %shard_map.104.latent_ref, ...), custom_call_target="tpu_custom_call" | custom-call | flops 1000 | bytes 1000 | tf_op jit(solution)/shard_map/pallas_call | solution.py:108
  76.1 3.7 %all-to-all-done.2 = bf16[32,64,128]{2,1,0:T(8,128)(2,1)S(1)} async-done(((bf16[32,64,128]{2,1,0:T(8,128)(2,1)}), bf16[32,64,128]{2,1,0:T(8,128)(2,1)S(1)}, u32[]{:S(2)}, u32[]{:S(2)}) %all-to-all-start.2) | async-done | bytes 524320 | tf_op jit(solution)/shard_map/all_to_all | solution.py:480
  79.9 0.7 broadcast_in_dim.11
  80.5 3.8 %all-to-all-start.3 = ((bf16[8,64,128]{2,1,0:T(8,128)(2,1)}), bf16[8,64,128]{2,1,0:T(8,128)(2,1)S(1)}, u32[]{:S(2)}, u32[]{:S(2)}) async-start(bf16[8,64,128]{2,1,0:T(8,128)(2,1)} %broadcast_in_dim.11), calls=%async_computation.3 | async-start | bytes 262144 | tf_op jit(solution)/shard_map/all_to_all | solution.py:491
  84.4 1.9 %add_convert_fusion = bf16[2,64,32,128]{3,2,1,0:T(8,128)(2,1)S(1)} fusion(f32[2,64,32,128]{3,2,1,0:T(8,128)} %get-tuple-element.37, bf16[2,64,32,128]{3,2,1,0:T(8,128)(2,1)S(1)} %collective-permute-done.3), kind=kLoop, calls=%fused_computation | loop fusion | flops 1572864 | bytes 4194304 | tf_op jit(solution)/shard_map/convert_element_type | solution.py:494
  86.3 5.8 %all-to-all-done.3 = bf16[8,64,128]{2,1,0:T(8,128)(2,1)S(1)} async-done(((bf16[8,64,128]{2,1,0:T(8,128)(2,1)}), bf16[8,64,128]{2,1,0:T(8,128)(2,1)S(1)}, u32[]{:S(2)}, u32[]{:S(2)}) %all-to-all-start.3) | async-done | bytes 131104 | tf_op jit(solution)/shard_map/all_to_all | solution.py:491
  92.2 1.2 pad_maximum_fusion
  93.4 4.3 %all-to-all-start.4 = ((bf16[16,320,128]{2,1,0:T(8,128)(2,1)}), bf16[16,320,128]{2,1,0:T(8,128)(2,1)S(1)}, u32[]{:S(2)}, u32[]{:S(2)}) async-start(bf16[16,320,128]{2,1,0:T(8,128)(2,1)} %pad_maximum_fusion), calls=%async_computation.4 | async-start | bytes 2621440 | tf_op jit(solution)/shard_map/all_to_all | solution.py:497
  97.7 4.5 %shard_map.107 = bf16[128,4096]{1,0:T(8,128)(2,1)} custom-call(s32[64,2]{1,0:T(8,128)} %bitcast.32, s32[1]{0:T(128)} %bitcast.core_ref, bf16[64,72,128]{2,1,0:T(8,128)(2,1)} %bitcast.23, bf16[64,72,128]{2,1,0:T(8,128)(2,1)} %copy-done.1, bf16[4096,128]{1,0:T(8,128)(2,1)} %get-tuple-element.41.state_ref, bf16[24,4096]{1,0:T(8,128)(2,1)} %table_ref.3, ...), custom_call_target="tpu_custom_call" | custom-call | flops 1000 | bytes 1000 | tf_op jit(solution)/shard_map/pallas_call | solution.py:108
  102.1 12.4 %all-to-all-done.4 = bf16[16,320,128]{2,1,0:T(8,128)(2,1)S(1)} async-done(((bf16[16,320,128]{2,1,0:T(8,128)(2,1)}), bf16[16,320,128]{2,1,0:T(8,128)(2,1)S(1)}, u32[]{:S(2)}, u32[]{:S(2)}) %all-to-all-start.4) | async-done | bytes 1310752 | tf_op jit(solution)/shard_map/all_to_all | solution.py:497
  114.7 0.7 broadcast_in_dim.14
  115.4 7.1 %all-to-all-start.5 = ((bf16[32,32,128]{2,1,0:T(8,128)(2,1)}), bf16[32,32,128]{2,1,0:T(8,128)(2,1)S(1)}, u32[]{:S(2)}, u32[]{:S(2)}) async-start(bf16[32,32,128]{2,1,0:T(8,128)(2,1)} %bitcast.11), calls=%async_computation.5 | async-start | bytes 524288 | tf_op jit(solution)/shard_map/all_to_all | solution.py:506
  123.0 1.2 collective-permute-done.4.other_ref
  124.2 0.7 copy-done.3
  124.9 2.0 %shard_map.108 = (f32[9,69,256]{2,1,0:T(8,128)}, f32[24,4096]{1,0:T(8,128)}) custom-call(s32[1]{0:T(128)} %bitcast.core_ref, bf16[16,64,128]{2,1,0:T(8,128)(2,1)} %copy-done.2, bf16[16,64,128]{2,1,0:T(8,128)(2,1)} %copy-done.3), custom_call_target="tpu_custom_call" | custom-call | flops 1000 | bytes 1000 | tf_op jit(solution)/shard_map/pallas_call | solution.py:108
  126.9 6.8 %all-to-all-done.5 = bf16[32,32,128]{2,1,0:T(8,128)(2,1)S(1)} async-done(((bf16[32,32,128]{2,1,0:T(8,128)(2,1)}), bf16[32,32,128]{2,1,0:T(8,128)(2,1)S(1)}, u32[]{:S(2)}, u32[]{:S(2)}) %all-to-all-start.5) | async-done | bytes 262176 | tf_op jit(solution)/shard_map/all_to_all | solution.py:506
  133.8 0.6 copy.36
  (30 shorter events, 3.5 us)
Async XLA Ops:
  3.8 16.9 %all-to-all-start = ((bf16[8,72,128]{2,1,0:T(8,128)(2,1)}), bf16[8,72,128]{2,1,0:T(8,128)(2,1)S(1)}, u32[]{:S(2)}, u32[]{:S(2)}) async-start(bf16[8,72,128]{2,1,0:T(8,128)(2,1)} %shard_map.102), calls=%async_computation | async-start | bytes 294912 | tf_op jit(solution)/shard_map/all_to_all | solution.py:465
  12.8 7.5 %collective-permute-start = (bf16[320,256]{1,0:T(8,128)(2,1)S(1)}, bf16[320,256]{1,0:T(8,128)(2,1)S(1)}, u32[]{:S(2)}, u32[]{:S(2)}) collective-permute-start(bf16[320,256]{1,0:T(8,128)(2,1)S(1)} %bitcast.36), channel_id=1, source_target_pairs={{0,1},{1,2},{2,3},{3,4},{4,5},{5,6},{6,7},{7,8},{8,9},{9,10},{10,1... | collective-permute-start | bytes 491528 | tf_op jit(solution)/shard_map/ppermute | solution.py:464
  20.3 1.6 %copy-start.6 = (bf16[320,256]{1,0:T(8,128)(2,1)}, bf16[320,256]{1,0:T(8,128)(2,1)S(1)}, u32[]{:S(2)}) copy-start(bf16[320,256]{1,0:T(8,128)(2,1)S(1)} %collective-permute-done.north_ref) | copy-start | bytes 491524
  21.9 25.5 %all-to-all-start.1 = ((bf16[8,8,72,128]{3,2,1,0:T(8,128)(2,1)}), bf16[8,8,72,128]{3,2,1,0:T(8,128)(2,1)S(1)}, u32[]{:S(2)}, u32[]{:S(2)}) async-start(bf16[8,8,72,128]{3,2,1,0:T(8,128)(2,1)} %broadcast_in_dim.10), calls=%async_computation.1 | async-start | bytes 2359296 | tf_op jit(solution)/shard_map/all_to_all | solution.py:467
  38.4 12.3 %copy-start.7 = (s32[2,4,4,8]{3,2,1,0:T(4,128)S(1)}, s32[2,4,4,8]{3,2,1,0:T(4,128)}, u32[]{:S(2)}) copy-start(s32[2,4,4,8]{3,2,1,0:T(4,128)} %param.12) | copy-start | bytes 3076
  38.4 13.0 %copy-start.4 = (bf16[240,128]{1,0:T(8,128)(2,1)S(1)}, bf16[240,128]{1,0:T(8,128)(2,1)}, u32[]{:S(2)}) copy-start(bf16[240,128]{1,0:T(8,128)(2,1)} %get-tuple-element.31.east_ref) | copy-start | bytes 184324
  47.4 6.6 %copy-start = (bf16[8,8,72,128]{3,2,1,0:T(8,128)(2,1)}, bf16[8,8,72,128]{3,2,1,0:T(8,128)(2,1)S(1)}, u32[]{:S(2)}) copy-start(bf16[8,8,72,128]{3,2,1,0:T(8,128)(2,1)S(1)} %all-to-all-done.1) | copy-start | bytes 3538948
  47.4 6.6 %collective-permute-start.1 = (bf16[64,72,128]{2,1,0:T(8,128)(2,1)S(1)}, bf16[64,72,128]{2,1,0:T(8,128)(2,1)S(1)}, u32[]{:S(2)}, u32[]{:S(2)}) collective-permute-start(bf16[64,72,128]{2,1,0:T(8,128)(2,1)S(1)} %bitcast.19), channel_id=1, source_target_pairs={{0,64},{64,0},{1,65},{65,1},{2,66},{66,2},{3,67},{67,3},{4,68},{68... | collective-permute-start | bytes 3538952 | tf_op jit(solution)/shard_map/ppermute | solution.py:474
  51.3 2.7 %collective-permute-start.2 = (bf16[240,128]{1,0:T(8,128)(2,1)S(1)}, bf16[240,128]{1,0:T(8,128)(2,1)S(1)}, u32[]{:S(2)}, u32[]{:S(2)}) collective-permute-start(bf16[240,128]{1,0:T(8,128)(2,1)S(1)} %copy-done.4), channel_id=1, source_target_pairs={{0,64},{64,128},{128,192},{192,0},{1,65},{65,129},{129,193},{193,1... | collective-permute-start | bytes 184328 | tf_op jit(solution)/shard_map/ppermute | solution.py:471
  54.0 0.6 copy-start.5
  54.1 1.1 copy-start.1
  63.2 16.6 %all-to-all-start.2 = ((bf16[32,64,128]{2,1,0:T(8,128)(2,1)}), bf16[32,64,128]{2,1,0:T(8,128)(2,1)S(1)}, u32[]{:S(2)}, u32[]{:S(2)}) async-start(bf16[32,64,128]{2,1,0:T(8,128)(2,1)} %bitcast.33), calls=%async_computation.2 | async-start | bytes 1048576 | tf_op jit(solution)/shard_map/all_to_all | solution.py:480
  79.8 4.6 %collective-permute-start.3 = (bf16[2,64,32,128]{3,2,1,0:T(8,128)(2,1)}, bf16[2,64,32,128]{3,2,1,0:T(8,128)(2,1)S(1)}, u32[]{:S(2)}, u32[]{:S(2)}) collective-permute-start(bf16[2,64,32,128]{3,2,1,0:T(8,128)(2,1)} %get-tuple-element.38), channel_id=1, source_target_pairs={{0,64},{64,0},{1,65},{65,1},{2,66},{66,2},{3,67},{67,3},{4,68},{68... | collective-permute-start | bytes 3145736 | tf_op jit(solution)/shard_map/ppermute | solution.py:488
  80.5 11.6 %all-to-all-start.3 = ((bf16[8,64,128]{2,1,0:T(8,128)(2,1)}), bf16[8,64,128]{2,1,0:T(8,128)(2,1)S(1)}, u32[]{:S(2)}, u32[]{:S(2)}) async-start(bf16[8,64,128]{2,1,0:T(8,128)(2,1)} %broadcast_in_dim.11), calls=%async_computation.3 | async-start | bytes 262144 | tf_op jit(solution)/shard_map/all_to_all | solution.py:491
  93.4 21.1 %all-to-all-start.4 = ((bf16[16,320,128]{2,1,0:T(8,128)(2,1)}), bf16[16,320,128]{2,1,0:T(8,128)(2,1)S(1)}, u32[]{:S(2)}, u32[]{:S(2)}) async-start(bf16[16,320,128]{2,1,0:T(8,128)(2,1)} %pad_maximum_fusion), calls=%async_computation.4 | async-start | bytes 2621440 | tf_op jit(solution)/shard_map/all_to_all | solution.py:497
  115.4 18.4 %all-to-all-start.5 = ((bf16[32,32,128]{2,1,0:T(8,128)(2,1)}), bf16[32,32,128]{2,1,0:T(8,128)(2,1)S(1)}, u32[]{:S(2)}, u32[]{:S(2)}) async-start(bf16[32,32,128]{2,1,0:T(8,128)(2,1)} %bitcast.11), calls=%async_computation.5 | async-start | bytes 524288 | tf_op jit(solution)/shard_map/all_to_all | solution.py:506
  122.6 1.6 %copy-start.2 = (bf16[16,64,128]{2,1,0:T(8,128)(2,1)}, bf16[16,64,128]{2,1,0:T(8,128)(2,1)S(1)}, u32[]{:S(2)}) copy-start(bf16[16,64,128]{2,1,0:T(8,128)(2,1)S(1)} %slice.14.own_ref) | copy-start | bytes 786436
  122.6 1.6 %collective-permute-start.4 = (bf16[16,64,128]{2,1,0:T(8,128)(2,1)S(1)}, bf16[16,64,128]{2,1,0:T(8,128)(2,1)S(1)}, u32[]{:S(2)}, u32[]{:S(2)}) collective-permute-start(bf16[16,64,128]{2,1,0:T(8,128)(2,1)S(1)} %slice.14.own_ref), channel_id=1, source_target_pairs={{0,64},{64,0},{1,65},{65,1},{2,66},{66,2},{3,67},{67,3},{4,68},{68... | collective-permute-start | bytes 786440 | tf_op jit(solution)/shard_map/ppermute | solution.py:503
  124.2 0.7 copy-start.3
